TPU v7x, 32 devices: a whole 2x2x4 slice. The times are simulated.
32 devices in a mesh: tok: 4 (over y, x), ch: 8 (over z, core).
Axes of the slice: x: 2, y: 2, z: 4, core: 2. Of those that a mesh axis runs over, the one named last changes fastest.
Arguments:
- block_input: bfloat16 [4096, 2048], P(('tok', 'ch')), may hold values from -6 to 6
- norm_gain: bfloat16 [2048], replicated, may hold values from 0.5 to 1.5
- in_weight: bfloat16 [3, 2048, 8192], P(None, None, 'ch'), may hold values from -0.125 to 0.125
- x_weight: bfloat16 [3, 160, 4096], P(None, None, 'ch'), may hold values from -0.09375 to 0.09375
- dt_weight: bfloat16 [3, 128, 4096], P(None, None, 'ch'), may hold values from -0.5 to 0.5
- dt_bias: bfloat16 [3, 4096], P(None, 'ch'), may hold values from -3 to 0
- conv_weight: bfloat16 [4, 4096], P(None, 'ch'), may hold values from -0.5 to 0.5
- conv_bias: bfloat16 [4096], P('ch'), may hold values from -0.5 to 0.5
- a_log: bfloat16 [16, 4096], P(None, 'ch'), may hold values from 0 to 2
- skip_gain: bfloat16 [4096], P('ch'), may hold values from 0.5 to 1.5
- out_weight: bfloat16 [3, 4096, 2048], P(None, 'ch'), may hold values from -0.75 to 0.75
- modality: int32 [4096], P(('tok', 'ch')), may hold values from 0 to 2
- cotangent: bfloat16 [4096, 2048], P(('tok', 'ch')), may hold values from -6 to 6
Outputs:
- block_out: bfloat16 [4096, 2048], P(('tok', 'ch'))
- input_grad: float32 [4096, 2048], P(('tok', 'ch'))
- gain_grad: float32 [2048], P('ch')
- in_weight_grad: float32 [3, 2048, 8192], P(None, None, 'ch')
- x_weight_grad: float32 [3, 160, 4096], P(None, None, 'ch')
- dt_weight_grad: float32 [3, 128, 4096], P(None, None, 'ch')
- dt_bias_grad: float32 [3, 4096], P(None, 'ch')
- conv_weight_grad: float32 [4, 4096], P(None, 'ch')
- conv_bias_grad: float32 [4096], P('ch')
- a_log_grad: float32 [16, 4096], P(None, 'ch')
- skip_gain_grad: float32 [4096], P('ch')
- out_weight_grad: float32 [3, 4096, 2048], P(None, 'ch')
All inputs are finite; a program needn't handle non-finite values.
Results may differ from a plain program's by a relative error of at most 0.0096.
Values may be sent and summed in bfloat16 or wider, within the bound.
A program may use at most 448 MiB of HBM per device.

v0:
```python
import jax
import jax.numpy as jnp
from jax import lax
from jax.sharding import PartitionSpec as P

highest = lax.Precision.HIGHEST


def mixer(xz_value, onehot, x_weight, dt_weight, dt_bias, conv_weight, conv_bias, a_log, skip_gain):
    channels = conv_weight.shape[1]
    tap_count = conv_weight.shape[0]
    length = xz_value.shape[0]
    inner_part = xz_value[:, :channels]
    gate_in = xz_value[:, channels:]
    padded = jnp.concatenate(
        [jnp.zeros((tap_count - 1, channels), jnp.float32), inner_part], axis=0
    )
    convolved = conv_bias[None, :]
    for tap in range(tap_count):
        convolved = convolved + conv_weight[tap][None, :] * padded[tap : tap + length]
    active = jax.nn.silu(convolved)
    modalities = x_weight.shape[0]
    low_width = dt_weight.shape[1]
    states = a_log.shape[0]
    mixed = jnp.zeros((length, x_weight.shape[1]), jnp.float32)
    for index in range(modalities):
        mixed = mixed + onehot[:, index : index + 1] * jnp.dot(
            active, x_weight[index].T, precision=highest
        )
    low_rank = mixed[:, :low_width]
    b_part = mixed[:, low_width : low_width + states]
    c_part = mixed[:, low_width + states :]
    speed_pre = jnp.zeros((length, channels), jnp.float32)
    for index in range(modalities):
        speed_pre = speed_pre + onehot[:, index : index + 1] * (
            jnp.dot(low_rank, dt_weight[index], precision=highest) + dt_bias[index][None, :]
        )
    step_size = jax.nn.softplus(speed_pre)
    decay_rates = -jnp.exp(a_log)

    def advance(carry_state, inputs):
        step_now, drive, b_row, c_row = inputs
        carry_state = (
            jnp.exp(step_now[None, :] * decay_rates) * carry_state + b_row[:, None] * drive[None, :]
        )
        return (carry_state, jnp.dot(c_row, carry_state, precision=highest))

    start_state = jnp.zeros((states, channels), jnp.float32)
    _, scanned = lax.scan(advance, start_state, (step_size, step_size * active, b_part, c_part))
    return (scanned + skip_gain[None, :] * active) * jax.nn.silu(gate_in)


def masks_of(labels, count):
    return labels[:, None] == jnp.arange(count, dtype=jnp.int32)[None, :]


def spread_rows(rows, hot):
    pieces = [
        jnp.where(hot[:, index : index + 1], rows, jnp.zeros_like(rows))
        for index in range(hot.shape[1])
    ]
    return jnp.concatenate(pieces, axis=1)


def select_columns(term, hot, width):
    total = None
    for index in range(hot.shape[1]):
        part = jnp.where(
            hot[:, index : index + 1],
            term[:, index * width : (index + 1) * width],
            jnp.zeros((), term.dtype),
        )
        total = part if total is None else total + part
    return total


def forward_select(rows, hot, weights):
    modalities, inner, outer = weights.shape
    joined = jnp.transpose(weights, (1, 0, 2)).reshape(inner, modalities * outer)
    term = jnp.dot(rows, joined, preferred_element_type=jnp.float32)
    return select_columns(term, hot, outer)


def forward_spread(rows, hot, weights):
    modalities, inner, outer = weights.shape
    return jnp.dot(
        spread_rows(rows, hot),
        weights.reshape(modalities * inner, outer),
        preferred_element_type=jnp.float32,
    )


def back_select(rows, hot, weights):
    modalities, inner, outer = weights.shape
    term = lax.dot_general(
        rows,
        weights.reshape(modalities * inner, outer),
        (((1,), (1,)), ((), ())),
        preferred_element_type=jnp.float32,
    )
    return select_columns(term, hot, inner)


def back_spread(rows, hot, joined):
    return lax.dot_general(
        spread_rows(rows, hot), joined, (((1,), (1,)), ((), ())), preferred_element_type=jnp.float32
    )


def on_device(
    block_input,
    norm_gain,
    in_weight,
    x_weight,
    dt_weight,
    dt_bias,
    conv_weight,
    conv_bias,
    a_log,
    skip_gain,
    out_weight,
    modality,
    cotangent,
):
    modalities = in_weight.shape[0]
    width = block_input.shape[1]
    in_slice = in_weight.shape[2]
    rows_float = block_input.astype(jnp.float32)
    gain = norm_gain.astype(jnp.float32)
    inverse = lax.rsqrt(jnp.mean(rows_float * rows_float, axis=-1, keepdims=True) + 1e-05)
    normed = rows_float * inverse
    scaled = (normed * gain[None, :]).astype(jnp.bfloat16)
    all_rows, all_labels = (
        lax.all_gather(scaled, "ch", axis=0, tiled=True),
        lax.all_gather(modality, "ch", axis=0, tiled=True),
    )
    all_hot = masks_of(all_labels, modalities)
    projected = forward_select(all_rows, all_hot, in_weight)
    sequence_xz = lax.all_to_all(
        projected.astype(jnp.bfloat16), "ch", split_axis=0, concat_axis=1, tiled=True
    )
    full_params = (
        lax.all_gather(x_weight, "ch", axis=2, tiled=True),
        lax.all_gather(dt_weight, "ch", axis=2, tiled=True),
        lax.all_gather(dt_bias, "ch", axis=1, tiled=True),
        lax.all_gather(conv_weight, "ch", axis=1, tiled=True),
        lax.all_gather(conv_bias, "ch", axis=0, tiled=True),
        lax.all_gather(a_log, "ch", axis=1, tiled=True),
        lax.all_gather(skip_gain, "ch", axis=0, tiled=True),
    )
    own_hot = masks_of(modality, modalities)
    own_float = own_hot.astype(jnp.float32)
    float_params = tuple((value.astype(jnp.float32) for value in full_params))

    def local_mixer(xz_value, values):
        return mixer(
            xz_value,
            own_float,
            values[0],
            values[1],
            values[2],
            values[3],
            values[4],
            values[5],
            values[6],
        )

    mixed, pullback = jax.vjp(local_mixer, sequence_xz.astype(jnp.float32), float_params)
    gated = mixed.astype(jnp.bfloat16)
    slice_width = out_weight.shape[1]
    channel_gated = lax.all_to_all(gated, "ch", split_axis=1, concat_axis=0, tiled=True)
    seq_grad = None
    rows = channel_gated
    hot = all_hot
    branch = lax.psum_scatter(
        forward_spread(rows, hot, out_weight), "ch", scatter_dimension=0, tiled=True
    )
    piece = lax.all_gather(cotangent, "ch", axis=0, tiled=True)
    rows = channel_gated
    hot = all_hot
    weight_acc = lax.dot_general(
        spread_rows(rows, hot), piece, (((0,), (0,)), ((), ())), preferred_element_type=jnp.float32
    )
    new_grad = back_select(piece, hot, out_weight)
    out_grad_part = weight_acc.reshape(modalities, slice_width, width)
    seq_grad = lax.all_to_all(
        new_grad.astype(jnp.bfloat16), "ch", split_axis=0, concat_axis=1, tiled=True
    )
    block_out = (rows_float + branch).astype(jnp.bfloat16)
    cot_float = cotangent.astype(jnp.float32)
    xz_grad, param_grads = pullback(seq_grad.astype(jnp.float32))
    channel_xz_grad = lax.all_to_all(
        xz_grad.astype(jnp.bfloat16), "ch", split_axis=1, concat_axis=0, tiled=True
    )
    spread_grad = spread_rows(channel_xz_grad, all_hot)
    in_grad_flat = lax.dot_general(
        all_rows, spread_grad, (((0,), (0,)), ((), ())), preferred_element_type=jnp.float32
    )
    in_grad_part = jnp.transpose(in_grad_flat.reshape(width, modalities, in_slice), (1, 0, 2))
    in_joined = jnp.transpose(in_weight, (1, 0, 2)).reshape(width, modalities * in_slice)
    hot = all_hot
    scaled_grad = lax.psum_scatter(
        back_spread(channel_xz_grad, hot, in_joined), "ch", scatter_dimension=0, tiled=True
    )
    gain_term = jnp.sum(scaled_grad * normed, axis=0)
    normed_grad = scaled_grad * gain[None, :]
    row_grad = cot_float + inverse * (
        normed_grad - normed * jnp.mean(normed_grad * normed, axis=-1, keepdims=True)
    )
    xw_grad, dtw_grad, dtb_grad, convw_grad, convb_grad, alog_grad, skip_grad = param_grads
    shards = (
        lax.psum_scatter(xw_grad, "ch", scatter_dimension=2, tiled=True),
        lax.psum_scatter(dtw_grad, "ch", scatter_dimension=2, tiled=True),
        lax.psum_scatter(dtb_grad, "ch", scatter_dimension=1, tiled=True),
        lax.psum_scatter(convw_grad, "ch", scatter_dimension=1, tiled=True),
        lax.psum_scatter(convb_grad, "ch", scatter_dimension=0, tiled=True),
        lax.psum_scatter(alog_grad, "ch", scatter_dimension=1, tiled=True),
        lax.psum_scatter(skip_grad, "ch", scatter_dimension=0, tiled=True),
        lax.psum_scatter(gain_term, "ch", scatter_dimension=0, tiled=True),
    )
    xw_shard, dtw_shard, dtb_shard, convw_shard, convb_shard, alog_shard, skip_shard, gain_shard = (
        shards
    )
    totals = lax.psum(
        (
            in_grad_part,
            out_grad_part,
            xw_shard,
            dtw_shard,
            dtb_shard,
            convw_shard,
            convb_shard,
            alog_shard,
            skip_shard,
            gain_shard,
        ),
        "tok",
    )
    return (
        block_out,
        row_grad,
        totals[9],
        totals[0],
        totals[2],
        totals[3],
        totals[4],
        totals[5],
        totals[6],
        totals[7],
        totals[8],
        totals[1],
    )


def solution(mesh):
    placed = (
        P(("tok", "ch"), None),
        P(),
        P(None, None, "ch"),
        P(None, None, "ch"),
        P(None, None, "ch"),
        P(None, "ch"),
        P(None, "ch"),
        P("ch"),
        P(None, "ch"),
        P("ch"),
        P(None, "ch", None),
        P(("tok", "ch")),
        P(("tok", "ch"), None),
    )
    return jax.shard_map(
        on_device,
        mesh=mesh,
        in_specs=placed,
        out_specs=(
            P(("tok", "ch"), None),
            P(("tok", "ch"), None),
            P("ch"),
            P(None, None, "ch"),
            P(None, None, "ch"),
            P(None, None, "ch"),
            P(None, "ch"),
            P(None, "ch"),
            P("ch"),
            P(None, "ch"),
            P("ch"),
            P(None, "ch", None),
        ),
        check_vma=False,
    )
```

profile of v0, /device:TPU:0, one launch (start us, length us, event | category | flops | bytes accessed | tf_op | source)
XLA Modules:
  0.0 3882.8 jit_solution(17598331085011218032)
XLA Ops:
  13.3 17.0 copy.47
  30.2 13.5 all-gather
  43.8 15.6 all-gather.14.cloned.1.call-done
  59.5 10.1 fusion.116
  71.2 3.6 all-to-all-start.2
  74.8 55.0 %all-gather.8.cloned.1.call-done = bf16[1024,2048]{1,0:T(8,128)(2,1)} async-done(((bf16[128,2048]{1,0:T(8,128)(2,1)}), bf16[1024,2048]{1,0:T(8,128)(2,1)}) %all-gather.8.cloned.1.call-update) | async-done | bytes 4194320 | tf_op jit(solution)/shard_map/all_gather | solution.py:134
  129.8 17.1 fusion.115
  149.2 4.5 all-to-all-start
  154.4 93.0 %all-gather.1 = bf16[8,1,512]{2,1,0:T(2,128)(2,1)S(1)} all-gather(bf16[1,1,512]{2,1,0:T(2,128)(2,1)S(1)} %reshape.183), channel_id=1, replica_groups=mesh['tok'=4,'ch'=8] {'ch'}, dimensions={0}, use_global_device_ids=true | all-gather | bytes 9216 | tf_op jit(solution)/shard_map/all_gather | solution.py:147
  247.4 14.0 all_gather.36
  261.4 14.0 all_gather.32
  275.4 13.9 all_gather.37
  290.1 2.8 convert_bitcast_fusion
  296.2 4.1 multiply_reduce_fusion.3
  300.2 3.9 fusion.57
  308.8 2.5 fusion.17
  312.5 5.3 fusion.103
  319.4 849.7 %while.50 = (s32[]{:T(128)}, f32[16,4096]{1,0:T(8,128)S(1)}, f32[128,4096]{1,0:T(8,128)}, f32[128,1,4096]{2,1,0:T(1,128)}, f32[128,16,4096]{2,1,0:T(8,128)}, /*i...) while((s32[]{:T(128)}, f32[16,4096]{1,0:T(8,128)S(1)}, ...), condition=%wide.region_2.3_spmd.clone, body=%wide.region_1.2_spmd.clone.sunk | while | flops 1179651 | bytes 2068331 | solution.py:49
  1171.5 1472.8 %while.51 = (s32[]{:T(128)}, f32[16,4096]{1,0:T(8,128)S(1)}, f32[16,4096]{1,0:T(8,128)S(1)}, f32[128,4096]{1,0:T(8,128)}, f32[128,4096]{1,0:T(8,128)S(1)}, /*ind...) while((s32[]{:T(128)}, f32[16,4096]{1,0:T(8,128)S(1)}, ...), condition=%wide.region_8.9_spmd.clone, body=%wide.region_4.8_spmd.clone.sunk | while | flops 1761268 | bytes 2885608 | solution.py:49
  2645.6 4.9 multiply_reduce_fusion.10
  2656.4 3.1 pad_add_fusion.1
  2660.5 2.7 fusion.39
  2666.2 2.7 convolution_bitcast_fusion.2
  2668.8 2.7 convolution_bitcast_fusion.1
  2671.5 2.7 convolution_bitcast_fusion
  2674.2 3.7 pad_add_fusion
  2678.5 13.8 all-gather.2
  2692.4 5.1 convolution_add_fusion.2
  2697.6 4.0 convolution_add_fusion.1
  2701.6 7.4 multiply_reduce_fusion.6
  2711.6 3.6 all-to-all-start.3
  2719.9 75.2 %all-to-all-done.3 = bf16[128,8,1024]{2,0,1:T(8,128)(2,1)S(1)} async-done(((bf16[128,8,1024]{2,0,1:T(8,128)(2,1)}), bf16[128,8,1024]{2,0,1:T(8,128)(2,1)S(1)}, u32[]{:S(2)}, u32[]{:S(2)}) %all-to-all-start.3) | async-done | bytes 2097184 | tf_op jit(solution)/shard_map/all_to_all | solution.py:192
  2798.7 18.2 fusion.22
  2819.2 4.0 all-to-all-start.1
  2824.1 34.3 all-to-all-done.1
  2860.3 10.7 fusion.49
  2871.3 12.0 fusion.48
  2883.3 21.3 fusion.21
  2908.2 33.2 reduce-scatter.24.cloned.1.call-done
  2942.4 89.7 %reduce-scatter.14.cloned.1.call-done = f32[128,2048]{1,0:T(8,128)} async-done(((f32[1024,2048]{1,0:T(8,128)}), f32[128,2048]{1,0:T(8,128)}) %reduce-scatter.14.cloned.1.call-update) | async-done | bytes 1048592 | tf_op jit(solution)/shard_map/reduce_scatter | solution.py:202
  3033.8 26.5 all-reduce.26
  3060.5 3.1 reduce-scatter.20.cloned.1.call-done
  3063.6 17.6 all-reduce.27
  3081.2 72.6 %reduce-scatter.12.cloned.1.call-done = f32[128,2048]{1,0:T(8,128)} async-done(((f32[1024,2048]{1,0:T(8,128)}), f32[128,2048]{1,0:T(8,128)}) %reduce-scatter.12.cloned.1.call-update) | async-done | bytes 1048592 | tf_op jit(solution)/shard_map/reduce_scatter | solution.py:175
  3153.8 2.8 fusion.68
  3156.6 680.4 %all-reduce.31.cloned.1.call-done = (f32[3,2048,1024]{1,2,0:T(8,128)}, f32[3,160,512]{2,1,0:T(8,128)}, f32[3,128,512]{2,1,0:T(8,128)}, f32[3,512,2048]{2,1,0:T(8,128)}) async-done(((f32[3,2048,1024]{1,2,0:T(8,128)}, f32[3,160,512]{2,1,0:T(8,128)}, f32[3,128,512]{2,1,0:T(8,128)}, f32[3,512,2048]{2,1,0:T(8,128)}), (f32[3,2048,1024]{1,2,0:T(8,128)}, f32[3,160,512]{2,1,0:T(8,128)}, f32[3,128,512]{2,1,0:T(8,128)}, ...) | async-done | bytes 39518224 | tf_op jit(solution)/shard_map/psum | solution.py:224
  3837.0 24.8 copy.58
  3864.1 11.5 copy.137
  (2510 shorter events, 2375.4 us)
Async XLA Ops:
  7.2 52.3 %all-gather.14.cloned.1.call-start = ((), (), s32[]{:S(2)}) async-start(), calls=%async_computation.15 | async-start | bytes 4718592 | tf_op jit(solution)/shard_map/all_gather | solution.py:178
  7.9 121.9 %all-gather.8.cloned.1.call-start = ((), (), s32[]{:S(2)}) async-start(), calls=%async_computation.11 | async-start | bytes 4718592 | tf_op jit(solution)/shard_map/all_gather | solution.py:134
  12.5 287.7 %all-gather.10.cloned.1.call-start = ((), (), s32[]{:S(2)}) async-start(), calls=%async_computation.12 | async-start | bytes 4423680 | tf_op jit(solution)/shard_map/all_gather | solution.py:143
  13.3 17.0 copy-start.49
  43.8 103.1 %copy-start.32 = (pred[1024]{0:T(1024)(128)(4,1)}, pred[1024]{0:T(1024)(128)(4,1)S(1)}, u32[]{:S(2)}) copy-start(pred[1024]{0:T(1024)(128)(4,1)S(1)} %get-tuple-element.640) | copy-start | bytes 3076
  43.8 103.1 %copy-start.34 = (pred[1024]{0:T(1024)(128)(4,1)}, pred[1024]{0:T(1024)(128)(4,1)S(1)}, u32[]{:S(2)}) copy-start(pred[1024]{0:T(1024)(128)(4,1)S(1)} %get-tuple-element.641) | copy-start | bytes 3076
  43.8 103.1 %copy-start.36 = (pred[1024]{0:T(1024)(128)(4,1)}, pred[1024]{0:T(1024)(128)(4,1)S(1)}, u32[]{:S(2)}) copy-start(pred[1024]{0:T(1024)(128)(4,1)S(1)} %get-tuple-element.642) | copy-start | bytes 3076
  71.2 77.9 %all-to-all-start.2 = ((bf16[8,128,512]{2,1,0:T(8,128)(2,1)}), bf16[8,128,512]{2,1,0:T(8,128)(2,1)S(1)}, u32[]{:S(2)}, u32[]{:S(2)}) async-start(bf16[8,128,512]{2,1,0:T(8,128)(2,1)} %bitcast.28), calls=%async_computation.3 | async-start | bytes 2097152 | tf_op jit(solution)/shard_map/all_to_all | solution.py:186
  149.1 5.2 copy-start.50
  149.1 98.2 %copy-start.47 = (bf16[3,512]{1,0:T(4,128)(2,1)S(1)}, bf16[3,512]{1,0:T(4,128)(2,1)}, u32[]{:S(2)}) copy-start(bf16[3,512]{1,0:T(4,128)(2,1)} %param.22) | copy-start | bytes 9220
  149.1 112.3 %copy-start.48 = (bf16[4,512]{1,0:T(4,128)(2,1)S(1)}, bf16[4,512]{1,0:T(4,128)(2,1)}, u32[]{:S(2)}) copy-start(bf16[4,512]{1,0:T(4,128)(2,1)} %param.23) | copy-start | bytes 12292
  149.1 126.2 %copy-start.40 = (bf16[16,512]{1,0:T(8,128)(2,1)S(1)}, bf16[16,512]{1,0:T(8,128)(2,1)}, u32[]{:S(2)}) copy-start(bf16[16,512]{1,0:T(8,128)(2,1)} %param.25) | copy-start | bytes 49156
  149.2 140.9 %all-to-all-start = ((bf16[8,128,1024]{2,1,0:T(8,128)(2,1)}), bf16[8,128,1024]{2,1,0:T(8,128)(2,1)}, u32[]{:S(2)}, u32[]{:S(2)}) async-start(bf16[8,128,1024]{2,1,0:T(8,128)(2,1)} %bitcast.7), calls=%async_computation | async-start | bytes 4194304 | tf_op jit(solution)/shard_map/all_to_all | solution.py:139
  153.7 155.1 %all-gather.12.cloned.1.call-start = ((), (), s32[]{:S(2)}) async-start(), calls=%async_computation.13 | async-start | bytes 3538944 | tf_op jit(solution)/shard_map/all_gather | solution.py:144
  154.2 2750.3 %reduce-scatter.18.cloned.1.call-start = ((), (), s32[]{:S(2)}) async-start(), calls=%async_computation.18 | async-start | bytes 7077888 | tf_op jit(solution)/shard_map/reduce_scatter | solution.py:213
  289.4 19.4 copy-start.43
  289.4 21.9 copy-start.38
  289.4 23.1 copy-start.41
  289.5 4.2 copy-start.30
  300.2 3.9 copy-start.20
  2645.6 4.9 copy-start.42
  2659.5 245.1 %reduce-scatter.16.cloned.1.call-start = ((), (), s32[]{:S(2)}) async-start(), calls=%async_computation.17 | async-start | bytes 8847360 | tf_op jit(solution)/shard_map/reduce_scatter | solution.py:212
  2677.9 14.5 copy-start.1
  2692.4 9.1 copy-start.7
  2692.4 9.1 copy-start.9
  2692.4 9.1 copy-start.12
  2697.5 4.0 copy-start.3
  2697.5 4.0 copy-start.31
  2711.6 83.5 %all-to-all-start.3 = ((bf16[128,8,1024]{2,0,1:T(8,128)(2,1)}), bf16[128,8,1024]{2,0,1:T(8,128)(2,1)S(1)}, u32[]{:S(2)}, u32[]{:S(2)}) async-start(bf16[128,8,1024]{2,0,1:T(8,128)(2,1)} %bitcast.225), calls=%async_computation.4 | async-start | bytes 4194304 | tf_op jit(solution)/shard_map/all_to_all | solution.py:192
  2715.2 192.0 %reduce-scatter.22.cloned.1.call-start = ((), (), s32[]{:S(2)}) async-start(), calls=%async_computation.20 | async-start | bytes 2359296
  2717.2 224.1 %reduce-scatter.24.cloned.1.call-start = ((), (), s32[]{:S(2)}) async-start(), calls=%async_computation.21 | async-start | bytes 2359296
  2717.4 77.7 %copy-start.33 = (pred[1024]{0:T(1024)(128)(4,1)S(1)}, pred[1024]{0:T(1024)(128)(4,1)}, u32[]{:S(2)}) copy-start(pred[1024]{0:T(1024)(128)(4,1)} %copy-done.32) | copy-start | bytes 3076
  2717.4 77.7 %copy-start.35 = (pred[1024]{0:T(1024)(128)(4,1)S(1)}, pred[1024]{0:T(1024)(128)(4,1)}, u32[]{:S(2)}) copy-start(pred[1024]{0:T(1024)(128)(4,1)} %copy-done.34) | copy-start | bytes 3076
  2717.4 77.7 %copy-start.37 = (pred[1024]{0:T(1024)(128)(4,1)S(1)}, pred[1024]{0:T(1024)(128)(4,1)}, u32[]{:S(2)}) copy-start(pred[1024]{0:T(1024)(128)(4,1)} %copy-done.36) | copy-start | bytes 3076
  2719.5 312.6 %reduce-scatter.14.cloned.1.call-start = ((), (), s32[]{:S(2)}) async-start(), calls=%async_computation.16 | async-start | bytes 9437184 | tf_op jit(solution)/shard_map/reduce_scatter | solution.py:202
  2819.2 39.2 %all-to-all-start.1 = ((bf16[128,8,512]{2,0,1:T(8,128)(2,1)}), bf16[128,8,512]{2,0,1:T(8,128)(2,1)S(1)}, u32[]{:S(2)}, u32[]{:S(2)}) async-start(bf16[128,8,512]{2,0,1:T(8,128)(2,1)} %bitcast.176), calls=%async_computation.1 | async-start | bytes 2097152 | tf_op jit(solution)/shard_map/all_to_all | solution.py:171
  2823.2 240.4 %reduce-scatter.20.cloned.1.call-start = ((), (), s32[]{:S(2)}) async-start(), calls=%async_computation.19 | async-start | bytes 294912 | tf_op jit(solution)/shard_map/reduce_scatter | solution.py:217
  2824.0 329.8 %reduce-scatter.12.cloned.1.call-start = ((), (), s32[]{:S(2)}) async-start(), calls=%async_computation.14 | async-start | bytes 9437184 | tf_op jit(solution)/shard_map/reduce_scatter | solution.py:175
  2859.3 11.7 copy-start.22
  2871.0 12.2 copy-start.16
  2871.1 965.9 %all-reduce.31.cloned.1.call-start = ((), (), s32[]{:S(2)}) async-start(), calls=%async_computation.22 | async-start | bytes 79036416 | tf_op jit(solution)/shard_map/psum | solution.py:224
  2904.6 127.5 %copy-start.13 = (bf16[128,2048]{1,0:T(8,128)(2,1)S(1)}, bf16[128,2048]{1,0:T(8,128)(2,1)}, u32[]{:S(2)}) copy-start(bf16[128,2048]{1,0:T(8,128)(2,1)} %param.17) | copy-start | bytes 1572868
  2904.6 127.5 %copy-start.28 = (f32[2048]{0:T(1024)S(1)}, f32[2048]{0:T(1024)}, u32[]{:S(2)}) copy-start(f32[2048]{0:T(1024)} %copy-done.27) | copy-start | bytes 24580
  2904.6 127.5 %copy-start.46 = (f32[128]{0:T(128)S(1)}, f32[128]{0:T(128)}, u32[]{:S(2)}) copy-start(f32[128]{0:T(128)} %copy-done.45) | copy-start | bytes 1540
  2904.6 129.2 %copy-start.29 = (f32[4096]{0:T(1024)S(1)}, f32[4096]{0:T(1024)}, u32[]{:S(2)}) copy-start(f32[4096]{0:T(1024)} %get-tuple-element.721) | copy-start | bytes 49156
  2904.7 249.1 %copy-start.19 = (bf16[128,2048]{1,0:T(8,128)(2,1)S(1)}, bf16[128,2048]{1,0:T(8,128)(2,1)}, u32[]{:S(2)}) copy-start(bf16[128,2048]{1,0:T(8,128)(2,1)} %param.29) | copy-start | bytes 1572868
  3032.1 121.7 %copy-start.14 = (f32[128,2048]{1,0:T(8,128)S(1)}, f32[128,2048]{1,0:T(8,128)}, u32[]{:S(2)}) copy-start(f32[128,2048]{1,0:T(8,128)} %reduce-scatter.14.cloned.1.call-done) | copy-start | bytes 3145732
  3837.0 24.8 copy-start.24
  (21 other events, 37.8 us)
Sparse Core Ops, SparseCore 0:
  9.6 49.8 all-gather.13
  61.7 68.1 all-gather.7
  131.5 59.0 all-gather.9
  192.0 53.2 all-gather.11
  2659.6 74.1 reduce-scatter.17
  2736.0 111.2 reduce-scatter.15
  2849.6 54.9 reduce-scatter.21
  2906.9 34.4 reduce-scatter.23
  2943.7 88.3 reduce-scatter.13
  3034.8 28.7 reduce-scatter.19
  3066.0 87.7 reduce-scatter.11
  3159.3 677.6 all-reduce.30
where the time goes:
time: 3930 us; the launch traced here: 3880 us
  local copies, waits for them, and re-layouts  1710 us (44%)
  waiting for transfers between devices  1060 us (27%)
  matrix products  442 us (11%)
  other arithmetic  422 us (11%)
  blocking collectives  206 us (5%)
    dynamic_update_slice x896, local copies, waits for them, and re-layouts, mixer(): lax.scan(advance, start_state, (step_size, step_size * active, b_part, c_...  987 us
    psum x1, waiting for transfers between devices, on_device(): lax.psum((in_grad_part, out_grad_part, xw_shard, dtw_shard, dtb_shard, co...  680 us
    dynamic_slice x384, local copies, waits for them, and re-layouts, mixer(): lax.scan(advance, start_state, (step_size, step_size * active, b_part, c_...  339 us
    dot_general x256, matrix products, advance(): return (carry_state, jnp.dot(c_row, carry_state, precision=highest))  300 us
    reduce_sum x128, other arithmetic, advance(): b_row[:, None] * drive[None, :]  254 us
    squeeze x128, local copies, waits for them, and re-layouts, mixer(): lax.scan(advance, start_state, (step_size, step_size * active, b_part, c_...  155 us
    mul x256, local copies, waits for them, and re-layouts, advance(): b_row[:, None] * drive[None, :]  150 us
    dynamic_update_slice x128, other arithmetic, mixer(): lax.scan(advance, start_state, (step_size, step_size * active, b_part, c_...  121 us
  transfers between devices with their start and end apart: 16, of which 9 were waited for; matrix products, arithmetic and copies ran while one was open for 5% of the time, Pallas kernels for 0%

commit v1 on v0

v1 whole, which is shorter than its diff:
```python
import functools
import math

import jax
import jax.numpy as jnp
from jax import lax
from jax.experimental import pallas as pl
from jax.experimental.pallas import tpu as pltpu
from jax.sharding import PartitionSpec as P

F32 = jnp.float32
BF16 = jnp.bfloat16
LOG2E = math.log2(math.e)
LN2 = math.log(2.0)
GROUP = 8
VMEM_LIMIT = 58 << 20


def params(**kw):
    return pltpu.CompilerParams(vmem_limit_bytes=VMEM_LIMIT, **kw)


def dot(a, b):
    return lax.dot_general(a, b, (((1,), (0,)), ((), ())), preferred_element_type=F32)


def dot_bt(a, b):
    return lax.dot_general(a, b, (((1,), (1,)), ((), ())), preferred_element_type=F32)


def dot_at(a, b):
    return lax.dot_general(a, b, (((0,), (0,)), ((), ())), preferred_element_type=F32)


def halves(x):
    high = x.astype(BF16)
    return high, (x - high.astype(F32)).astype(BF16)


def pick(parts, label):
    total = parts[-1]
    for index in range(len(parts) - 2, -1, -1):
        total = jnp.where(label == index, parts[index], total)
    return total


def sigmoid(x):
    return 1.0 / (1.0 + jnp.exp(-x))


def select_kernel(transposed, x_ref, label_ref, w_ref, out_ref):
    x = x_ref[...]
    label = label_ref[...]
    product = dot_bt if transposed else dot
    parts = [product(x, w_ref[m]) for m in range(w_ref.shape[0])]
    out_ref[...] = pick(parts, label).astype(out_ref.dtype)


def routed_select(x, label, w, tile, transposed):
    rows, depth = x.shape
    mods = w.shape[0]
    outer = w.shape[1] if transposed else w.shape[2]
    tile = min(tile, outer)
    block = min(rows, 1024)
    if transposed:
        w_spec = pl.BlockSpec((mods, tile, depth), lambda i, j: (0, j, 0))
    else:
        w_spec = pl.BlockSpec((mods, depth, tile), lambda i, j: (0, 0, j))
    return pl.pallas_call(
        functools.partial(select_kernel, transposed),
        out_shape=jax.ShapeDtypeStruct((rows, outer), BF16),
        grid=(rows // block, outer // tile),
        in_specs=[
            pl.BlockSpec((block, depth), lambda i, j: (i, 0)),
            pl.BlockSpec((block, 1), lambda i, j: (i, 0)),
            w_spec,
        ],
        out_specs=pl.BlockSpec((block, tile), lambda i, j: (i, j)),
        compiler_params=params(),
        cost_estimate=pl.CostEstimate(
            flops=2 * rows * depth * outer * mods, bytes_accessed=2 * mods * depth * outer + 2 * rows * (depth + outer), transcendentals=0
        ),
        name="routed_select",
    )(x, label, w)


def spread_kernel(transposed, x_ref, label_ref, w_ref, out_ref):
    x = x_ref[...]
    label = label_ref[...]
    product = dot_bt if transposed else dot
    total = None
    for m in range(w_ref.shape[0]):
        part = product(jnp.where(label == m, x, jnp.zeros_like(x)), w_ref[m])
        total = part if total is None else total + part
    out_ref[...] = total.astype(out_ref.dtype)


def routed_spread(x, label, w, tile, transposed, dtype):
    rows, depth = x.shape
    mods = w.shape[0]
    outer = w.shape[1] if transposed else w.shape[2]
    tile = min(tile, outer)
    block = min(rows, 1024)
    if transposed:
        w_spec = pl.BlockSpec((mods, tile, depth), lambda i, j: (0, j, 0))
    else:
        w_spec = pl.BlockSpec((mods, depth, tile), lambda i, j: (0, 0, j))
    return pl.pallas_call(
        functools.partial(spread_kernel, transposed),
        out_shape=jax.ShapeDtypeStruct((rows, outer), dtype),
        grid=(rows // block, outer // tile),
        in_specs=[
            pl.BlockSpec((block, depth), lambda i, j: (i, 0)),
            pl.BlockSpec((block, 1), lambda i, j: (i, 0)),
            w_spec,
        ],
        out_specs=pl.BlockSpec((block, tile), lambda i, j: (i, j)),
        compiler_params=params(),
        cost_estimate=pl.CostEstimate(
            flops=2 * rows * depth * outer * mods, bytes_accessed=2 * mods * depth * outer + 2 * rows * (depth + outer), transcendentals=0
        ),
        name="routed_spread",
    )(x, label, w)


def by_time(x):
    rows, width = x.shape
    return jnp.swapaxes(x.astype(F32).reshape(GROUP, rows // GROUP, width), 0, 1).reshape(rows, width)


def by_sequence(x):
    rows, width = x.shape
    return jnp.swapaxes(x.reshape(rows // GROUP, GROUP, width), 0, 1).reshape(rows, width)


def conv_kernel(inner_ref, label_ref, cw_ref, cb_ref, xw_ref, conv_ref, inner_out_ref, proj_ref, pad_ref):
    rows, channels = inner_ref.shape
    taps = cw_ref.shape[0]
    lead = (taps - 1) * GROUP
    inner = by_time(inner_ref[...])
    inner_out_ref[...] = inner.astype(BF16)
    pad_ref[pl.ds(0, lead), :] = jnp.zeros((lead, channels), F32)
    pad_ref[pl.ds(lead, rows), :] = inner
    conv = jnp.broadcast_to(cb_ref[...].astype(F32), (rows, channels))
    for tap in range(taps):
        conv = conv + cw_ref[pl.ds(tap, 1), :].astype(F32) * pad_ref[pl.ds(tap * GROUP, rows), :]
    conv_ref[...] = conv
    high, low = halves(conv * sigmoid(conv))
    label = label_ref[...]
    parts = [dot_bt(high, xw_ref[m]) + dot_bt(low, xw_ref[m]) for m in range(xw_ref.shape[0])]
    proj_ref[...] = pick(parts, label)


def conv_forward(inner, label, cw, cb, xw):
    rows, channels = inner.shape
    wide = xw.shape[1]
    lead = (cw.shape[0] - 1) * GROUP
    return pl.pallas_call(
        conv_kernel,
        out_shape=(
            jax.ShapeDtypeStruct((rows, channels), F32),
            jax.ShapeDtypeStruct((rows, channels), BF16),
            jax.ShapeDtypeStruct((rows, wide), F32),
        ),
        scratch_shapes=[pltpu.VMEM((rows + lead, channels), F32)],
        compiler_params=params(),
        name="conv_forward",
    )(inner, label, cw, cb[None, :], xw)


def scan_kernel(
    conv_ref, proj_ref, gate_ref, grad_ref, label_ref, dtw_ref, dtb_ref, alog_ref, skip_ref,
    gated_ref, dgate_ref, dact_ref, dproj_ref, ddtw_ref, ddtb_ref, dalog_ref, dskip_ref,
    hist, mix, prod, rate, drate, act, step, slope, dout, scanned, ddrive, dstep, dlow,
):
    rows, width = conv_ref.shape
    length = rows // GROUP
    states = alog_ref.shape[0]
    mods, low_width = dtw_ref.shape[0], dtw_ref.shape[1]
    tile = pl.program_id(0)
    label = label_ref[...]

    @pl.when(tile == 0)
    def _():
        prod[...] = jnp.zeros_like(prod)
        dlow[...] = jnp.zeros_like(dlow)
        for s in range(2 * states):
            mix[s] = jnp.broadcast_to(proj_ref[:, pl.ds(low_width + s, 1)], (rows, width))

    low_rank = proj_ref[:, pl.ds(0, low_width)]
    low_high, low_low = halves(low_rank)
    parts = [
        dot(low_high, dtw_ref[m]) + dot(low_low, dtw_ref[m]) + dtb_ref[pl.ds(m, 1), :].astype(F32) for m in range(mods)
    ]
    speed = pick(parts, label)
    step[...] = jnp.maximum(speed, 0.0) + jnp.log1p(jnp.exp(-jnp.abs(speed)))
    slope[...] = sigmoid(speed)
    conv = conv_ref[...]
    act[...] = conv * sigmoid(conv)
    for s in range(states):
        rate[s] = jnp.broadcast_to(-LOG2E * jnp.exp(alog_ref[pl.ds(s, 1), :].astype(F32)), (GROUP, width))
        drate[s] = jnp.zeros((GROUP, width), F32)
        hist[0, s] = jnp.zeros((GROUP, width), F32)

    def forward(t, state):
        at = pl.ds(pl.multiple_of(t * GROUP, GROUP), GROUP)
        now = step[at, :]
        drive = now * act[at, :]
        total = None
        new = []
        for s in range(states):
            value = jnp.exp2(now * rate[s]) * state[s] + mix[s, at, :] * drive
            hist[t + 1, s] = value
            new.append(value)
            term = mix[states + s, at, :] * value
            total = term if total is None else total + term
        scanned[at, :] = total
        return tuple(new)

    zero = jnp.zeros((GROUP, width), F32)
    lax.fori_loop(0, length, forward, (zero,) * states)

    gate = by_time(gate_ref[...])
    grad = by_time(grad_ref[...])
    soft = sigmoid(gate)
    opened = gate * soft
    skip = skip_ref[...].astype(F32)
    summed = scanned[...] + skip * act[...]
    gated_ref[...] = by_sequence(summed * opened).astype(BF16)
    dgate = grad * summed * (soft + opened * (1.0 - soft))
    dgate_ref[...] = by_sequence(dgate).astype(BF16)
    dsummed = grad * opened
    dout[...] = dsummed
    dskip_ref[...] = jnp.sum(dsummed * act[...], axis=0, keepdims=True)

    def backward(i, carry):
        t = length - 1 - i
        at = pl.ds(pl.multiple_of(t * GROUP, GROUP), GROUP)
        now = step[at, :]
        drive = now * act[at, :]
        out = dout[at, :]
        dd, ds = None, None
        new = []
        for s in range(states):
            decay = jnp.exp2(now * rate[s])
            dstate = carry[s] + mix[states + s, at, :] * out
            prod[states + s, at, :] += out * hist[t + 1, s]
            prod[s, at, :] += dstate * drive
            term = dstate * mix[s, at, :]
            dd = term if dd is None else dd + term
            passed = dstate * decay
            new.append(passed)
            change = passed * hist[t, s]
            term = change * rate[s]
            ds = term if ds is None else ds + term
            drate[s] += change * now
        ddrive[at, :] = dd
        dstep[at, :] = ds
        return tuple(new)

    lax.fori_loop(0, length, backward, (zero,) * states)

    for s in range(states):
        dalog_ref[pl.ds(s, 1), :] = LN2 * jnp.sum(drate[s] * rate[s], axis=0, keepdims=True)
    dact_ref[...] = ddrive[...] * step[...] + skip * dout[...]
    dspeed = (dstep[...] * LN2 + ddrive[...] * act[...]) * slope[...]
    high, low = halves(dspeed)
    parts = [dot_bt(high, dtw_ref[m]) + dot_bt(low, dtw_ref[m]) for m in range(mods)]
    dlow[...] += pick(parts, label)
    for m in range(mods):
        own = label == m
        masked = jnp.where(own, dspeed, 0.0)
        high, low = halves(masked)
        ddtw_ref[m] = dot_at(low_high, high) + dot_at(low_high, low) + dot_at(low_low, high)
        ddtb_ref[pl.ds(m, 1), :] = jnp.sum(masked, axis=0, keepdims=True)

    @pl.when(tile == pl.num_programs(0) - 1)
    def _():
        column = lax.broadcasted_iota(jnp.int32, (rows, 2 * states), 1)
        sums = jnp.zeros((rows, 2 * states), F32)
        for s in range(2 * states):
            sums = jnp.where(column == s, jnp.sum(prod[s], axis=1, keepdims=True), sums)
        dproj_ref[:, pl.ds(0, low_width)] = dlow[...]
        dproj_ref[:, pl.ds(low_width, 2 * states)] = sums


def scan_both(conv, proj, gate, grad, label, dtw, dtb, alog, skip):
    rows, channels = conv.shape
    width = min(128, channels)
    length = rows // GROUP
    states = alog.shape[0]
    mods, low_width = dtw.shape[0], dtw.shape[1]
    wide = proj.shape[1]

    def whole(shape):
        return pl.BlockSpec(shape, lambda j: (0,) * len(shape), pipeline_mode=pl.Buffered(1))

    def cut(*shape):
        return pl.BlockSpec(shape + (width,), lambda j: (0,) * len(shape) + (j,))

    plane = (GROUP, width)
    flat = pltpu.VMEM((rows, width), F32)
    return pl.pallas_call(
        scan_kernel,
        out_shape=(
            jax.ShapeDtypeStruct((rows, channels), BF16),
            jax.ShapeDtypeStruct((rows, channels), BF16),
            jax.ShapeDtypeStruct((rows, channels), F32),
            jax.ShapeDtypeStruct((rows, wide), F32),
            jax.ShapeDtypeStruct((mods, low_width, channels), F32),
            jax.ShapeDtypeStruct((mods, channels), F32),
            jax.ShapeDtypeStruct((states, channels), F32),
            jax.ShapeDtypeStruct((1, channels), F32),
        ),
        grid=(channels // width,),
        in_specs=[
            cut(rows), whole((rows, wide)), cut(rows), cut(rows), whole((rows, 1)),
            cut(mods, low_width), cut(mods), cut(states), cut(1),
        ],
        out_specs=(
            cut(rows), cut(rows), cut(rows), whole((rows, wide)), cut(mods, low_width), cut(mods), cut(states), cut(1),
        ),
        scratch_shapes=[
            pltpu.VMEM((length + 1, states) + plane, F32),
            pltpu.VMEM((2 * states, rows, width), F32),
            pltpu.VMEM((2 * states, rows, width), F32),
            pltpu.VMEM((states,) + plane, F32),
            pltpu.VMEM((states,) + plane, F32),
            flat, flat, flat, flat, flat, flat, flat,
            pltpu.VMEM((rows, low_width), F32),
        ],
        compiler_params=params(),
        name="scan_both",
    )(conv, proj, gate, grad, label, dtw, dtb, alog, skip[None, :])


def conv_back_kernel(
    conv_ref, inner_ref, dact_ref, dproj_ref, label_ref, cw_ref, xw_ref,
    dinner_ref, dxw_ref, dcw_ref, dcb_ref, pad_ref,
):
    rows, channels = conv_ref.shape
    taps = cw_ref.shape[0]
    tail = (taps - 1) * GROUP
    label = label_ref[...]
    conv = conv_ref[...]
    soft = sigmoid(conv)
    act = conv * soft
    dproj = dproj_ref[...]
    high, low = halves(dproj)
    parts = [dot(high, xw_ref[m]) + dot(low, xw_ref[m]) for m in range(xw_ref.shape[0])]
    dact = dact_ref[...] + pick(parts, label)
    act_high, act_low = halves(act)
    for m in range(xw_ref.shape[0]):
        high, low = halves(jnp.where(label == m, dproj, 0.0))
        dxw_ref[m] = dot_at(high, act_high) + dot_at(low, act_high) + dot_at(high, act_low)
    dconv = dact * (soft + act * (1.0 - soft))
    dcb_ref[...] = jnp.sum(dconv, axis=0, keepdims=True)
    pad_ref[pl.ds(0, rows), :] = dconv
    pad_ref[pl.ds(rows, tail), :] = jnp.zeros((tail, channels), F32)
    inner = inner_ref[...].astype(F32)
    total = None
    for tap in range(taps):
        shift = (taps - 1 - tap) * GROUP
        later = pad_ref[pl.ds(shift, rows), :]
        term = cw_ref[pl.ds(tap, 1), :].astype(F32) * later
        total = term if total is None else total + term
        dcw_ref[pl.ds(tap, 1), :] = jnp.sum(later * inner, axis=0, keepdims=True)
    dinner_ref[...] = by_sequence(total).astype(BF16)


def conv_backward(conv, inner, dact, dproj, label, cw, xw):
    rows, channels = conv.shape
    mods, wide = xw.shape[0], xw.shape[1]
    taps = cw.shape[0]
    return pl.pallas_call(
        conv_back_kernel,
        out_shape=(
            jax.ShapeDtypeStruct((rows, channels), BF16),
            jax.ShapeDtypeStruct((mods, wide, channels), F32),
            jax.ShapeDtypeStruct((taps, channels), F32),
            jax.ShapeDtypeStruct((1, channels), F32),
        ),
        scratch_shapes=[pltpu.VMEM((rows + (taps - 1) * GROUP, channels), F32)],
        compiler_params=params(),
        name="conv_backward",
    )(conv, inner, dact, dproj, label, cw, xw)


def by_groups(fn, count, arrays, joined):
    if count == 1:
        return fn(*arrays)
    size = arrays[0].shape[0] // count
    outs = [fn(*(a[i * size : (i + 1) * size] for a in arrays)) for i in range(count)]
    return tuple(
        jnp.concatenate(values, axis=0) if at < joined else functools.reduce(jnp.add, values)
        for at, values in enumerate(zip(*outs, strict=True))
    )


def exchange_pairs(n):
    half = n // 2
    first = [(c, 2 * c) if c < half else (c, 2 * (c - half) + 1) for c in range(n)]
    second = [(c, 2 * c + 1) if c < half else (c, 2 * (c - half)) for c in range(n)]
    return first, second


def to_owners(xz, n):
    first, second = exchange_pairs(n)
    c = lax.axis_index("ch")
    width = xz.shape[1] // 2
    left, right = xz[:, :width], xz[:, width:]
    lower = c < n // 2
    one = lax.ppermute(jnp.where(lower, left, right), "ch", first)
    two = lax.ppermute(jnp.where(lower, right, left), "ch", second)
    even = c % 2 == 0
    return jnp.where(even, one, two), jnp.where(even, two, one)


def to_columns(dinner, dgate, n):
    first, second = exchange_pairs(n)
    c = lax.axis_index("ch")
    even = c % 2 == 0
    one = lax.ppermute(jnp.where(even, dinner, dgate), "ch", [(b, a) for a, b in first])
    two = lax.ppermute(jnp.where(even, dgate, dinner), "ch", [(b, a) for a, b in second])
    lower = c < n // 2
    return jnp.concatenate([jnp.where(lower, one, two), jnp.where(lower, two, one)], axis=1)


def weight_grad(left, right, label, mods, spread_left):
    parts = []
    for m in range(mods):
        own = (label == m)[:, None]
        if spread_left:
            parts.append(dot_at(jnp.where(own, left, jnp.zeros_like(left)), right))
        else:
            parts.append(dot_at(left, jnp.where(own, right, jnp.zeros_like(right))))
    return jnp.stack(parts)


def on_device(
    n,
    block_input,
    norm_gain,
    in_weight,
    x_weight,
    dt_weight,
    dt_bias,
    conv_weight,
    conv_bias,
    a_log,
    skip_gain,
    out_weight,
    modality,
    cotangent,
):
    mods = in_weight.shape[0]
    length = block_input.shape[0]
    count = n // GROUP
    rows_float = block_input.astype(F32)
    gain = norm_gain.astype(F32)
    inverse = lax.rsqrt(jnp.mean(rows_float * rows_float, axis=-1, keepdims=True) + 1e-05)
    normed = rows_float * inverse
    scaled = (normed * gain[None, :]).astype(BF16)

    group_rows = lax.all_gather(scaled, "ch", axis=0, tiled=True)
    every_label = lax.all_gather(modality, ("tok", "ch"), axis=0, tiled=True)
    token_group = n * length
    group_label = lax.dynamic_slice_in_dim(every_label, lax.axis_index("tok") * token_group, token_group, 0)
    label = group_label[:, None]
    label_by_time = group_label.reshape(count, GROUP, length).transpose(0, 2, 1).reshape(token_group, 1)

    xz = routed_select(group_rows, label, in_weight, 256, False)
    inner, gate = to_owners(xz, n)
    group_cot = lax.all_gather(cotangent, "ch", axis=0, tiled=True)
    gated_grad = routed_select(group_cot, label, out_weight, 128, True)

    conv, inner_by_time, proj_part = by_groups(
        lambda a, b: conv_forward(a, b, conv_weight, conv_bias, x_weight), count, (inner, label_by_time), 3
    )
    proj = lax.psum(proj_part, "ch")

    gated, dgate, dact, dproj_part, ddtw, ddtb, dalog, dskip = by_groups(
        lambda a, b, c, d, e: scan_both(a, b, c, d, e, dt_weight, dt_bias, a_log, skip_gain),
        count,
        (conv, proj, gate, gated_grad, label_by_time),
        4,
    )
    dproj = lax.psum(dproj_part, "ch")

    dinner, dxw, dcw, dcb = by_groups(
        lambda a, b, c, d, e: conv_backward(a, b, c, d, e, conv_weight, x_weight),
        count,
        (conv, inner_by_time, dact, dproj, label_by_time),
        1,
    )
    xz_grad = to_columns(dinner, dgate, n)

    branch_part = routed_spread(gated, label, out_weight, 512, False, BF16)
    branch = lax.psum_scatter(branch_part, "ch", scatter_dimension=0, tiled=True).astype(F32)
    block_out = (rows_float + branch).astype(BF16)

    scaled_part = routed_spread(xz_grad, label, in_weight, 256, True, BF16)
    scaled_grad = lax.psum_scatter(scaled_part, "ch", scatter_dimension=0, tiled=True).astype(F32)
    gain_grad = jnp.sum(scaled_grad * normed, axis=0)
    ng = scaled_grad * gain[None, :]
    row_grad = cotangent.astype(F32) + inverse * (ng - normed * jnp.mean(ng * normed, axis=-1, keepdims=True))

    every_scaled = lax.all_gather(scaled, ("tok", "ch"), axis=0, tiled=True)
    every_cot = lax.all_gather(cotangent, ("tok", "ch"), axis=0, tiled=True)
    every_gated = lax.all_gather(gated, "tok", axis=0, tiled=True)
    every_grad = lax.all_gather(xz_grad, "tok", axis=0, tiled=True)
    out_weight_grad = weight_grad(every_gated, every_cot, every_label, mods, True)
    in_weight_grad = weight_grad(every_scaled, every_grad, every_label, mods, False)

    small = lax.psum((dxw, ddtw, ddtb, dcw, dcb, dalog, dskip), "tok")
    gain_grad = lax.psum(gain_grad, ("tok", "ch"))
    own = gain_grad.shape[0] // n
    gain_grad = lax.dynamic_slice_in_dim(gain_grad, lax.axis_index("ch") * own, own, 0)
    dxw, ddtw, ddtb, dcw, dcb, dalog, dskip = small
    return (
        block_out,
        row_grad,
        gain_grad,
        in_weight_grad,
        dxw,
        ddtw,
        ddtb,
        dcw,
        dcb[0],
        dalog,
        dskip[0],
        out_weight_grad,
    )


def solution(mesh):
    placed = (
        P(("tok", "ch"), None),
        P(),
        P(None, None, "ch"),
        P(None, None, "ch"),
        P(None, None, "ch"),
        P(None, "ch"),
        P(None, "ch"),
        P("ch"),
        P(None, "ch"),
        P("ch"),
        P(None, "ch", None),
        P(("tok", "ch")),
        P(("tok", "ch"), None),
    )
    return jax.shard_map(
        functools.partial(on_device, mesh.shape["ch"]),
        mesh=mesh,
        in_specs=placed,
        out_specs=(
            P(("tok", "ch"), None),
            P(("tok", "ch"), None),
            P("ch"),
            P(None, None, "ch"),
            P(None, None, "ch"),
            P(None, None, "ch"),
            P(None, "ch"),
            P(None, "ch"),
            P("ch"),
            P(None, "ch"),
            P("ch"),
            P(None, "ch", None),
        ),
        check_vma=False,
    )
```

time: 3930 us -> 1020 us (0.26); the launches traced: 3880 us -> 1020 us
  local copies, waits for them, and re-layouts: 1710 us -> 8.32 us
  waiting for transfers between devices: 1060 us -> 566 us
  other arithmetic: 422 us -> 43.7 us
  matrix products: 442 us -> 124 us
  Pallas kernels: 0 us -> 153 us
  blocking collectives: 206 us -> 101 us
    dynamic_update_slice x896 -> x0, local copies, waits for them, and re-layouts: 987 us -> none  [mixer(): lax.scan(advance, start_state, (step_size, step_size * active, b_part, c_...]
    psum x1 -> x3, waiting for transfers between devices: 680 us -> 120 us  [the longest x1 62.3 us: on_device(): proj = lax.psum(proj_part, 'ch')]
    dynamic_slice x384 -> x2, local copies, waits for them, and re-layouts: 339 us -> 0.64 us  [the longest x1 0.63 us: on_device(): lax.dynamic_slice_in_dim(gain_grad, lax.axis_index('ch') * own, own, 0)]
    dot_general x280 -> x6, matrix products: 442 us -> 124 us  [dot_at(): lax.dot_general(a, b, (((0,), (0,)), ((), ())), preferred_element_type=F32)]
    reduce_sum x131 -> x1, other arithmetic: 265 us -> 1.47 us  [on_device(): gain_grad = jnp.sum(scaled_grad * normed, axis=0)]
    all_gather x4 -> x6, waiting for transfers between devices: 70.7 us -> 325 us  [the longest x1 118 us: on_device(): every_scaled = lax.all_gather(scaled, ('tok', 'ch'), axis=0, tiled=True)]
    squeeze x128 -> x0, local copies, waits for them, and re-layouts: 155 us -> none  [mixer(): lax.scan(advance, start_state, (step_size, step_size * active, b_part, c_...]
    pallas_call x0 -> x7, Pallas kernels: none -> 153 us  [the longest x1 74.4 us: scan_both(): pl.pallas_call(scan_kernel, out_shape=(jax.ShapeDtypeStruct((rows, channe...]
  transfers between devices with their start and end apart: 16 -> 15, of which waited for: 9 -> 11; matrix products, arithmetic and copies ran while one was open for 5% -> 16% of each run, Pallas kernels for 0% -> 5%
where the time goes in v1:
time: 1020 us
  waiting for transfers between devices  566 us (55%)
  Pallas kernels  153 us (15%)
  matrix products  124 us (12%)
  blocking collectives  101 us (10%)
  other arithmetic  43.7 us (4%)
  between operations  14.5 us (1%)
    dot_general x6, matrix products, dot_at(): lax.dot_general(a, b, (((0,), (0,)), ((), ())), preferred_element_type=F32)  124 us
    all_gather x1, waiting for transfers between devices, on_device(): every_scaled = lax.all_gather(scaled, ('tok', 'ch'), axis=0, tiled=True)  118 us
    all_gather x1, waiting for transfers between devices, on_device(): every_cot = lax.all_gather(cotangent, ('tok', 'ch'), axis=0, tiled=True)  118 us
    all_gather x1, waiting for transfers between devices, on_device(): every_grad = lax.all_gather(xz_grad, 'tok', axis=0, tiled=True)  84.8 us
    pallas_call x1, Pallas kernels, scan_both(): pl.pallas_call(scan_kernel, out_shape=(jax.ShapeDtypeStruct((rows, channe...  74.4 us
    psum x1, waiting for transfers between devices, on_device(): proj = lax.psum(proj_part, 'ch')  62.3 us
    psum x1, waiting for transfers between devices, on_device(): dproj = lax.psum(dproj_part, 'ch')  58 us
    ppermute x1, waiting for transfers between devices, to_owners(): two = lax.ppermute(jnp.where(lower, right, left), 'ch', second)  44.8 us
  transfers between devices with their start and end apart: 15, of which 11 were waited for; matrix products, arithmetic and copies ran while one was open for 16% of the time, Pallas kernels for 5%

profile of v1, /device:TPU:0, one launch (start us, length us, event | category | flops | bytes accessed | tf_op | source)
XLA Modules:
  0.0 1016.9 jit_solution(8062140088777223801)
XLA Ops:
  7.2 0.7 convert_element_type.22
  7.9 1.2 fusion.52
  9.2 2.1 fusion.49
  11.3 0.7 all-gather.10.cloned.1.call-update
  12.0 43.7 %all-gather = s32[32,1,128]{2,1,0:T(1,128)S(1)} all-gather(s32[1,1,128]{2,1,0:T(1,128)} %bitcast.33), channel_id=1, replica_groups=mesh['tok'=4,'ch'=8] {'tok','ch'}, dimensions={0}, use_global_device_ids=true | all-gather | bytes 16896 | tf_op jit(solution)/shard_map/all_gather | solution.py:466
  55.7 1.0 copy.33.label_ref
  56.7 4.5 all-gather.8.cloned.1.call-done.x_ref
  61.3 17.7 %routed_select.2 = bf16[1024,1024]{1,0:T(8,128)(2,1)} custom-call(bf16[1024,2048]{1,0:T(8,128)(2,1)} %all-gather.8.cloned.1.call-done.x_ref, s32[1024,1]{1,0:T(8,128)} %copy.33.label_ref, bf16[3,2048,1024]{2,1,0:T(8,128)(2,1)} %w_ref.7), custom_call_target="tpu_custom_call" | custom-call | flops 12884901888 | bytes 18874368 | tf_op jit(solution)/shard_map/routed_select/pallas_call | solution.py:69
  79.0 2.6 broadcast_select_fusion.2
  82.0 0.7 collective-permute-start
  82.8 1.1 reshape.50.label_ref
  85.1 44.8 %collective-permute-done.1 = bf16[1024,512]{1,0:T(8,128)(2,1)S(1)} collective-permute-done((bf16[1024,512]{1,0:T(8,128)(2,1)}, bf16[1024,512]{1,0:T(8,128)(2,1)S(1)}, u32[]{:S(2)}, u32[]{:S(2)}) %collective-permute-start.1) | collective-permute-done | bytes 1048608 | tf_op jit(solution)/shard_map/ppermute | solution.py:414
  129.9 1.5 broadcast_select_fusion.6
  131.3 5.6 conv_forward.1
  137.0 17.4 %routed_select.3.grad_ref = bf16[1024,512]{1,0:T(8,128)(2,1)} custom-call(bf16[1024,2048]{1,0:T(8,128)(2,1)} %all-gather.10.cloned.1.call-done.x_ref, s32[1024,1]{1,0:T(8,128)} %copy.33.label_ref, bf16[3,512,2048]{2,1,0:T(8,128)(2,1)} %w_ref.6), custom_call_target="tpu_custom_call" | custom-call | flops 6442450944 | bytes 11534336 | tf_op jit(solution)/shard_map/routed_select/pallas_call | solution.py:69
  154.3 62.3 %all-reduce.6.cloned.1.call-done.proj_ref = f32[1024,160]{1,0:T(8,128)} async-done(((f32[1024,160]{1,0:T(8,128)}), f32[1024,160]{1,0:T(8,128)}) %all-reduce.6.cloned.1.call-update) | async-done | bytes 655376 | tf_op jit(solution)/shard_map/psum | solution.py:480
  216.6 74.4 %scan_both.1 = (bf16[1024,512]{1,0:T(8,128)(2,1)}, bf16[1024,512]{1,0:T(8,128)(2,1)}, f32[1024,512]{1,0:T(8,128)}, f32[1024,160]{1,0:T(8,128)}, f32[3,128,512]{2...) custom-call(f32[1024,512]{1,0:T(8,128)} %get-tuple-element.27.conv_ref, ...), custom_call_target="tpu_custom_call" | custom-call | tf_op jit(solution)/shard_map/scan_both/pallas_call | solution.py:303
  291.1 58.0 %all-reduce.8.cloned.1.call-done.dproj_ref = f32[1024,160]{1,0:T(8,128)} async-done(((f32[1024,160]{1,0:T(8,128)}), f32[1024,160]{1,0:T(8,128)}) %all-reduce.8.cloned.1.call-update) | async-done | bytes 655376 | tf_op jit(solution)/shard_map/psum | solution.py:488
  349.1 9.7 conv_backward.1
  358.8 1.4 broadcast_select_fusion.5
  360.2 0.7 collective-permute-start.2
  360.9 3.4 collective-permute-start.3
  364.3 22.2 %collective-permute-done.3 = bf16[1024,512]{1,0:T(8,128)(2,1)S(1)} collective-permute-done((bf16[1024,512]{1,0:T(8,128)(2,1)S(1)}, bf16[1024,512]{1,0:T(8,128)(2,1)S(1)}, u32[]{:S(2)}, u32[]{:S(2)}) %collective-permute-start.3) | collective-permute-done | bytes 1048608 | tf_op jit(solution)/shard_map/ppermute | solution.py:424
  386.6 1.6 pad_maximum_fusion.2.x_ref
  388.3 18.2 %routed_spread.3 = bf16[1024,2048]{1,0:T(8,128)(2,1)} custom-call(bf16[1024,1024]{1,0:T(8,128)(2,1)} %pad_maximum_fusion.2.x_ref, s32[1024,1]{1,0:T(8,128)} %copy.33.label_ref, bf16[3,2048,1024]{2,1,0:T(8,128)(2,1)} %w_ref.7), custom_call_target="tpu_custom_call" | custom-call | flops 12884901888 | bytes 18874368 | tf_op jit(solution)/shard_map/routed_spread/pallas_call | solution.py:108
  406.5 10.3 %routed_spread.2 = bf16[1024,2048]{1,0:T(8,128)(2,1)} custom-call(bf16[1024,512]{1,0:T(8,128)(2,1)} %get-tuple-element.29.x_ref, s32[1024,1]{1,0:T(8,128)} %copy.33.label_ref, bf16[3,512,2048]{2,1,0:T(8,128)(2,1)} %w_ref.6), custom_call_target="tpu_custom_call" | custom-call | flops 6442450944 | bytes 11534336 | tf_op jit(solution)/shard_map/routed_spread/pallas_call | solution.py:108
  417.0 0.7 all-gather.14.cloned.1.call-update
  417.7 0.7 all-gather.12.cloned.1.call-update
  418.5 0.7 all-gather.16.cloned.1.call-update
  420.5 17.4 %all-reduce = (f32[3,512]{1,0:T(4,128)}, f32[4,512]{1,0:T(4,128)}, f32[512]{0:T(512)}, f32[16,512]{1,0:T(8,128)}, f32[512]{0:T(512)}) all-reduce(f32[3,512]{1,0:T(4,128)S(1)} %copy-done.4, f32[4,512]{1,0:T(4,128)S(1)} %copy-done.5, f32[512]{0:T(512)S(1)} %bitcast.32, ...), channel_id=1, replica_groups=mesh['tok'=4,'ch'=8] {'tok'}, use_global_device_ids=true, to_apply=%region_10.11 | all-reduce | flops 12800 | bytes 102400 | tf_op jit(solution)/shard_map/psum | solution.py:515
  438.0 39.7 %reduce-scatter.5.cloned.1.call-done = bf16[128,2048]{1,0:T(8,128)(2,1)} async-done(((bf16[1024,2048]{1,0:T(8,128)(2,1)}), bf16[128,2048]{1,0:T(8,128)(2,1)}) %reduce-scatter.5.cloned.1.call-update) | async-done | bytes 524304 | tf_op jit(solution)/shard_map/reduce_scatter | solution.py:503
  477.7 1.5 fusion.51
  479.2 40.1 %psum.72 = f32[2048]{0:T(1024)S(1)} all-reduce(f32[2048]{0:T(1024)S(1)} %get-tuple-element.42), channel_id=1, replica_groups=mesh['tok'=4,'ch'=8] {'tok','ch'}, use_global_device_ids=true, to_apply=%region_7.8 | all-reduce | flops 2048 | bytes 16384 | tf_op jit(solution)/shard_map/psum | solution.py:516
  519.9 9.7 reduce-scatter.3.cloned.1.call-done
  529.6 2.8 fusion.48
  532.4 84.8 %all-gather.14.cloned.1.call-done = bf16[4096,1024]{1,0:T(8,128)(2,1)} async-done(((bf16[1024,1024]{1,0:T(8,128)(2,1)}), bf16[4096,1024]{1,0:T(8,128)(2,1)}) %all-gather.14.cloned.1.call-update) | async-done | bytes 8388624 | tf_op jit(solution)/shard_map/all_gather | solution.py:511
  617.3 118.0 %all-gather.12.cloned.1.call-done = bf16[4096,2048]{1,0:T(8,128)(2,1)} async-done(((bf16[128,2048]{1,0:T(8,128)(2,1)}), bf16[4096,2048]{1,0:T(8,128)(2,1)}) %all-gather.12.cloned.1.call-update) | async-done | bytes 16777232 | tf_op jit(solution)/shard_map/all_gather | solution.py:508
  735.2 25.8 %fusion.15 = f32[1,2048,1024]{2,1,0:T(8,128)} fusion(bf16[4096,2048]{1,0:T(8,128)(2,1)} %all-gather.12.cloned.1.call-done, bf16[4096,1024]{1,0:T(8,128)(2,1)} %all-gather.14.cloned.1.call-done, pred[4096]{0:T(1024)(128)(4,1)S(1)} %get-tuple-element.62), kind=kOutput, calls=%fused_computation.13 | convolution fusion | flops 17184063488 | bytes 33558528 | tf_op jit(solution)/shard_map/dot_general | solution.py:32
  761.0 26.7 %fusion.12 = f32[1,2048,1024]{2,1,0:T(8,128)} fusion(bf16[4096,2048]{1,0:T(8,128)(2,1)} %all-gather.12.cloned.1.call-done, bf16[4096,1024]{1,0:T(8,128)(2,1)} %all-gather.14.cloned.1.call-done, pred[4096]{0:T(1024)(128)(4,1)S(1)} %get-tuple-element.63), kind=kOutput, calls=%fused_computation.12 | convolution fusion | flops 17184063488 | bytes 33558528 | tf_op jit(solution)/shard_map/dot_general | solution.py:32
  788.0 117.8 %all-gather.18.cloned.1.call-done = bf16[4096,2048]{1,0:T(8,128)(2,1)} async-done(((bf16[128,2048]{1,0:T(8,128)(2,1)}), bf16[4096,2048]{1,0:T(8,128)(2,1)}) %all-gather.18.cloned.1.call-update) | async-done | bytes 16777232 | tf_op jit(solution)/shard_map/all_gather | solution.py:509
  905.8 16.0 %fusion.36 = f32[1,512,2048]{2,1,0:T(8,128)S(1)} fusion(bf16[4096,2048]{1,0:T(8,128)(2,1)} %all-gather.18.cloned.1.call-done, bf16[4096,512]{1,0:T(8,128)(2,1)} %all-gather.16.cloned.1.call-done, pred[4096]{0:T(1024)(128)(4,1)S(1)} %get-tuple-element.62), kind=kOutput, calls=%fused_computation.28 | convolution fusion | flops 8592031744 | bytes 25169920 | tf_op jit(solution)/shard_map/dot_general | solution.py:32
  921.8 14.3 %fusion.33 = f32[1,512,2048]{2,1,0:T(8,128)} fusion(bf16[4096,2048]{1,0:T(8,128)(2,1)} %all-gather.18.cloned.1.call-done, bf16[4096,512]{1,0:T(8,128)(2,1)S(1)} %copy-done.10, pred[4096]{0:T(1024)(128)(4,1)S(1)} %get-tuple-element.63), kind=kOutput, calls=%fused_computation.27 | convolution fusion | flops 8592031744 | bytes 25169920 | tf_op jit(solution)/shard_map/dot_general | solution.py:32
  936.1 25.9 %fusion.9 = f32[1,2048,1024]{2,1,0:T(8,128)} fusion(bf16[4096,2048]{1,0:T(8,128)(2,1)} %all-gather.12.cloned.1.call-done, bf16[4096,1024]{1,0:T(8,128)(2,1)} %all-gather.14.cloned.1.call-done, pred[4096]{0:T(1024)(128)(4,1)S(1)} %get-tuple-element.61), kind=kOutput, calls=%fused_computation.11 | convolution fusion | flops 17184063488 | bytes 33558528 | tf_op jit(solution)/shard_map/dot_general | solution.py:32
  962.0 15.5 %fusion.30 = f32[1,512,2048]{2,1,0:T(8,128)} fusion(bf16[4096,2048]{1,0:T(8,128)(2,1)} %all-gather.18.cloned.1.call-done, bf16[4096,512]{1,0:T(8,128)(2,1)} %all-gather.16.cloned.1.call-done, pred[4096]{0:T(1024)(128)(4,1)S(1)} %get-tuple-element.61), kind=kOutput, calls=%fused_computation.26 | convolution fusion | flops 8592031744 | bytes 25169920 | tf_op jit(solution)/shard_map/dot_general | solution.py:32
  977.5 10.1 pad_maximum_fusion.1
  987.6 18.1 %pad_maximum_fusion = f32[3,2048,1024]{2,1,0:T(8,128)} fusion(f32[1,2048,1024]{2,1,0:T(8,128)} %fusion.15, f32[1,2048,1024]{2,1,0:T(8,128)} %fusion.12, f32[1,2048,1024]{2,1,0:T(8,128)} %fusion.9), kind=kLoop, calls=%fused_computation | loop fusion | flops 12582912 | bytes 50331648 | tf_op jit(solution)/shard_map/stack | solution.py:437
  1005.6 2.2 copy.45
  1007.8 2.1 copy.46
  (56 shorter events, 4.5 us)
Async XLA Ops:
  7.2 54.1 %all-gather.8.cloned.1.call-start = ((), (), s32[]{:S(2)}) async-start(), calls=%async_computation.2 | async-start | bytes 4718592 | tf_op jit(solution)/shard_map/all_gather | solution.py:465
  11.2 125.7 %all-gather.10.cloned.1.call-start = ((), (), s32[]{:S(2)}) async-start(), calls=%async_computation.4 | async-start | bytes 4718592 | tf_op jit(solution)/shard_map/all_gather | solution.py:474
  12.0 204.6 %all-reduce.6.cloned.1.call-start = ((), (), s32[]{:S(2)}) async-start(), calls=%async_computation.3 | async-start | bytes 2097152 | tf_op jit(solution)/shard_map/psum | solution.py:480
  56.7 27.2 %copy-start.8 = (bf16[512]{0:T(512)(128)(2,1)S(1)}, bf16[512]{0:T(512)(128)(2,1)}, u32[]{:S(2)}) copy-start(bf16[512]{0:T(512)(128)(2,1)} %param.20) | copy-start | bytes 3076
  56.7 27.8 %copy-start.9 = (bf16[512]{0:T(512)(128)(2,1)S(1)}, bf16[512]{0:T(512)(128)(2,1)}, u32[]{:S(2)}) copy-start(bf16[512]{0:T(512)(128)(2,1)} %param.22) | copy-start | bytes 3076
  81.7 48.2 %collective-permute-start.1 = (bf16[1024,512]{1,0:T(8,128)(2,1)}, bf16[1024,512]{1,0:T(8,128)(2,1)S(1)}, u32[]{:S(2)}, u32[]{:S(2)}) collective-permute-start(bf16[1024,512]{1,0:T(8,128)(2,1)} %get-tuple-element.57), channel_id=1, source_target_pairs={{0,1},{1,3},{2,5},{3,7},{4,0},{5,2},{6,4},{7,6},{8,9},{9,11},{10,1... | collective-permute-start | bytes 3145736 | tf_op jit(solution)/shard_map/ppermute | solution.py:414
  82.0 47.9 %collective-permute-start = (bf16[1024,512]{1,0:T(8,128)(2,1)S(1)}, bf16[1024,512]{1,0:T(8,128)(2,1)S(1)}, u32[]{:S(2)}, u32[]{:S(2)}) collective-permute-start(bf16[1024,512]{1,0:T(8,128)(2,1)S(1)} %get-tuple-element.58), channel_id=1, source_target_pairs={{0,0},{1,2},{2,4},{3,6},{4,1},{5,3},{6,5},{7,7},{8,8},{9,10},{10,1... | collective-permute-start | bytes 3145736 | tf_op jit(solution)/shard_map/ppermute | solution.py:413
  136.9 212.2 %all-reduce.8.cloned.1.call-start = ((), (), s32[]{:S(2)}) async-start(), calls=%async_computation.6 | async-start | bytes 2097152 | tf_op jit(solution)/shard_map/psum | solution.py:488
  291.0 67.8 %copy-start.2 = (bf16[1024,512]{1,0:T(8,128)(2,1)S(1)}, bf16[1024,512]{1,0:T(8,128)(2,1)}, u32[]{:S(2)}) copy-start(bf16[1024,512]{1,0:T(8,128)(2,1)} %get-tuple-element.34) | copy-start | bytes 3145732
  291.1 186.6 %reduce-scatter.5.cloned.1.call-start = ((), (), s32[]{:S(2)}) async-start(), calls=%async_computation.7 | async-start | bytes 4718592 | tf_op jit(solution)/shard_map/reduce_scatter | solution.py:503
  360.2 4.1 collective-permute-start.2
  360.9 25.6 %collective-permute-start.3 = (bf16[1024,512]{1,0:T(8,128)(2,1)S(1)}, bf16[1024,512]{1,0:T(8,128)(2,1)S(1)}, u32[]{:S(2)}, u32[]{:S(2)}) collective-permute-start(bf16[1024,512]{1,0:T(8,128)(2,1)S(1)} %get-tuple-element.54), channel_id=1, source_target_pairs={{1,0},{3,1},{5,2},{7,3},{0,4},{2,5},{4,6},{6,7},{9,8},{11,9},{13,1... | collective-permute-start | bytes 3145736 | tf_op jit(solution)/shard_map/ppermute | solution.py:424
  406.5 123.2 %reduce-scatter.3.cloned.1.call-start = ((), (), s32[]{:S(2)}) async-start(), calls=%async_computation.5 | async-start | bytes 4718592 | tf_op jit(solution)/shard_map/reduce_scatter | solution.py:499
  416.9 3.6 copy-start.3
  416.9 3.7 copy-start.4
  416.9 3.7 copy-start.5
  416.9 3.7 copy-start.6
  416.9 3.7 copy-start.7
  416.9 60.8 %copy-start = (bf16[128,2048]{1,0:T(8,128)(2,1)S(1)}, bf16[128,2048]{1,0:T(8,128)(2,1)}, u32[]{:S(2)}) copy-start(bf16[128,2048]{1,0:T(8,128)(2,1)} %param.13) | copy-start | bytes 1572868
  416.9 112.7 %copy-start.1 = (bf16[128,2048]{1,0:T(8,128)(2,1)S(1)}, bf16[128,2048]{1,0:T(8,128)(2,1)}, u32[]{:S(2)}) copy-start(bf16[128,2048]{1,0:T(8,128)(2,1)} %param.25) | copy-start | bytes 1572868
  416.9 200.3 %all-gather.14.cloned.1.call-start = ((), (), s32[]{:S(2)}) async-start(), calls=%async_computation.9 | async-start | bytes 10485760 | tf_op jit(solution)/shard_map/all_gather | solution.py:511
  417.7 317.5 %all-gather.12.cloned.1.call-start = ((), (), s32[]{:S(2)}) async-start(), calls=%async_computation.8 | async-start | bytes 17301504 | tf_op jit(solution)/shard_map/all_gather | solution.py:508
  418.4 369.5 %all-gather.16.cloned.1.call-start = ((), (), s32[]{:S(2)}) async-start(), calls=%async_computation.10 | async-start | bytes 5242880 | tf_op jit(solution)/shard_map/all_gather | solution.py:510
  419.2 486.6 %all-gather.18.cloned.1.call-start = ((), (), s32[]{:S(2)}) async-start(), calls=%async_computation.11 | async-start | bytes 17301504 | tf_op jit(solution)/shard_map/all_gather | solution.py:509
  419.8 585.9 %all-reduce.10.cloned.1.call-start = ((), (), s32[]{:S(2)}) async-start(), calls=%async_computation.12 | async-start | bytes 3538944 | tf_op jit(solution)/shard_map/psum | solution.py:515
  905.8 16.0 %copy-start.10 = (bf16[4096,512]{1,0:T(8,128)(2,1)S(1)}, bf16[4096,512]{1,0:T(8,128)(2,1)}, u32[]{:S(2)}) copy-start(bf16[4096,512]{1,0:T(8,128)(2,1)} %all-gather.16.cloned.1.call-done) | copy-start | bytes 12582916
Sparse Core Ops, SparseCore 0:
  11.3 49.8 all-gather.7
  62.9 57.0 all-gather.9
  137.0 79.5 all-reduce.5
  291.2 57.8 all-reduce.7
  406.6 71.0 reduce-scatter.4
  480.4 49.1 reduce-scatter.2
  531.5 85.7 all-gather.13
  620.3 114.8 all-gather.11
  737.1 50.8 all-gather.15
  790.8 114.8 all-gather.17
  909.6 62.5 all-reduce.9

commit v2 on v1

--- a/solution.py
+++ b/solution.py
@@ -147,7 +147,7 @@
     conv_ref[...] = conv
     high, low = halves(conv * sigmoid(conv))
     label = label_ref[...]
-    parts = [dot_bt(high, xw_ref[m]) + dot_bt(low, xw_ref[m]) for m in range(xw_ref.shape[0])]
+    parts = [dot_bt(xw_ref[m], high) + dot_bt(xw_ref[m], low) for m in range(xw_ref.shape[0])]
     proj_ref[...] = pick(parts, label)
 
 
@@ -160,7 +160,7 @@
         out_shape=(
             jax.ShapeDtypeStruct((rows, channels), F32),
             jax.ShapeDtypeStruct((rows, channels), BF16),
-            jax.ShapeDtypeStruct((rows, wide), F32),
+            jax.ShapeDtypeStruct((wide, rows), F32),
         ),
         scratch_shapes=[pltpu.VMEM((rows + lead, channels), F32)],
         compiler_params=params(),
@@ -169,7 +169,7 @@
 
 
 def scan_kernel(
-    conv_ref, proj_ref, gate_ref, grad_ref, label_ref, dtw_ref, dtb_ref, alog_ref, skip_ref,
+    conv_ref, proj_ref, gate_ref, grad_ref, label_ref, label_row_ref, dtw_ref, dtb_ref, alog_ref, skip_ref,
     gated_ref, dgate_ref, dact_ref, dproj_ref, ddtw_ref, ddtb_ref, dalog_ref, dskip_ref,
     hist, mix, prod, rate, drate, act, step, slope, dout, scanned, ddrive, dstep, dlow,
 ):
@@ -184,13 +184,15 @@
     def _():
         prod[...] = jnp.zeros_like(prod)
         dlow[...] = jnp.zeros_like(dlow)
+        high, low = halves(proj_ref[pl.ds(low_width, 2 * states), :])
+        row = lax.broadcasted_iota(jnp.int32, (2 * states, width), 0)
         for s in range(2 * states):
-            mix[s] = jnp.broadcast_to(proj_ref[:, pl.ds(low_width + s, 1)], (rows, width))
-
-    low_rank = proj_ref[:, pl.ds(0, low_width)]
-    low_high, low_low = halves(low_rank)
+            spread = (row == s).astype(BF16)
+            mix[s] = dot_at(high, spread) + dot_at(low, spread)
+
+    low_high, low_low = halves(proj_ref[pl.ds(0, low_width), :])
     parts = [
-        dot(low_high, dtw_ref[m]) + dot(low_low, dtw_ref[m]) + dtb_ref[pl.ds(m, 1), :].astype(F32) for m in range(mods)
+        dot_at(low_high, dtw_ref[m]) + dot_at(low_low, dtw_ref[m]) + dtb_ref[pl.ds(m, 1), :].astype(F32) for m in range(mods)
     ]
     speed = pick(parts, label)
     step[...] = jnp.maximum(speed, 0.0) + jnp.log1p(jnp.exp(-jnp.abs(speed)))
@@ -265,32 +267,34 @@
     dact_ref[...] = ddrive[...] * step[...] + skip * dout[...]
     dspeed = (dstep[...] * LN2 + ddrive[...] * act[...]) * slope[...]
     high, low = halves(dspeed)
-    parts = [dot_bt(high, dtw_ref[m]) + dot_bt(low, dtw_ref[m]) for m in range(mods)]
-    dlow[...] += pick(parts, label)
+    parts = [dot_bt(dtw_ref[m], high) + dot_bt(dtw_ref[m], low) for m in range(mods)]
+    dlow[...] += pick(parts, label_row_ref[...])
     for m in range(mods):
         own = label == m
         masked = jnp.where(own, dspeed, 0.0)
         high, low = halves(masked)
-        ddtw_ref[m] = dot_at(low_high, high) + dot_at(low_high, low) + dot_at(low_low, high)
+        ddtw_ref[m] = dot(low_high, high) + dot(low_high, low) + dot(low_low, high)
         ddtb_ref[pl.ds(m, 1), :] = jnp.sum(masked, axis=0, keepdims=True)
 
     @pl.when(tile == pl.num_programs(0) - 1)
     def _():
-        column = lax.broadcasted_iota(jnp.int32, (rows, 2 * states), 1)
+        column = lax.broadcasted_iota(jnp.int32, (width, 2 * states), 1)
         sums = jnp.zeros((rows, 2 * states), F32)
         for s in range(2 * states):
-            sums = jnp.where(column == s, jnp.sum(prod[s], axis=1, keepdims=True), sums)
-        dproj_ref[:, pl.ds(0, low_width)] = dlow[...]
-        dproj_ref[:, pl.ds(low_width, 2 * states)] = sums
-
-
-def scan_both(conv, proj, gate, grad, label, dtw, dtb, alog, skip):
+            gather = (column == s).astype(BF16)
+            high, low = halves(prod[s])
+            sums = sums + (dot(high, gather) + dot(low, gather))
+        dproj_ref[pl.ds(0, low_width), :] = dlow[...]
+        dproj_ref[pl.ds(low_width, 2 * states), :] = sums.T
+
+
+def scan_both(conv, proj, gate, grad, label, label_row, dtw, dtb, alog, skip):
     rows, channels = conv.shape
     width = min(128, channels)
     length = rows // GROUP
     states = alog.shape[0]
     mods, low_width = dtw.shape[0], dtw.shape[1]
-    wide = proj.shape[1]
+    wide = proj.shape[0]
 
     def whole(shape):
         return pl.BlockSpec(shape, lambda j: (0,) * len(shape), pipeline_mode=pl.Buffered(1))
@@ -306,7 +310,7 @@
             jax.ShapeDtypeStruct((rows, channels), BF16),
             jax.ShapeDtypeStruct((rows, channels), BF16),
             jax.ShapeDtypeStruct((rows, channels), F32),
-            jax.ShapeDtypeStruct((rows, wide), F32),
+            jax.ShapeDtypeStruct((wide, rows), F32),
             jax.ShapeDtypeStruct((mods, low_width, channels), F32),
             jax.ShapeDtypeStruct((mods, channels), F32),
             jax.ShapeDtypeStruct((states, channels), F32),
@@ -314,11 +318,11 @@
         ),
         grid=(channels // width,),
         in_specs=[
-            cut(rows), whole((rows, wide)), cut(rows), cut(rows), whole((rows, 1)),
+            cut(rows), whole((wide, rows)), cut(rows), cut(rows), whole((rows, 1)), whole((1, rows)),
             cut(mods, low_width), cut(mods), cut(states), cut(1),
         ],
         out_specs=(
-            cut(rows), cut(rows), cut(rows), whole((rows, wide)), cut(mods, low_width), cut(mods), cut(states), cut(1),
+            cut(rows), cut(rows), cut(rows), whole((wide, rows)), cut(mods, low_width), cut(mods), cut(states), cut(1),
         ),
         scratch_shapes=[
             pltpu.VMEM((length + 1, states) + plane, F32),
@@ -327,32 +331,33 @@
             pltpu.VMEM((states,) + plane, F32),
             pltpu.VMEM((states,) + plane, F32),
             flat, flat, flat, flat, flat, flat, flat,
-            pltpu.VMEM((rows, low_width), F32),
+            pltpu.VMEM((low_width, rows), F32),
         ],
         compiler_params=params(),
+        cost_estimate=pl.CostEstimate(flops=5000 * rows * channels * states, bytes_accessed=20 * rows * channels, transcendentals=0),
         name="scan_both",
-    )(conv, proj, gate, grad, label, dtw, dtb, alog, skip[None, :])
+    )(conv, proj, gate, grad, label, label_row, dtw, dtb, alog, skip[None, :])
 
 
 def conv_back_kernel(
-    conv_ref, inner_ref, dact_ref, dproj_ref, label_ref, cw_ref, xw_ref,
+    conv_ref, inner_ref, dact_ref, dproj_ref, label_ref, label_row_ref, cw_ref, xw_ref,
     dinner_ref, dxw_ref, dcw_ref, dcb_ref, pad_ref,
 ):
     rows, channels = conv_ref.shape
     taps = cw_ref.shape[0]
     tail = (taps - 1) * GROUP
-    label = label_ref[...]
+    label, label_row = label_ref[...], label_row_ref[...]
     conv = conv_ref[...]
     soft = sigmoid(conv)
     act = conv * soft
     dproj = dproj_ref[...]
     high, low = halves(dproj)
-    parts = [dot(high, xw_ref[m]) + dot(low, xw_ref[m]) for m in range(xw_ref.shape[0])]
+    parts = [dot_at(high, xw_ref[m]) + dot_at(low, xw_ref[m]) for m in range(xw_ref.shape[0])]
     dact = dact_ref[...] + pick(parts, label)
     act_high, act_low = halves(act)
     for m in range(xw_ref.shape[0]):
-        high, low = halves(jnp.where(label == m, dproj, 0.0))
-        dxw_ref[m] = dot_at(high, act_high) + dot_at(low, act_high) + dot_at(high, act_low)
+        high, low = halves(jnp.where(label_row == m, dproj, 0.0))
+        dxw_ref[m] = dot(high, act_high) + dot(low, act_high) + dot(high, act_low)
     dconv = dact * (soft + act * (1.0 - soft))
     dcb_ref[...] = jnp.sum(dconv, axis=0, keepdims=True)
     pad_ref[pl.ds(0, rows), :] = dconv
@@ -368,7 +373,7 @@
     dinner_ref[...] = by_sequence(total).astype(BF16)
 
 
-def conv_backward(conv, inner, dact, dproj, label, cw, xw):
+def conv_backward(conv, inner, dact, dproj, label, label_row, cw, xw):
     rows, channels = conv.shape
     mods, wide = xw.shape[0], xw.shape[1]
     taps = cw.shape[0]
@@ -383,16 +388,141 @@
         scratch_shapes=[pltpu.VMEM((rows + (taps - 1) * GROUP, channels), F32)],
         compiler_params=params(),
         name="conv_backward",
-    )(conv, inner, dact, dproj, label, cw, xw)
-
-
-def by_groups(fn, count, arrays, joined):
+    )(conv, inner, dact, dproj, label, label_row, cw, xw)
+
+
+MESH = pl.DeviceIdType.MESH
+
+
+def sum_kernel(chips, x_ref, out_ref, near, mine, far, total, every, other, near_sems, far_sems, back_sems, other_sems):
+    wide, rows = x_ref.shape
+    half, part = rows // 2, rows // 2 // chips
+    tok, ch = lax.axis_index("tok"), lax.axis_index("ch")
+    chip, core = ch // 2, ch % 2
+    partner = (tok, 2 * chip + 1 - core)
+    chips_away = [(tok, 2 * (chip ^ d) + core) for d in range(1, chips)]
+
+    barrier = pltpu.get_barrier_semaphore()
+    for device in [partner] + chips_away:
+        pl.semaphore_signal(barrier, inc=1, device_id=device, device_id_type=MESH)
+    pl.semaphore_wait(barrier, chips)
+
+    def send(src, dst, sems, device):
+        copy = pltpu.make_async_remote_copy(
+            src_ref=src, dst_ref=dst, send_sem=sems.at[0], recv_sem=sems.at[1], device_id=device, device_id_type=MESH
+        )
+        copy.start()
+        return copy
+
+    def columns(index, size):
+        return pl.ds(pl.multiple_of(index * size, size), size)
+
+    copy = send(x_ref.at[:, columns(1 - core, half)], near, near_sems, partner)
+    copy.wait()
+    mine[...] = (x_ref[:, columns(core, half)] + near[...]).astype(BF16)
+    copies = [
+        send(mine.at[:, columns(chip ^ d, part)], far.at[d - 1], far_sems.at[d - 1], chips_away[d - 1])
+        for d in range(1, chips)
+    ]
+    value = mine[:, columns(chip, part)].astype(F32)
+    for d, copy in enumerate(copies):
+        copy.wait()
+        value = value + far[d].astype(F32)
+    total[...] = value.astype(BF16)
+    copies = [send(total, every.at[d - 1], back_sems.at[d - 1], chips_away[d - 1]) for d in range(1, chips)]
+    copies += [send(total, other.at[0], other_sems.at[0], partner)]
+    out_ref[:, columns(core * chips + chip, part)] = total[...].astype(F32)
+    for d in range(1, chips):
+        copies[d - 1].wait()
+        copies += [send(every.at[d - 1], other.at[d], other_sems.at[d], partner)]
+        out_ref[:, columns(core * chips + (chip ^ d), part)] = every[d - 1].astype(F32)
+    for d in range(chips):
+        copies[chips - 1 + d].wait()
+        out_ref[:, columns((1 - core) * chips + (chip ^ d), part)] = other[d].astype(F32)
+
+
+def sum_over_ch(x, n, collective_id):
+    wide, rows = x.shape
+    chips = n // 2
+    half, part = rows // 2, rows // 2 // chips
+    dma = pltpu.SemaphoreType.DMA
+    return pl.pallas_call(
+        functools.partial(sum_kernel, chips),
+        out_shape=jax.ShapeDtypeStruct((wide, rows), F32),
+        in_specs=[pl.BlockSpec(memory_space=pltpu.VMEM)],
+        out_specs=pl.BlockSpec(memory_space=pltpu.VMEM),
+        scratch_shapes=[
+            pltpu.VMEM((wide, half), F32),
+            pltpu.VMEM((wide, half), BF16),
+            pltpu.VMEM((chips - 1, wide, part), BF16),
+            pltpu.VMEM((wide, part), BF16),
+            pltpu.VMEM((chips - 1, wide, part), BF16),
+            pltpu.VMEM((chips, wide, part), BF16),
+            dma((2,)), dma((chips - 1, 2)), dma((chips - 1, 2)), dma((chips, 2)),
+        ],
+        compiler_params=pltpu.CompilerParams(collective_id=collective_id, has_side_effects=True, vmem_limit_bytes=16 << 20),
+        name="sum_over_ch",
+    )(x)
+
+
+def total_over_ch(x, n, collective_id):
+    if x.shape[1] // n % 128 == 0 and n // 2 & (n // 2 - 1) == 0 and n <= 8:
+        return sum_over_ch(x, n, collective_id)
+    return lax.psum(x, "ch")
+
+
+def grad_kernel(left_ref, right_ref, label_ref, out_ref):
+    left, right, label = left_ref[...], right_ref[...], label_ref[...]
+    turned = left.T
+    for m in range(out_ref.shape[0]):
+        out_ref[m] = dot(jnp.where(label == m, turned, jnp.zeros_like(turned)), right)
+
+
+def grad_part_kernel(left_ref, right_ref, label_ref, out_ref):
+    left, right, label = left_ref[...], right_ref[...], label_ref[...]
+    turned = left.T
+    first = pl.program_id(1) == 0
+    for m in range(out_ref.shape[0]):
+        part = dot(jnp.where(label == m, turned, jnp.zeros_like(turned)), right)
+        out_ref[m] = jnp.where(first, part, out_ref[m] + part)
+
+
+def weight_grad(left, right, label, mods, tile):
+    rows, deep = left.shape
+    wide = right.shape[1]
+    block = min(rows, 4096)
+    tile = min(tile, deep)
+    return pl.pallas_call(
+        grad_kernel if block == rows else grad_part_kernel,
+        out_shape=jax.ShapeDtypeStruct((mods, deep, wide), F32),
+        grid=(deep // tile, rows // block),
+        in_specs=[
+            pl.BlockSpec((block, tile), lambda i, j: (j, i)),
+            pl.BlockSpec((block, wide), lambda i, j: (j, 0)),
+            pl.BlockSpec((1, block), lambda i, j: (0, j)),
+        ],
+        out_specs=pl.BlockSpec((mods, tile, wide), lambda i, j: (0, i, 0)),
+        compiler_params=params(),
+        cost_estimate=pl.CostEstimate(
+            flops=2 * mods * rows * deep * wide,
+            bytes_accessed=2 * rows * (deep + wide) + 4 * mods * deep * wide,
+            transcendentals=0,
+        ),
+        name="weight_grad",
+    )(left, right, label)
+
+
+def by_groups(fn, count, arrays, axes, joined):
     if count == 1:
         return fn(*arrays)
-    size = arrays[0].shape[0] // count
-    outs = [fn(*(a[i * size : (i + 1) * size] for a in arrays)) for i in range(count)]
+
+    def cut(a, axis, i):
+        size = a.shape[axis] // count
+        return lax.slice_in_dim(a, i * size, (i + 1) * size, axis=axis)
+
+    outs = [fn(*(cut(a, axis, i) for a, axis in zip(arrays, axes, strict=True))) for i in range(count)]
     return tuple(
-        jnp.concatenate(values, axis=0) if at < joined else functools.reduce(jnp.add, values)
+        jnp.concatenate(values, axis=joined[at]) if at < len(joined) else functools.reduce(jnp.add, values)
         for at, values in enumerate(zip(*outs, strict=True))
     )
 
@@ -424,17 +554,6 @@
     two = lax.ppermute(jnp.where(even, dgate, dinner), "ch", [(b, a) for a, b in second])
     lower = c < n // 2
     return jnp.concatenate([jnp.where(lower, one, two), jnp.where(lower, two, one)], axis=1)
-
-
-def weight_grad(left, right, label, mods, spread_left):
-    parts = []
-    for m in range(mods):
-        own = (label == m)[:, None]
-        if spread_left:
-            parts.append(dot_at(jnp.where(own, left, jnp.zeros_like(left)), right))
-        else:
-            parts.append(dot_at(left, jnp.where(own, right, jnp.zeros_like(right))))
-    return jnp.stack(parts)
 
 
 def on_device(
@@ -468,33 +587,42 @@
     group_label = lax.dynamic_slice_in_dim(every_label, lax.axis_index("tok") * token_group, token_group, 0)
     label = group_label[:, None]
     label_by_time = group_label.reshape(count, GROUP, length).transpose(0, 2, 1).reshape(token_group, 1)
-
+    label_row = label_by_time.reshape(1, token_group)
+
+    every_scaled = lax.all_gather(scaled, ("tok", "ch"), axis=0, tiled=True)
+    every_cot = lax.all_gather(cotangent, ("tok", "ch"), axis=0, tiled=True)
     xz = routed_select(group_rows, label, in_weight, 256, False)
     inner, gate = to_owners(xz, n)
     group_cot = lax.all_gather(cotangent, "ch", axis=0, tiled=True)
     gated_grad = routed_select(group_cot, label, out_weight, 128, True)
 
     conv, inner_by_time, proj_part = by_groups(
-        lambda a, b: conv_forward(a, b, conv_weight, conv_bias, x_weight), count, (inner, label_by_time), 3
+        lambda a, b: conv_forward(a, b, conv_weight, conv_bias, x_weight), count, (inner, label_row), (0, 1), (0, 0, 1)
     )
-    proj = lax.psum(proj_part, "ch")
+    proj = total_over_ch(proj_part, n, 0)
 
     gated, dgate, dact, dproj_part, ddtw, ddtb, dalog, dskip = by_groups(
-        lambda a, b, c, d, e: scan_both(a, b, c, d, e, dt_weight, dt_bias, a_log, skip_gain),
+        lambda a, b, c, d, e, f: scan_both(a, b, c, d, e, f, dt_weight, dt_bias, a_log, skip_gain),
         count,
-        (conv, proj, gate, gated_grad, label_by_time),
-        4,
+        (conv, proj, gate, gated_grad, label_by_time, label_row),
+        (0, 1, 0, 0, 0, 1),
+        (0, 0, 0, 1),
     )
-    dproj = lax.psum(dproj_part, "ch")
+    if count == 1:
+        dproj_part, every_scaled = lax.optimization_barrier((dproj_part, every_scaled))
+    dproj = total_over_ch(dproj_part, n, 1)
 
     dinner, dxw, dcw, dcb = by_groups(
-        lambda a, b, c, d, e: conv_backward(a, b, c, d, e, conv_weight, x_weight),
+        lambda a, b, c, d, e, f: conv_backward(a, b, c, d, e, f, conv_weight, x_weight),
         count,
-        (conv, inner_by_time, dact, dproj, label_by_time),
-        1,
+        (conv, inner_by_time, dact, dproj, label_by_time, label_row),
+        (0, 0, 0, 1, 0, 1),
+        (0,),
     )
     xz_grad = to_columns(dinner, dgate, n)
 
+    if count == 1:
+        xz_grad, every_cot = lax.optimization_barrier((xz_grad, every_cot))
     branch_part = routed_spread(gated, label, out_weight, 512, False, BF16)
     branch = lax.psum_scatter(branch_part, "ch", scatter_dimension=0, tiled=True).astype(F32)
     block_out = (rows_float + branch).astype(BF16)
@@ -505,12 +633,11 @@
     ng = scaled_grad * gain[None, :]
     row_grad = cotangent.astype(F32) + inverse * (ng - normed * jnp.mean(ng * normed, axis=-1, keepdims=True))
 
-    every_scaled = lax.all_gather(scaled, ("tok", "ch"), axis=0, tiled=True)
-    every_cot = lax.all_gather(cotangent, ("tok", "ch"), axis=0, tiled=True)
     every_gated = lax.all_gather(gated, "tok", axis=0, tiled=True)
     every_grad = lax.all_gather(xz_grad, "tok", axis=0, tiled=True)
-    out_weight_grad = weight_grad(every_gated, every_cot, every_label, mods, True)
-    in_weight_grad = weight_grad(every_scaled, every_grad, every_label, mods, False)
+    every_label = every_label[None, :]
+    out_weight_grad = weight_grad(every_gated, every_cot, every_label, mods, 128)
+    in_weight_grad = weight_grad(every_scaled, every_grad, every_label, mods, 256)
 
     small = lax.psum((dxw, ddtw, ddtb, dcw, dcb, dalog, dskip), "tok")
     gain_grad = lax.psum(gain_grad, ("tok", "ch"))

time: 1020 us -> 742 us (0.73)
  waiting for transfers between devices: 566 us -> 257 us
  Pallas kernels: 153 us -> 323 us
  matrix products: 124 us -> 0 us
  other arithmetic: 43.7 us -> 15.4 us
    pallas_call x0 -> x4, Pallas kernels: none -> 169 us  [the longest x2 94 us: weight_grad(): pl.pallas_call(grad_kernel if block == rows else grad_part_kernel, out_sh...]
    dot_general x6 -> x0, matrix products: 124 us -> none  [dot_at(): lax.dot_general(a, b, (((0,), (0,)), ((), ())), preferred_element_type=F32)]
    psum x2 -> x0, waiting for transfers between devices: 120 us -> none  [the longest x1 62.3 us: on_device(): proj = lax.psum(proj_part, 'ch')]
    all_gather x1, waiting for transfers between devices: 118 us -> 0.02 us  [on_device(): every_scaled = lax.all_gather(scaled, ('tok', 'ch'), axis=0, tiled=True)]
    all_gather x1, waiting for transfers between devices: 118 us -> 43.8 us  [on_device(): every_cot = lax.all_gather(cotangent, ('tok', 'ch'), axis=0, tiled=True)]
    ppermute x1, waiting for transfers between devices: 44.8 us -> 0.01 us  [to_owners(): two = lax.ppermute(jnp.where(lower, right, left), 'ch', second)]
    all_gather x1, waiting for transfers between devices: 0.02 us -> 34.3 us  [on_device(): group_cot = lax.all_gather(cotangent, 'ch', axis=0, tiled=True)]
    another operation x2 -> x0, other arithmetic: 28.1 us -> none  [weight_grad(): return jnp.stack(parts)]
  transfers between devices with their start and end apart: 15 -> 13, of which waited for: 11 -> 9; matrix products, arithmetic and copies ran while one was open for 16% -> 2% of each run, Pallas kernels for 5% -> 44%
where the time goes in v2:
time: 742 us; the launch traced here: 734 us
  Pallas kernels  323 us (44%)
  waiting for transfers between devices  257 us (35%)
  blocking collectives  103 us (14%)
  other arithmetic  15.4 us (2%)
  between operations  14.6 us (2%)
  local copies, waits for them, and re-layouts  12.8 us (2%)
  starting transfers between devices  8.35 us (1%)
    pallas_call x2, Pallas kernels, weight_grad(): pl.pallas_call(grad_kernel if block == rows else grad_part_kernel, out_sh...  94 us
    all_gather x1, waiting for transfers between devices, on_device(): every_grad = lax.all_gather(xz_grad, 'tok', axis=0, tiled=True)  84.8 us
    pallas_call x2, Pallas kernels, sum_over_ch(): pl.pallas_call(functools.partial(sum_kernel, chips), out_shape=jax.ShapeD...  75 us
    pallas_call x1, Pallas kernels, scan_both(): pl.pallas_call(scan_kernel, out_shape=(jax.ShapeDtypeStruct((rows, channe...  74.7 us
    ppermute x1, waiting for transfers between devices, to_columns(): lax.ppermute(jnp.where(even, dgate, dinner), 'ch', [(b, a) for a, b in se...  45.3 us
    all_gather x1, waiting for transfers between devices, on_device(): every_cot = lax.all_gather(cotangent, ('tok', 'ch'), axis=0, tiled=True)  43.8 us
    all_gather x1, blocking collectives, on_device(): every_label = lax.all_gather(modality, ('tok', 'ch'), axis=0, tiled=True)  43.8 us
    psum x1, blocking collectives, on_device(): gain_grad = lax.psum(gain_grad, ('tok', 'ch'))  39.9 us
  transfers between devices with their start and end apart: 13, of which 9 were waited for; matrix products, arithmetic and copies ran while one was open for 2% of the time, Pallas kernels for 44%

profile of v2, /device:TPU:0, one launch (start us, length us, event | category | flops | bytes accessed | tf_op | source)
XLA Modules:
  0.0 734.1 jit_solution(13423028380157709701)
XLA Ops:
  7.2 1.2 fusion.10
  8.5 0.7 convert_element_type.22
  9.2 2.0 fusion.7
  11.3 0.7 all-gather.10.cloned.1.call-update
  12.0 0.7 all-gather.12.cloned.1.call-update
  13.3 43.8 %all-gather = s32[32,1,128]{2,1,0:T(1,128)S(1)} all-gather(s32[1,1,128]{2,1,0:T(1,128)} %bitcast.17), channel_id=1, replica_groups=mesh['tok'=4,'ch'=8] {'tok','ch'}, dimensions={0}, use_global_device_ids=true | all-gather | bytes 16896 | tf_op jit(solution)/shard_map/all_gather | solution.py:585
  57.1 1.0 copy.33.label_ref
  58.1 3.2 all-gather.8.cloned.1.call-done.x_ref
  61.3 17.7 %routed_select.2 = bf16[1024,1024]{1,0:T(8,128)(2,1)} custom-call(bf16[1024,2048]{1,0:T(8,128)(2,1)} %all-gather.8.cloned.1.call-done.x_ref, s32[1024,1]{1,0:T(8,128)} %copy.33.label_ref, bf16[3,2048,1024]{2,1,0:T(8,128)(2,1)} %w_ref.7), custom_call_target="tpu_custom_call" | custom-call | flops 12884901888 | bytes 18874368 | tf_op jit(solution)/shard_map/routed_select/pallas_call | solution.py:69
  79.0 2.7 broadcast_select_fusion.2
  82.0 0.7 collective-permute-start
  82.9 0.7 reshape_reshape.3.label_ref.label_row_ref
  83.6 1.0 reshape.48.label_ref
  85.8 34.3 %all-gather.10.cloned.1.call-done.x_ref = bf16[1024,2048]{1,0:T(8,128)(2,1)} async-done(((bf16[128,2048]{1,0:T(8,128)(2,1)}), bf16[1024,2048]{1,0:T(8,128)(2,1)}) %all-gather.10.cloned.1.call-update) | async-done | bytes 4194320 | tf_op jit(solution)/shard_map/all_gather | solution.py:596
  120.1 17.3 %routed_select.3.grad_ref = bf16[1024,512]{1,0:T(8,128)(2,1)} custom-call(bf16[1024,2048]{1,0:T(8,128)(2,1)} %all-gather.10.cloned.1.call-done.x_ref, s32[1024,1]{1,0:T(8,128)} %copy.33.label_ref, bf16[3,512,2048]{2,1,0:T(8,128)(2,1)} %w_ref.6), custom_call_target="tpu_custom_call" | custom-call | flops 6442450944 | bytes 11534336 | tf_op jit(solution)/shard_map/routed_select/pallas_call | solution.py:69
  137.4 1.5 broadcast_select_fusion.6
  138.9 5.8 conv_forward.1
  144.6 1.1 copy-done.3
  145.7 51.7 %sum_over_ch.2.proj_ref = f32[160,1024]{1,0:T(8,128)S(1)} custom-call(f32[160,1024]{1,0:T(8,128)S(1)} %copy-done.3), custom_call_target="tpu_custom_call" | custom-call | tf_op jit(solution)/shard_map/sum_over_ch/pallas_call | solution.py:449
  197.4 0.8 copy-done.2
  198.2 74.7 %scan_both.1 = (bf16[1024,512]{1,0:T(8,128)(2,1)}, bf16[1024,512]{1,0:T(8,128)(2,1)}, f32[1024,512]{1,0:T(8,128)}, f32[160,1024]{1,0:T(8,128)}, f32[3,128,512]{2...) custom-call(f32[1024,512]{1,0:T(8,128)} %get-tuple-element.31.conv_ref, ...), custom_call_target="tpu_custom_call" | custom-call | flops 41943040000 | bytes 10485760 | tf_op jit(solution)/shard_map/scan_both/pallas_call | solution.py:307
  273.3 1.1 copy-done.1
  274.4 23.3 %sum_over_ch.3.dproj_ref = f32[160,1024]{1,0:T(8,128)S(1)} custom-call(f32[160,1024]{1,0:T(8,128)S(1)} %copy-done.1), custom_call_target="tpu_custom_call" | custom-call | tf_op jit(solution)/shard_map/sum_over_ch/pallas_call | solution.py:449
  297.7 0.8 copy-done
  298.6 9.7 %conv_backward.1 = (bf16[1024,512]{1,0:T(8,128)(2,1)}, f32[3,160,512]{2,1,0:T(8,128)}, f32[4,512]{1,0:T(4,128)}, f32[1,512]{1,0:T(1,128)}) custom-call(f32[1024,512]{1,0:T(8,128)} %get-tuple-element.31.conv_ref, bf16[1024,512]{1,0:T(8,128)(2,1)} %get-tuple-element.34.inner_ref, f32[1024,512]{1,0:T(8,128)} %get-tuple-element.35.dact_ref, ...), custom_call_target="tpu_custom_call" | custom-call | tf_op jit(solution)/shard_map/conv_backward/pallas_call | solution.py:380
  308.2 1.4 broadcast_select_fusion.5
  309.6 0.7 collective-permute-start.2
  310.3 6.0 collective-permute-start.3
  316.3 45.3 %collective-permute-done.3 = bf16[1024,512]{1,0:T(8,128)(2,1)S(1)} collective-permute-done((bf16[1024,512]{1,0:T(8,128)(2,1)S(1)}, bf16[1024,512]{1,0:T(8,128)(2,1)S(1)}, u32[]{:S(2)}, u32[]{:S(2)}) %collective-permute-start.3) | collective-permute-done | bytes 1048608 | tf_op jit(solution)/shard_map/ppermute | solution.py:554
  361.8 1.6 pad_maximum_fusion.x_ref
  363.3 43.8 %all-gather.14.cloned.1.call-done.right_ref = bf16[4096,2048]{1,0:T(8,128)(2,1)} async-done(((bf16[128,2048]{1,0:T(8,128)(2,1)}), bf16[4096,2048]{1,0:T(8,128)(2,1)}) %all-gather.14.cloned.1.call-update) | async-done | bytes 16777232 | tf_op jit(solution)/shard_map/all_gather | solution.py:593
  407.2 18.2 %routed_spread.3 = bf16[1024,2048]{1,0:T(8,128)(2,1)} custom-call(bf16[1024,1024]{1,0:T(8,128)(2,1)} %pad_maximum_fusion.x_ref, s32[1024,1]{1,0:T(8,128)} %copy.33.label_ref, bf16[3,2048,1024]{2,1,0:T(8,128)(2,1)} %w_ref.7), custom_call_target="tpu_custom_call" | custom-call | flops 12884901888 | bytes 18874368 | tf_op jit(solution)/shard_map/routed_spread/pallas_call | solution.py:108
  425.4 10.4 %routed_spread.2 = bf16[1024,2048]{1,0:T(8,128)(2,1)} custom-call(bf16[1024,512]{1,0:T(8,128)(2,1)} %get-tuple-element.33.x_ref, s32[1024,1]{1,0:T(8,128)} %copy.33.label_ref, bf16[3,512,2048]{2,1,0:T(8,128)(2,1)} %w_ref.6), custom_call_target="tpu_custom_call" | custom-call | flops 6442450944 | bytes 11534336 | tf_op jit(solution)/shard_map/routed_spread/pallas_call | solution.py:108
  435.9 0.7 all-gather.16.cloned.1.call-update
  436.7 0.7 all-reduce.4.cloned.1.call-update
  437.4 19.6 %all-reduce = (f32[3,512]{1,0:T(4,128)}, f32[4,512]{1,0:T(4,128)}, f32[512]{0:T(512)}, f32[16,512]{1,0:T(8,128)}, f32[512]{0:T(512)}) all-reduce(f32[3,512]{1,0:T(4,128)S(1)} %copy-done.9, f32[4,512]{1,0:T(4,128)S(1)} %copy-done.10, f32[512]{0:T(512)S(1)} %bitcast.16, ...), channel_id=1, replica_groups=mesh['tok'=4,'ch'=8] {'tok'}, use_global_device_ids=true, to_apply=%region_8.9 | all-reduce | flops 12800 | bytes 102400 | tf_op jit(solution)/shard_map/psum | solution.py:642
  457.1 5.6 all-gather.18.cloned.1.call-done.left_ref
  462.6 34.7 %weight_grad.3 = f32[3,512,2048]{2,1,0:T(8,128)} custom-call(bf16[4096,512]{1,0:T(8,128)(2,1)} %all-gather.18.cloned.1.call-done.left_ref, bf16[4096,2048]{1,0:T(8,128)(2,1)} %all-gather.14.cloned.1.call-done.right_ref, s32[1,4096]{1,0:T(1,128)} %bitcast.12), custom_call_target="tpu_custom_call" | custom-call | flops 25769803776 | bytes 33554432 | tf_op jit(solution)/shard_map/weight_grad/pallas_call | solution.py:495
  497.3 18.1 %reduce-scatter.5.cloned.1.call-done = bf16[128,2048]{1,0:T(8,128)(2,1)} async-done(((bf16[1024,2048]{1,0:T(8,128)(2,1)}), bf16[128,2048]{1,0:T(8,128)(2,1)}) %reduce-scatter.5.cloned.1.call-update) | async-done | bytes 524304 | tf_op jit(solution)/shard_map/reduce_scatter | solution.py:631
  515.4 1.5 fusion.9
  516.9 39.9 %psum.56 = f32[2048]{0:T(1024)S(1)} all-reduce(f32[2048]{0:T(1024)S(1)} %get-tuple-element.50), channel_id=1, replica_groups=mesh['tok'=4,'ch'=8] {'tok','ch'}, use_global_device_ids=true, to_apply=%region_5.6 | all-reduce | flops 2048 | bytes 16384 | tf_op jit(solution)/shard_map/psum | solution.py:643
  557.4 9.5 %reduce-scatter.3.cloned.1.call-done = bf16[128,2048]{1,0:T(8,128)(2,1)} async-done(((bf16[1024,2048]{1,0:T(8,128)(2,1)}), bf16[128,2048]{1,0:T(8,128)(2,1)}) %reduce-scatter.3.cloned.1.call-update) | async-done | bytes 524304 | tf_op jit(solution)/shard_map/reduce_scatter | solution.py:627
  567.0 2.8 fusion.6
  569.8 84.8 %all-gather.16.cloned.1.call-done.right_ref = bf16[4096,1024]{1,0:T(8,128)(2,1)} async-done(((bf16[1024,1024]{1,0:T(8,128)(2,1)}), bf16[4096,1024]{1,0:T(8,128)(2,1)}) %all-gather.16.cloned.1.call-update) | async-done | bytes 8388624 | tf_op jit(solution)/shard_map/all_gather | solution.py:637
  654.6 59.3 %weight_grad.2 = f32[3,2048,1024]{2,1,0:T(8,128)} custom-call(bf16[4096,2048]{1,0:T(8,128)(2,1)} %all-gather.12.cloned.1.call-done.left_ref, bf16[4096,1024]{1,0:T(8,128)(2,1)} %all-gather.16.cloned.1.call-done.right_ref, s32[1,4096]{1,0:T(1,128)} %bitcast.13), custom_call_target="tpu_custom_call" | custom-call | flops 51539607552 | bytes 50331648 | tf_op jit(solution)/shard_map/weight_grad/pallas_call | solution.py:495
  713.9 9.0 %all-reduce.4.cloned.1.call-done = (f32[3,160,512]{2,1,0:T(8,128)}, f32[3,128,512]{2,1,0:T(8,128)}) async-done(((f32[3,160,512]{2,1,0:T(8,128)}, f32[3,128,512]{2,1,0:T(8,128)}), (f32[3,160,512]{2,1,0:T(8,128)}, f32[3,128,512]{2,1,0:T(8,128)})) %all-reduce.4.cloned.1.call-update) | async-done | bytes 1769488 | tf_op jit(solution)/shard_map/psum | solution.py:642
  722.8 2.2 copy.43
  725.0 2.1 copy.44
  (54 shorter events, 3.6 us)
Async XLA Ops:
  7.2 54.2 %all-gather.8.cloned.1.call-start = ((), (), s32[]{:S(2)}) async-start(), calls=%async_computation.2 | async-start | bytes 4718592 | tf_op jit(solution)/shard_map/all_gather | solution.py:584
  11.2 108.9 %all-gather.10.cloned.1.call-start = ((), (), s32[]{:S(2)}) async-start(), calls=%async_computation.3 | async-start | bytes 4718592 | tf_op jit(solution)/shard_map/all_gather | solution.py:596
  12.0 261.3 %all-gather.12.cloned.1.call-start = ((), (), s32[]{:S(2)}) async-start(), calls=%async_computation.5 | async-start | bytes 17301504 | tf_op jit(solution)/shard_map/all_gather | solution.py:592
  12.7 394.5 %all-gather.14.cloned.1.call-start = ((), (), s32[]{:S(2)}) async-start(), calls=%async_computation.6 | async-start | bytes 17301504 | tf_op jit(solution)/shard_map/all_gather | solution.py:593
  13.3 449.4 %all-gather.18.cloned.1.call-start = ((), (), s32[]{:S(2)}) async-start(), calls=%async_computation.9 | async-start | bytes 5242880 | tf_op jit(solution)/shard_map/all_gather | solution.py:636
  57.1 25.7 %copy-start.7 = (s32[32,1,128]{2,1,0:T(1,128)}, s32[32,1,128]{2,1,0:T(1,128)S(1)}, u32[]{:S(2)}) copy-start(s32[32,1,128]{2,1,0:T(1,128)S(1)} %all-gather) | copy-start | bytes 49156
  79.0 5.6 copy-start.13
  79.0 6.1 copy-start.14
  81.7 55.7 %collective-permute-start.1 = (bf16[1024,512]{1,0:T(8,128)(2,1)}, bf16[1024,512]{1,0:T(8,128)(2,1)S(1)}, u32[]{:S(2)}, u32[]{:S(2)}) collective-permute-start(bf16[1024,512]{1,0:T(8,128)(2,1)} %get-tuple-element.65), channel_id=1, source_target_pairs={{0,1},{1,3},{2,5},{3,7},{4,0},{5,2},{6,4},{7,6},{8,9},{9,11},{10,1... | collective-permute-start | bytes 3145736 | tf_op jit(solution)/shard_map/ppermute | solution.py:544
  82.0 55.4 %collective-permute-start = (bf16[1024,512]{1,0:T(8,128)(2,1)S(1)}, bf16[1024,512]{1,0:T(8,128)(2,1)S(1)}, u32[]{:S(2)}, u32[]{:S(2)}) collective-permute-start(bf16[1024,512]{1,0:T(8,128)(2,1)S(1)} %get-tuple-element.66), channel_id=1, source_target_pairs={{0,0},{1,2},{2,4},{3,6},{4,1},{5,3},{6,5},{7,7},{8,8},{9,10},{10,1... | collective-permute-start | bytes 3145736 | tf_op jit(solution)/shard_map/ppermute | solution.py:543
  144.6 1.1 copy-start.3
  197.4 0.8 copy-start.2
  272.9 35.3 %copy-start.6 = (bf16[1024,512]{1,0:T(8,128)(2,1)S(1)}, bf16[1024,512]{1,0:T(8,128)(2,1)}, u32[]{:S(2)}) copy-start(bf16[1024,512]{1,0:T(8,128)(2,1)} %get-tuple-element.39) | copy-start | bytes 3145732
  273.0 242.4 %reduce-scatter.5.cloned.1.call-start = ((), (), s32[]{:S(2)}) async-start(), calls=%async_computation.7 | async-start | bytes 4718592 | tf_op jit(solution)/shard_map/reduce_scatter | solution.py:631
  273.3 1.1 copy-start.1
  297.7 0.9 copy-start
  309.6 6.8 collective-permute-start.2
  310.3 51.3 %collective-permute-start.3 = (bf16[1024,512]{1,0:T(8,128)(2,1)S(1)}, bf16[1024,512]{1,0:T(8,128)(2,1)S(1)}, u32[]{:S(2)}, u32[]{:S(2)}) collective-permute-start(bf16[1024,512]{1,0:T(8,128)(2,1)S(1)} %get-tuple-element.62), channel_id=1, source_target_pairs={{1,0},{3,1},{5,2},{7,3},{0,4},{2,5},{4,6},{6,7},{9,8},{11,9},{13,1... | collective-permute-start | bytes 3145736 | tf_op jit(solution)/shard_map/ppermute | solution.py:554
  425.4 141.6 %reduce-scatter.3.cloned.1.call-start = ((), (), s32[]{:S(2)}) async-start(), calls=%async_computation.4 | async-start | bytes 4718592 | tf_op jit(solution)/shard_map/reduce_scatter | solution.py:627
  435.8 1.5 copy-start.8
  435.8 1.6 copy-start.9
  435.8 1.6 copy-start.10
  435.8 1.6 copy-start.11
  435.8 1.6 copy-start.12
  435.9 218.7 %all-gather.16.cloned.1.call-start = ((), (), s32[]{:S(2)}) async-start(), calls=%async_computation.8 | async-start | bytes 10485760 | tf_op jit(solution)/shard_map/all_gather | solution.py:637
  436.6 286.2 %all-reduce.4.cloned.1.call-start = ((), (), s32[]{:S(2)}) async-start(), calls=%async_computation.10 | async-start | bytes 3538944 | tf_op jit(solution)/shard_map/psum | solution.py:642
  462.6 52.8 %copy-start.4 = (bf16[128,2048]{1,0:T(8,128)(2,1)S(1)}, bf16[128,2048]{1,0:T(8,128)(2,1)}, u32[]{:S(2)}) copy-start(bf16[128,2048]{1,0:T(8,128)(2,1)} %param.13) | copy-start | bytes 1572868
  462.6 104.3 %copy-start.5 = (bf16[128,2048]{1,0:T(8,128)(2,1)S(1)}, bf16[128,2048]{1,0:T(8,128)(2,1)}, u32[]{:S(2)}) copy-start(bf16[128,2048]{1,0:T(8,128)(2,1)} %param.25) | copy-start | bytes 1572868
Sparse Core Ops, SparseCore 0:
  11.3 49.9 all-gather.7
  62.9 57.1 all-gather.9
  123.7 120.1 all-gather.11
  246.8 160.3 all-gather.13
  408.9 53.7 all-gather.17
  465.4 50.0 reduce-scatter.4
  517.7 49.2 reduce-scatter.2
  568.8 85.7 all-gather.15
  658.4 64.3 all-reduce.3

commit v3 on v2

--- a/solution.py
+++ b/solution.py
@@ -394,18 +394,13 @@
 MESH = pl.DeviceIdType.MESH
 
 
-def sum_kernel(chips, x_ref, out_ref, near, mine, far, total, every, other, near_sems, far_sems, back_sems, other_sems):
+def sum_body(chips, x_ref, out_ref, near, mine, far, total, every, other, near_sems, far_sems, back_sems, other_sems):
     wide, rows = x_ref.shape
     half, part = rows // 2, rows // 2 // chips
     tok, ch = lax.axis_index("tok"), lax.axis_index("ch")
     chip, core = ch // 2, ch % 2
     partner = (tok, 2 * chip + 1 - core)
     chips_away = [(tok, 2 * (chip ^ d) + core) for d in range(1, chips)]
-
-    barrier = pltpu.get_barrier_semaphore()
-    for device in [partner] + chips_away:
-        pl.semaphore_signal(barrier, inc=1, device_id=device, device_id_type=MESH)
-    pl.semaphore_wait(barrier, chips)
 
     def send(src, dst, sems, device):
         copy = pltpu.make_async_remote_copy(
@@ -441,55 +436,616 @@
         out_ref[:, columns((1 - core) * chips + (chip ^ d), part)] = other[d].astype(F32)
 
 
+def sum_kernel(chips, *refs):
+    tok, ch = lax.axis_index("tok"), lax.axis_index("ch")
+    barrier = pltpu.get_barrier_semaphore()
+    for device in [(tok, ch ^ 1)] + [(tok, ch ^ (2 * d)) for d in range(1, chips)]:
+        pl.semaphore_signal(barrier, inc=1, device_id=device, device_id_type=MESH)
+    pl.semaphore_wait(barrier, chips)
+    sum_body(chips, *refs)
+
+
+def sum_scratch(wide, rows, chips):
+    half, part = rows // 2, rows // 2 // chips
+    dma = pltpu.SemaphoreType.DMA
+    return [
+        pltpu.VMEM((wide, half), F32),
+        pltpu.VMEM((wide, half), BF16),
+        pltpu.VMEM((chips - 1, wide, part), BF16),
+        pltpu.VMEM((wide, part), BF16),
+        pltpu.VMEM((chips - 1, wide, part), BF16),
+        pltpu.VMEM((chips, wide, part), BF16),
+        dma((2,)),
+        dma((chips - 1, 2)),
+        dma((chips - 1, 2)),
+        dma((chips, 2)),
+    ]
+
+
 def sum_over_ch(x, n, collective_id):
     wide, rows = x.shape
-    chips = n // 2
-    half, part = rows // 2, rows // 2 // chips
-    dma = pltpu.SemaphoreType.DMA
     return pl.pallas_call(
-        functools.partial(sum_kernel, chips),
+        functools.partial(sum_kernel, n // 2),
         out_shape=jax.ShapeDtypeStruct((wide, rows), F32),
         in_specs=[pl.BlockSpec(memory_space=pltpu.VMEM)],
         out_specs=pl.BlockSpec(memory_space=pltpu.VMEM),
-        scratch_shapes=[
-            pltpu.VMEM((wide, half), F32),
-            pltpu.VMEM((wide, half), BF16),
-            pltpu.VMEM((chips - 1, wide, part), BF16),
-            pltpu.VMEM((wide, part), BF16),
-            pltpu.VMEM((chips - 1, wide, part), BF16),
-            pltpu.VMEM((chips, wide, part), BF16),
-            dma((2,)), dma((chips - 1, 2)), dma((chips - 1, 2)), dma((chips, 2)),
-        ],
+        scratch_shapes=sum_scratch(wide, rows, n // 2),
         compiler_params=pltpu.CompilerParams(collective_id=collective_id, has_side_effects=True, vmem_limit_bytes=16 << 20),
         name="sum_over_ch",
     )(x)
 
 
-def total_over_ch(x, n, collective_id):
-    if x.shape[1] // n % 128 == 0 and n // 2 & (n // 2 - 1) == 0 and n <= 8:
-        return sum_over_ch(x, n, collective_id)
-    return lax.psum(x, "ch")
+def front_kernel(
+    chips, input_ref, gain_ref, cot_ref, label_ref, iw_ref, ow_ref, cw_ref, cb_ref, xw_ref,
+    scaled_ref, core_cot_ref, near_cot_ref, labels_ref, gate_ref, gated_grad_ref, conv_ref, inner_out_ref, proj_ref,
+    own_rows, in_w, out_w, chunk_rows, staged, xz, proj_part, pad,
+    in_sem, out_sem, load_sem, own_sem,
+    line_send, line_recv, near_send, near_recv, tok_send, tok_recv, diag_send, diag_recv,
+    xz_send, xz_recv, lab_send, lab_recv, lab_tok_send, lab_tok_recv, *sum_refs,
+):
+    n = 2 * chips
+    length, deep = input_ref.shape
+    group, chunk = n * length, 2 * length
+    mods, width = ow_ref.shape[0], ow_ref.shape[1]
+    tok, ch = lax.axis_index("tok"), lax.axis_index("ch")
+    chip, core = ch // 2, ch % 2
+
+    fetch_in = pltpu.make_async_copy(iw_ref, in_w, in_sem)
+    fetch_in.start()
+    fetch_out = pltpu.make_async_copy(ow_ref, out_w, out_sem)
+    fetch_out.start()
+
+    rows = input_ref[...].astype(F32)
+    inverse = lax.rsqrt(jnp.mean(rows * rows, axis=-1, keepdims=True) + 1e-05)
+    own_rows[...] = (rows * inverse * gain_ref[...].astype(F32)).astype(BF16)
+    labels_ref[tok, ch] = label_ref[...]
+
+    def block(g, device):
+        return pl.ds(pl.multiple_of(g * group + device * length, length), length)
+
+    own = (
+        pltpu.make_async_copy(own_rows, scaled_ref.at[block(tok, ch)], own_sem.at[0]),
+        pltpu.make_async_copy(cot_ref, core_cot_ref.at[pl.ds(pl.multiple_of(chip * length, length), length)], own_sem.at[1]),
+    )
+    for copy in own:
+        copy.start()
+
+    barrier = pltpu.get_barrier_semaphore()
+    peers = [(tok, ch ^ e) for e in range(1, n)] + [(tok ^ g, ch) for g in range(1, 4)]
+    for device in peers:
+        pl.semaphore_signal(barrier, inc=1, device_id=device, device_id_type=MESH)
+    pl.semaphore_wait(barrier, len(peers))
+
+    def remote(src, dst, send_sem, recv_sem, device):
+        return pltpu.make_async_remote_copy(
+            src_ref=src, dst_ref=dst, send_sem=send_sem, recv_sem=recv_sem, device_id=device, device_id_type=MESH
+        )
+
+    def arrive(ref, sem):
+        pltpu.make_async_copy(ref, ref, sem).wait()
+
+    label_copies = [
+        remote(labels_ref.at[tok, ch], labels_ref.at[tok, ch], lab_send.at[e - 1], lab_recv.at[e - 1], (tok, ch ^ e))
+        for e in range(1, n)
+    ]
+    for copy in label_copies:
+        copy.start()
+
+    def from_line(x, o):
+        if x == 0:
+            return scaled_ref.at[block(tok, 2 * o + core)]
+        return core_cot_ref.at[pl.ds(pl.multiple_of(o * length, length), length)]
+
+    def line_copy(x, o, side):
+        ref = from_line(x, o)
+        target = lax.rem(ch + (2 if side == 0 else n - 2), n)
+        return remote(ref, ref, line_send.at[x, side, o], line_recv.at[x, o], (tok, target))
+
+    def near_copy(x, o, g):
+        if x == 0:
+            src = dst = scaled_ref.at[block(tok ^ g, 2 * o + core)]
+        else:
+            src, dst = from_line(1, o), near_cot_ref.at[pl.ds(pl.multiple_of(o * length, length), length)]
+        return remote(src, dst, near_send.at[x, g, o], near_recv.at[x, g, o], (tok, ch ^ 1))
+
+    def tok_copy(o, side):
+        ref = scaled_ref.at[block(tok, 2 * o + core)]
+        return remote(ref, ref, tok_send.at[side, o], tok_recv.at[side, o], (tok ^ (1 + side), ch))
+
+    def half_block(g, o, side):
+        start = g * group + (2 * o + core) * length + side * (length // 2)
+        return pl.ds(pl.multiple_of(start, length // 2), length // 2)
+
+    def diag_copy(o, side):
+        ref = scaled_ref.at[half_block(tok ^ (1 + side), o, side)]
+        return remote(ref, ref, diag_send.at[side, o], diag_recv.at[side, o], (tok ^ (2 - side), ch))
+
+    def goes(o, side):
+        return (o <= chip) & (chip < chips - 1) if side == 0 else (o >= chip) & (chip > 0)
+
+    def launch(x, o):
+        for side in range(2):
+            pl.when(goes(o, side))(line_copy(x, o, side).start)
+        near_copy(x, o, 0).start()
+        if x == 0:
+            for side in range(2):
+                tok_copy(o, side).start()
+
+    def accept(x, o):
+        arrive(from_line(x, o), line_recv.at[x, o])
+        launch(x, o)
+
+    def pass_on(o):
+        for side in range(2):
+            arrive(scaled_ref.at[block(tok ^ (1 + side), 2 * o + core)], tok_recv.at[side, o])
+            diag_copy(o, side).start()
+            near_copy(0, o, 1 + side).start()
+
+    def pass_last(o):
+        for side in range(2):
+            arrive(scaled_ref.at[half_block(tok ^ 3, o, side)], diag_recv.at[side, o])
+        near_copy(0, o, 3).start()
+
+    def load(x, o):
+        if x == 0:
+            arrive(scaled_ref.at[block(tok, 2 * o + 1 - core)], near_recv.at[0, 0, o])
+            source = scaled_ref.at[pl.ds(pl.multiple_of(tok * group + o * chunk, chunk), chunk)]
+            copies = [pltpu.make_async_copy(source, chunk_rows, load_sem.at[0])]
+        else:
+            other = near_cot_ref.at[pl.ds(pl.multiple_of(o * length, length), length)]
+            arrive(other, near_recv.at[1, 0, o])
+            copies = [
+                pltpu.make_async_copy(
+                    ref, chunk_rows.at[pl.ds(pl.multiple_of(q * length, length), length)], load_sem.at[at]
+                )
+                for at, (ref, q) in enumerate(((from_line(1, o), core), (other, 1 - core)))
+            ]
+        for copy in copies:
+            copy.start()
+        for copy in copies:
+            copy.wait()
+
+    def label_column(o):
+        return jnp.concatenate(
+            [labels_ref[tok, 2 * o + q].astype(F32).T[:, 0:1] for q in range(2)], axis=0
+        )
+
+    kind = ch // chips
+    pair = ch % chips
+
+    def xz_copies(o, h):
+        target = 2 * pair + h
+        src = staged.at[o, h]
+        dst = xz.at[kind, pl.ds(pl.multiple_of(o * chunk, chunk), chunk)]
+        return target, remote(src, dst, xz_send.at[o, h], xz_recv.at[kind, o], (tok, target)), pltpu.make_async_copy(
+            src, dst, xz_recv.at[kind, o]
+        )
+
+    def project(o):
+        load(0, o)
+        label = label_column(o)
+        for h in range(2):
+            x = chunk_rows[...]
+            parts = [dot(x, in_w[m, :, pl.ds(h * width, width)]) for m in range(mods)]
+            staged[o, h] = pick(parts, label).astype(BF16)
+            target, copy, local = xz_copies(o, h)
+            pl.when(target != ch)(copy.start)
+            pl.when(target == ch)(local.start)
+
+    def project_back(o):
+        load(1, o)
+        label = label_column(o)
+        x = chunk_rows[...]
+        parts = [dot_bt(x, out_w[m]) for m in range(mods)]
+        gated_grad_ref[pl.ds(pl.multiple_of(o * chunk, chunk), chunk), :] = pick(parts, label).astype(BF16)
+
+    def both_sides(i, fn):
+        for o in (chip - i, chip + i):
+            pl.when((o >= 0) & (o < chips))(functools.partial(fn, o))
+
+    def every_distance(fn):
+        fn(chip)
+
+        def body(i, carry):
+            both_sides(i, fn)
+            return carry
+
+        lax.fori_loop(1, chips, body, 0)
+
+    own[0].wait()
+    launch(0, chip)
+    for e in range(1, n):
+        arrive(labels_ref.at[tok, ch ^ e], lab_recv.at[e - 1])
+    fetch_in.wait()
+    project(chip)
+
+    def step(i, carry):
+        both_sides(i, functools.partial(accept, 0))
+        both_sides(i, project)
+        pl.when(i == 1)(functools.partial(pass_on, chip))
+        pl.when(i > 1)(functools.partial(both_sides, i - 1, pass_on))
+        return carry
+
+    lax.fori_loop(1, chips, step, 0)
+    own[1].wait()
+    launch(1, chip)
+    label_tok = [
+        remote(labels_ref.at[tok], labels_ref.at[tok], lab_tok_send.at[g - 1], lab_tok_recv.at[g - 1], (tok ^ g, ch))
+        for g in range(1, 4)
+    ]
+    for copy in label_tok:
+        copy.start()
+    fetch_out.wait()
+    project_back(chip)
+    both_sides(chips - 1, pass_on)
+
+    def step_back(i, carry):
+        both_sides(i, functools.partial(accept, 1))
+        both_sides(i, project_back)
+        return carry
+
+    lax.fori_loop(1, chips - 1, step_back, 0)
+    every_distance(pass_last)
+
+    for o in range(chips):
+        for a in range(2):
+            arrive(xz.at[a, pl.ds(o * chunk, chunk)], xz_recv.at[a, o])
+    gate_ref[...] = xz[1]
+    taps = cw_ref.shape[0]
+    lead = (taps - 1) * GROUP
+    inner = by_time(xz[0])
+    inner_out_ref[...] = inner.astype(BF16)
+    pad[pl.ds(0, lead), :] = jnp.zeros((lead, width), F32)
+    pad[pl.ds(lead, group), :] = inner
+    conv = jnp.broadcast_to(cb_ref[...].astype(F32), (group, width))
+    for tap in range(taps):
+        conv = conv + cw_ref[pl.ds(tap, 1), :].astype(F32) * pad[pl.ds(tap * GROUP, group), :]
+    conv_ref[...] = conv
+    act = conv * sigmoid(conv)
+    label = jnp.concatenate(
+        [jnp.broadcast_to(labels_ref[tok, d].astype(F32).T[:, 0:1], (length, 128)) for d in range(n)], axis=0
+    )
+    label = jnp.concatenate([by_time(label)] * (width // 128), axis=1)
+    total = None
+    for m in range(mods):
+        high, low = halves(jnp.where(label == m, act, 0.0))
+        part = dot_bt(xw_ref[m], high) + dot_bt(xw_ref[m], low)
+        total = part if total is None else total + part
+    proj_part[...] = total
+
+    both_sides(chips - 1, functools.partial(accept, 1))
+    sum_body(chips, proj_part, proj_ref, *sum_refs)
+    both_sides(chips - 1, project_back)
+
+    def finish(o, carry):
+        for g in range(4):
+            if g > 0:
+                arrive(scaled_ref.at[block(tok ^ g, 2 * o + 1 - core)], near_recv.at[0, g, o])
+            near_copy(0, o, g).wait_send()
+        near_copy(1, o, 0).wait_send()
+        for side in range(2):
+            for x in range(2):
+                pl.when(goes(o, side))(line_copy(x, o, side).wait_send)
+            tok_copy(o, side).wait_send()
+            diag_copy(o, side).wait_send()
+        return carry
+
+    lax.fori_loop(0, chips, finish, 0)
+    for o in range(chips):
+        for h in range(2):
+            target, copy, _ = xz_copies(o, h)
+            pl.when(target != ch)(copy.wait_send)
+    for copy in label_copies:
+        copy.wait_send()
+    for g in range(1, 4):
+        arrive(labels_ref.at[tok ^ g], lab_tok_recv.at[g - 1])
+        label_tok[g - 1].wait_send()
+
+
+def way_in(block_input, gain, cotangent, modality, in_weight, out_weight, conv_weight, conv_bias, x_weight, n, collective_id):
+    length, deep = block_input.shape
+    mods, width = out_weight.shape[0], out_weight.shape[1]
+    group, chips = n * length, n // 2
+    wide = x_weight.shape[1]
+    lead = (conv_weight.shape[0] - 1) * GROUP
+    dma = pltpu.SemaphoreType.DMA
+    vmem = pl.BlockSpec(memory_space=pltpu.VMEM)
+    any_space = pl.BlockSpec(memory_space=pl.ANY)
+    return pl.pallas_call(
+        functools.partial(front_kernel, chips),
+        out_shape=(
+            jax.ShapeDtypeStruct((4 * group, deep), BF16),
+            jax.ShapeDtypeStruct((chips * length, deep), BF16),
+            jax.ShapeDtypeStruct((chips * length, deep), BF16),
+            jax.ShapeDtypeStruct((4, n, 8, length), jnp.int32),
+            jax.ShapeDtypeStruct((group, width), BF16),
+            jax.ShapeDtypeStruct((group, width), BF16),
+            jax.ShapeDtypeStruct((group, width), F32),
+            jax.ShapeDtypeStruct((group, width), BF16),
+            jax.ShapeDtypeStruct((wide, group), F32),
+        ),
+        in_specs=[vmem, vmem, any_space, vmem, any_space, any_space, vmem, vmem, vmem],
+        out_specs=(any_space, any_space, any_space, vmem, vmem, vmem, vmem, vmem, vmem),
+        scratch_shapes=[
+            pltpu.VMEM((length, deep), BF16),
+            pltpu.VMEM(in_weight.shape, BF16),
+            pltpu.VMEM(out_weight.shape, BF16),
+            pltpu.VMEM((2 * length, deep), BF16),
+            pltpu.VMEM((chips, 2, 2 * length, width), BF16),
+            pltpu.VMEM((2, group, width), BF16),
+            pltpu.VMEM((wide, group), F32),
+            pltpu.VMEM((group + lead, width), F32),
+            dma, dma, dma((2,)), dma((2,)),
+            dma((2, 2, chips)), dma((2, chips)), dma((2, 4, chips)), dma((2, 4, chips)),
+            dma((2, chips)), dma((2, chips)), dma((2, chips)), dma((2, chips)),
+            dma((chips, 2)), dma((2, chips)), dma((n - 1,)), dma((n - 1,)), dma((3,)), dma((3,)),
+        ] + sum_scratch(wide, group, chips),
+        compiler_params=params(collective_id=collective_id, has_side_effects=True),
+        cost_estimate=pl.CostEstimate(flops=10**11, bytes_accessed=10**8, transcendentals=0),
+        name="way_in",
+    )(
+        block_input, gain[None, :], cotangent, jnp.broadcast_to(modality[None, :], (8, length)),
+        in_weight, out_weight, conv_weight, conv_bias[None, :], x_weight,
+    )
+
+
+def back_kernel(
+    chips, dinner_ref, dgate_ref, w_ref, label_ref, input_ref, cot_ref, gain_ref, half_cot_ref,
+    xall_ref, row_grad_ref, gain_sum_ref, near_cot_ref,
+    weights, sends, near_part, chip_sums, arrived, mine, gain_send, gain_arrived, gain_mine, gain_others,
+    w_sem, to_col, from_own, to_tok, from_tok, to_diag, from_diag, to_near, from_near, to_row, from_row, to_gain, from_gain, to_gain_tok, from_gain_tok, cot_sems,
+):
+    n = 2 * chips
+    group, width = dinner_ref.shape
+    mods, deep = w_ref.shape[0], w_ref.shape[1]
+    length = group // n
+    chunk = 2 * length
+    tok, ch = lax.axis_index("tok"), lax.axis_index("ch")
+    chip, core = ch // 2, ch % 2
+    beside, below = tok ^ 1, tok ^ 2
+
+    fetch = pltpu.make_async_copy(w_ref, weights, w_sem)
+    fetch.start()
+
+    barrier = pltpu.get_barrier_semaphore()
+    peers = [(tok, ch ^ e) for e in range(1, n)] + [(tok ^ g, ch) for g in range(1, 4)]
+    for device in peers:
+        pl.semaphore_signal(barrier, inc=1, device_id=device, device_id_type=MESH)
+    pl.semaphore_wait(barrier, len(peers))
+
+    def remote(src, dst, send_sem, recv_sem, device):
+        return pltpu.make_async_remote_copy(
+            src_ref=src, dst_ref=dst, send_sem=send_sem, recv_sem=recv_sem, device_id=device, device_id_type=MESH
+        )
+
+    def rows_of(index, size):
+        return pl.ds(pl.multiple_of(index * size, size), size)
+
+    def all_rows(group_index, chunk_index):
+        return pl.ds(pl.multiple_of(group_index * group + chunk_index * chunk, chunk), chunk)
+
+    cot_near = remote(half_cot_ref, near_cot_ref, cot_sems.at[0], cot_sems.at[1], (tok, ch ^ 1))
+
+    order = [2, 3, 1, 0]
+    owners = [ch // 2, chips + ch // 2]
+    out_copies = []
+
+    def give(j):
+        for a, src_ref in enumerate((dinner_ref, dgate_ref)):
+            owner = owners[a]
+            k = owner // 2 ^ j
+            src = src_ref.at[rows_of(k, chunk)]
+            dst = xall_ref.at[core, all_rows(tok, k)]
+            copy = remote(src, dst, to_col.at[j, a], from_own.at[j, core], (tok, owner))
+            local = pltpu.make_async_copy(src, dst, from_own.at[j, core])
+            pl.when(owner != ch)(copy.start)
+            pl.when(owner == ch)(local.start)
+            out_copies.append((owner, copy))
+
+    give(order[0])
+    give(order[1])
+    fetch.wait()
+    cot_near.start()
+    tok_copies, row_copies, diag_copies, near_copies = [], [], [], []
+
+    def pass_on(j):
+        k = chip ^ j
+        for side, (source, target) in enumerate(((beside, below), (below, beside))):
+            whole = xall_ref.at[:, all_rows(source, k)]
+            pltpu.make_async_copy(whole, whole, from_tok.at[side, j]).wait()
+            part = xall_ref.at[side, all_rows(source, k)]
+            copy = remote(part, part, to_diag.at[side, j], from_diag.at[side, j], (target, ch))
+            copy.start()
+            diag_copies.append(copy)
+
+    def both_cores(j):
+        pltpu.make_async_copy(near_part.at[j], near_part.at[j], from_near.at[j]).wait()
+        value = sends[j, rows_of(core, length), :].astype(F32) + near_part[j].astype(F32)
+        if j == 0:
+            mine[...] = value
+        else:
+            chip_sums[j - 1] = value.astype(BF16)
+            target = 2 * (chip ^ j) + core
+            copy = remote(chip_sums.at[j - 1], arrived.at[j - 1], to_row.at[j - 1], from_row.at[j - 1], (tok, target))
+            copy.start()
+            row_copies.append(copy)
+
+    for at, j in enumerate(order):
+        k = chip ^ j
+        for h in range(2):
+            half = xall_ref.at[h, all_rows(tok, k)]
+            pltpu.make_async_copy(half, half, from_own.at[j, h]).wait()
+        whole = xall_ref.at[:, all_rows(tok, k)]
+        for side, target in enumerate((beside, below)):
+            copy = remote(whole, whole, to_tok.at[side, j], from_tok.at[side, j], (target, ch))
+            copy.start()
+            tok_copies.append(copy)
+        if at + 2 < chips:
+            give(order[at + 2])
+        label = label_ref[rows_of(k, chunk), :]
+        halves_of = [xall_ref[h, all_rows(tok, k), :] for h in range(2)]
+        tile = min(deep, 512)
+
+        def product(i, carry, label=label, halves_of=halves_of, j=j):
+            at = pl.ds(pl.multiple_of(i * tile, tile), tile)
+            total = None
+            for m in range(mods):
+                for h in range(2):
+                    x = jnp.where(label == m, halves_of[h], jnp.zeros_like(halves_of[h]))
+                    part = dot_bt(x, weights[m, at, pl.ds(h * width, width)])
+                    total = part if total is None else total + part
+            sends[j, :, at] = total.astype(BF16)
+            return carry
+
+        lax.fori_loop(0, deep // tile, product, 0)
+        copy = remote(
+            sends.at[j, rows_of(1 - core, length)], near_part.at[j], to_near.at[j], from_near.at[j], (tok, ch ^ 1)
+        )
+        copy.start()
+        near_copies.append(copy)
+        if at >= 1:
+            pass_on(order[at - 1])
+            both_cores(order[at - 1])
+    pass_on(order[-1])
+    both_cores(order[-1])
+
+    total = mine[...]
+    for e in range(chips - 1):
+        pltpu.make_async_copy(arrived.at[e], arrived.at[e], from_row.at[e]).wait()
+        total = total + arrived[e].astype(F32)
+    rows = input_ref[...].astype(F32)
+    inverse = lax.rsqrt(jnp.mean(rows * rows, axis=-1, keepdims=True) + 1e-05)
+    normed = rows * inverse
+    ng = total * gain_ref[...].astype(F32)
+    row_grad_ref[...] = cot_ref[...].astype(F32) + inverse * (
+        ng - normed * jnp.mean(ng * normed, axis=-1, keepdims=True)
+    )
+    own = deep // n
+    gain_term = jnp.sum(total * normed, axis=0, keepdims=True)
+    for d in range(n):
+        gain_send[d] = jnp.broadcast_to(gain_term[:, d * own : (d + 1) * own], (8, own))
+    gain_copies = []
+    for e in range(1, n):
+        copy = remote(gain_send.at[ch ^ e], gain_arrived.at[e - 1], to_gain.at[e - 1], from_gain.at[e - 1], (tok, ch ^ e))
+        copy.start()
+        gain_copies.append(copy)
+    value = gain_send[ch]
+    for e in range(1, n):
+        gain_copies[e - 1].wait()
+        value = value + gain_arrived[e - 1]
+    gain_mine[...] = value
+    gain_copies = []
+    for g in range(1, 4):
+        copy = remote(gain_mine, gain_others.at[g - 1], to_gain_tok.at[g - 1], from_gain_tok.at[g - 1], (tok ^ g, ch))
+        copy.start()
+        gain_copies.append(copy)
+    for copy in gain_copies:
+        copy.wait()
+    even, odd = gain_mine[...] + gain_others[0], gain_others[1] + gain_others[2]
+    gain_sum_ref[...] = even + odd
+
+    for j in range(chips):
+        for side in range(2):
+            part = xall_ref.at[side, all_rows(tok ^ 3, chip ^ j)]
+            pltpu.make_async_copy(part, part, from_diag.at[side, j]).wait()
+    for owner, copy in out_copies:
+        pl.when(owner != ch)(copy.wait_send)
+    for copy in tok_copies + diag_copies + row_copies + near_copies:
+        copy.wait_send()
+    cot_near.wait()
+
+
+def way_back(dinner, dgate, w, label, block_input, cotangent, gain, half_cot, n, collective_id):
+    group, width = dinner.shape
+    mods, deep, _ = w.shape
+    chips, length = n // 2, group // n
+    dma = pltpu.SemaphoreType.DMA
+    vmem = pl.BlockSpec(memory_space=pltpu.VMEM)
+    any_space = pl.BlockSpec(memory_space=pl.ANY)
+    return pl.pallas_call(
+        functools.partial(back_kernel, chips),
+        out_shape=(
+            jax.ShapeDtypeStruct((2, 4 * group, width), BF16),
+            jax.ShapeDtypeStruct((length, deep), F32),
+            jax.ShapeDtypeStruct((8, deep // n), F32),
+            jax.ShapeDtypeStruct(half_cot.shape, BF16),
+        ),
+        in_specs=[vmem, vmem, any_space, vmem, vmem, vmem, vmem, any_space],
+        out_specs=(vmem, vmem, vmem, any_space),
+        scratch_shapes=[
+            pltpu.VMEM(w.shape, BF16),
+            pltpu.VMEM((chips, 2 * length, deep), BF16),
+            pltpu.VMEM((chips, length, deep), BF16),
+            pltpu.VMEM((chips - 1, length, deep), BF16),
+            pltpu.VMEM((chips - 1, length, deep), BF16),
+            pltpu.VMEM((length, deep), F32),
+            pltpu.VMEM((n, 8, deep // n), F32),
+            pltpu.VMEM((n - 1, 8, deep // n), F32),
+            pltpu.VMEM((8, deep // n), F32),
+            pltpu.VMEM((3, 8, deep // n), F32),
+            dma, dma((chips, 2)), dma((chips, 2)), dma((2, chips)), dma((2, chips)), dma((2, chips)), dma((2, chips)),
+            dma((chips,)), dma((chips,)), dma((chips - 1,)), dma((chips - 1,)), dma((n - 1,)), dma((n - 1,)), dma((3,)), dma((3,)), dma((2,)),
+        ],
+        compiler_params=params(collective_id=collective_id, has_side_effects=True),
+        cost_estimate=pl.CostEstimate(flops=10**11, bytes_accessed=10**8, transcendentals=0),
+        name="way_back",
+    )(dinner, dgate, w, label, block_input, cotangent, gain[None, :], half_cot)
+
+
+def grad_two_kernel(left_ref, right_ref, other_ref, label_ref, out_ref):
+    half = right_ref.shape[0]
+    turned, label = left_ref[...].T, label_ref[...]
+    for m in range(out_ref.shape[0]):
+        masked = jnp.where(label == m, turned, jnp.zeros_like(turned))
+        out_ref[m] = dot(masked[:, :half], right_ref[...]) + dot(masked[:, half:], other_ref[...])
+
+
+def weight_grad_two(left, right, other, label, mods, tile):
+    rows, deep = left.shape
+    half, wide = right.shape
+    whole = pl.BlockSpec((half, wide), lambda i: (0, 0), pipeline_mode=pl.Buffered(1))
+    return pl.pallas_call(
+        grad_two_kernel,
+        out_shape=jax.ShapeDtypeStruct((mods, deep, wide), F32),
+        grid=(deep // tile,),
+        in_specs=[pl.BlockSpec((rows, tile), lambda i: (0, i)), whole, whole, pl.BlockSpec((1, rows), lambda i: (0, 0))],
+        out_specs=pl.BlockSpec((mods, tile, wide), lambda i: (0, i, 0)),
+        compiler_params=params(),
+        cost_estimate=pl.CostEstimate(
+            flops=2 * mods * rows * deep * wide,
+            bytes_accessed=2 * rows * (deep + wide) + 4 * mods * deep * wide,
+            transcendentals=0,
+        ),
+        name="weight_grad_two",
+    )(left, right, other, label)
 
 
 def grad_kernel(left_ref, right_ref, label_ref, out_ref):
-    left, right, label = left_ref[...], right_ref[...], label_ref[...]
+    left, label = left_ref[...], label_ref[...]
+    wide = right_ref.shape[2]
     turned = left.T
     for m in range(out_ref.shape[0]):
-        out_ref[m] = dot(jnp.where(label == m, turned, jnp.zeros_like(turned)), right)
+        masked = jnp.where(label == m, turned, jnp.zeros_like(turned))
+        for h in range(right_ref.shape[0]):
+            out_ref[m, :, pl.ds(h * wide, wide)] = dot(masked, right_ref[h])
 
 
 def grad_part_kernel(left_ref, right_ref, label_ref, out_ref):
-    left, right, label = left_ref[...], right_ref[...], label_ref[...]
+    left, label = left_ref[...], label_ref[...]
+    wide = right_ref.shape[2]
     turned = left.T
     first = pl.program_id(1) == 0
     for m in range(out_ref.shape[0]):
-        part = dot(jnp.where(label == m, turned, jnp.zeros_like(turned)), right)
-        out_ref[m] = jnp.where(first, part, out_ref[m] + part)
+        masked = jnp.where(label == m, turned, jnp.zeros_like(turned))
+        for h in range(right_ref.shape[0]):
+            at = pl.ds(h * wide, wide)
+            part = dot(masked, right_ref[h])
+            out_ref[m, :, at] = jnp.where(first, part, out_ref[m, :, at] + part)
 
 
 def weight_grad(left, right, label, mods, tile):
     rows, deep = left.shape
-    wide = right.shape[1]
+    wide = right.shape[0] * right.shape[2]
     block = min(rows, 4096)
     tile = min(tile, deep)
     return pl.pallas_call(
@@ -498,7 +1054,7 @@
         grid=(deep // tile, rows // block),
         in_specs=[
             pl.BlockSpec((block, tile), lambda i, j: (j, i)),
-            pl.BlockSpec((block, wide), lambda i, j: (j, 0)),
+            pl.BlockSpec((right.shape[0], block, right.shape[2]), lambda i, j: (0, j, 0)),
             pl.BlockSpec((1, block), lambda i, j: (0, j)),
         ],
         out_specs=pl.BlockSpec((mods, tile, wide), lambda i, j: (0, i, 0)),
@@ -575,31 +1131,39 @@
     mods = in_weight.shape[0]
     length = block_input.shape[0]
     count = n // GROUP
+    fast = n == GROUP and lax.axis_size("tok") == 4 and length % 128 == 0
     rows_float = block_input.astype(F32)
     gain = norm_gain.astype(F32)
     inverse = lax.rsqrt(jnp.mean(rows_float * rows_float, axis=-1, keepdims=True) + 1e-05)
     normed = rows_float * inverse
     scaled = (normed * gain[None, :]).astype(BF16)
 
-    group_rows = lax.all_gather(scaled, "ch", axis=0, tiled=True)
-    every_label = lax.all_gather(modality, ("tok", "ch"), axis=0, tiled=True)
     token_group = n * length
+    if fast:
+        every_scaled, core_cot, _, labels, gate, gated_grad, conv, inner_by_time, proj = way_in(
+            block_input, norm_gain, cotangent, modality, in_weight, out_weight, conv_weight, conv_bias, x_weight, n, 0
+        )
+        every_label = labels[:, :, 0, :].reshape(4 * token_group)
+        half_cot = lax.all_gather(core_cot, "tok", axis=0, tiled=False)
+    else:
+        every_label = lax.all_gather(modality, ("tok", "ch"), axis=0, tiled=True)
     group_label = lax.dynamic_slice_in_dim(every_label, lax.axis_index("tok") * token_group, token_group, 0)
     label = group_label[:, None]
     label_by_time = group_label.reshape(count, GROUP, length).transpose(0, 2, 1).reshape(token_group, 1)
     label_row = label_by_time.reshape(1, token_group)
 
-    every_scaled = lax.all_gather(scaled, ("tok", "ch"), axis=0, tiled=True)
-    every_cot = lax.all_gather(cotangent, ("tok", "ch"), axis=0, tiled=True)
-    xz = routed_select(group_rows, label, in_weight, 256, False)
-    inner, gate = to_owners(xz, n)
-    group_cot = lax.all_gather(cotangent, "ch", axis=0, tiled=True)
-    gated_grad = routed_select(group_cot, label, out_weight, 128, True)
-
-    conv, inner_by_time, proj_part = by_groups(
-        lambda a, b: conv_forward(a, b, conv_weight, conv_bias, x_weight), count, (inner, label_row), (0, 1), (0, 0, 1)
-    )
-    proj = total_over_ch(proj_part, n, 0)
+    if not fast:
+        group_rows = lax.all_gather(scaled, "ch", axis=0, tiled=True)
+        every_scaled = lax.all_gather(scaled, ("tok", "ch"), axis=0, tiled=True)
+        every_cot = lax.all_gather(cotangent, ("tok", "ch"), axis=0, tiled=True)
+        xz = routed_select(group_rows, label, in_weight, 256, False)
+        inner, gate = to_owners(xz, n)
+        group_cot = lax.all_gather(cotangent, "ch", axis=0, tiled=True)
+        gated_grad = routed_select(group_cot, label, out_weight, 128, True)
+        conv, inner_by_time, proj_part = by_groups(
+            lambda a, b: conv_forward(a, b, conv_weight, conv_bias, x_weight), count, (inner, label_row), (0, 1), (0, 0, 1)
+        )
+        proj = lax.psum(proj_part, "ch")
 
     gated, dgate, dact, dproj_part, ddtw, ddtb, dalog, dskip = by_groups(
         lambda a, b, c, d, e, f: scan_both(a, b, c, d, e, f, dt_weight, dt_bias, a_log, skip_gain),
@@ -608,9 +1172,7 @@
         (0, 1, 0, 0, 0, 1),
         (0, 0, 0, 1),
     )
-    if count == 1:
-        dproj_part, every_scaled = lax.optimization_barrier((dproj_part, every_scaled))
-    dproj = total_over_ch(dproj_part, n, 1)
+    dproj = sum_over_ch(dproj_part, n, 1) if fast else lax.psum(dproj_part, "ch")
 
     dinner, dxw, dcw, dcb = by_groups(
         lambda a, b, c, d, e, f: conv_backward(a, b, c, d, e, f, conv_weight, x_weight),
@@ -619,31 +1181,52 @@
         (0, 0, 0, 1, 0, 1),
         (0,),
     )
-    xz_grad = to_columns(dinner, dgate, n)
-
-    if count == 1:
-        xz_grad, every_cot = lax.optimization_barrier((xz_grad, every_cot))
+    every_label = every_label[None, :]
+    if fast:
+        half_cot = half_cot.reshape(2 * token_group, half_cot.shape[-1])
+        every_grad, row_grad, gain_grad, near_cot = way_back(
+            dinner, dgate, in_weight, label, block_input, cotangent, norm_gain, half_cot, n, 2
+        )
+        gain_grad = gain_grad[0]
+    else:
+        xz_grad = to_columns(dinner, dgate, n)
+        scaled_part = routed_spread(xz_grad, label, in_weight, 256, True, BF16)
+        scaled_grad = lax.psum_scatter(scaled_part, "ch", scatter_dimension=0, tiled=True).astype(F32)
+        gain_grad = lax.psum_scatter(jnp.sum(scaled_grad * normed, axis=0), "ch", scatter_dimension=0, tiled=True)
+        ng = scaled_grad * gain[None, :]
+        row_grad = cotangent.astype(F32) + inverse * (ng - normed * jnp.mean(ng * normed, axis=-1, keepdims=True))
+        every_grad = lax.all_gather(xz_grad, "tok", axis=0, tiled=True)[None]
+
+    small = (dxw, ddtw, ddtb, dcw, dcb, dalog, dskip)
+    every_gated = lax.all_gather(gated, "tok", axis=0, tiled=True)
+    if fast:
+        gated, row_grad, small = lax.optimization_barrier((gated, row_grad, small))
     branch_part = routed_spread(gated, label, out_weight, 512, False, BF16)
     branch = lax.psum_scatter(branch_part, "ch", scatter_dimension=0, tiled=True).astype(F32)
     block_out = (rows_float + branch).astype(BF16)
-
-    scaled_part = routed_spread(xz_grad, label, in_weight, 256, True, BF16)
-    scaled_grad = lax.psum_scatter(scaled_part, "ch", scatter_dimension=0, tiled=True).astype(F32)
-    gain_grad = jnp.sum(scaled_grad * normed, axis=0)
-    ng = scaled_grad * gain[None, :]
-    row_grad = cotangent.astype(F32) + inverse * (ng - normed * jnp.mean(ng * normed, axis=-1, keepdims=True))
-
-    every_gated = lax.all_gather(gated, "tok", axis=0, tiled=True)
-    every_grad = lax.all_gather(xz_grad, "tok", axis=0, tiled=True)
-    every_label = every_label[None, :]
-    out_weight_grad = weight_grad(every_gated, every_cot, every_label, mods, 128)
+    if fast:
+        core = lax.axis_index("ch") % 2
+
+        def own_first(value):
+            halved = value.reshape((-1, 2, length) + value.shape[1:])
+            swapped = jnp.where(core == 0, halved, halved[:, ::-1])
+            return jnp.moveaxis(swapped, 1, 0).reshape(value.shape)
+
+        out_weight_grad = weight_grad_two(
+            own_first(every_gated), half_cot, near_cot, own_first(every_label[0])[None, :], mods, 128
+        )
+    else:
+        out_weight_grad = weight_grad(every_gated, every_cot[None], every_label, mods, 128)
     in_weight_grad = weight_grad(every_scaled, every_grad, every_label, mods, 256)
-
-    small = lax.psum((dxw, ddtw, ddtb, dcw, dcb, dalog, dskip), "tok")
-    gain_grad = lax.psum(gain_grad, ("tok", "ch"))
-    own = gain_grad.shape[0] // n
-    gain_grad = lax.dynamic_slice_in_dim(gain_grad, lax.axis_index("ch") * own, own, 0)
-    dxw, ddtw, ddtb, dcw, dcb, dalog, dskip = small
+    if not fast:
+        gain_grad = lax.psum(gain_grad, "tok")
+    flat = [value.reshape(-1, value.shape[-1]) for value in small]
+    total = lax.psum(jnp.concatenate(flat, axis=0), "tok")
+    start, sums = 0, []
+    for value, rows in zip(small, flat, strict=True):
+        sums.append(lax.slice_in_dim(total, start, start + rows.shape[0], axis=0).reshape(value.shape))
+        start += rows.shape[0]
+    dxw, ddtw, ddtb, dcw, dcb, dalog, dskip = sums
     return (
         block_out,
         row_grad,

time: 742 us -> 508 us (0.68)
  waiting for transfers between devices: 257 us -> 0.07 us
  Pallas kernels: 323 us -> 454 us
  blocking collectives: 103 us -> 0 us
  local copies, waits for them, and re-layouts: 12.8 us -> 29.6 us
  other arithmetic: 15.4 us -> 5.73 us
  starting transfers between devices: 8.35 us -> 0.55 us
    pallas_call x5 -> x4, Pallas kernels: 116 us -> 299 us  [the longest x1 135 us: way_in(): pl.pallas_call(functools.partial(front_kernel, chips), out_shape=(jax.Sha...]
    all_gather x5 -> x1, waiting for transfers between devices: 166 us -> 0.01 us  [on_device(): half_cot = lax.all_gather(core_cot, 'tok', axis=0, tiled=False)]
    psum x2 -> x0, blocking collectives: 59.6 us -> none  [the longest x1 39.9 us: on_device(): gain_grad = lax.psum(gain_grad, ('tok', 'ch'))]
    ppermute x4 -> x0, waiting for transfers between devices: 45.3 us -> none  [the longest x1 45.3 us: to_columns(): lax.ppermute(jnp.where(even, dgate, dinner), 'ch', [(b, a) for a, b in se...]
    all_gather x1 -> x0, blocking collectives: 43.8 us -> none  [on_device(): every_label = lax.all_gather(modality, ('tok', 'ch'), axis=0, tiled=True)]
    pallas_call x2 -> x1, Pallas kernels: 94 us -> 59.7 us  [weight_grad(): pl.pallas_call(grad_kernel if block == rows else grad_part_kernel, out_sh...]
    pallas_call x2 -> x1, Pallas kernels: 28.6 us -> 10.4 us  [routed_spread(): pl.pallas_call(functools.partial(spread_kernel, transposed), out_shape=ja...]
    reduce_scatter x1 -> x0, waiting for transfers between devices: 18.1 us -> none  [on_device(): lax.psum_scatter(scaled_part, 'ch', scatter_dimension=0, tiled=True)]
  transfers between devices with their start and end apart: 13 -> 4, of which waited for: 9 -> 0; matrix products, arithmetic and copies ran while one was open for 2% -> 5% of each run, Pallas kernels for 44% -> 63%
where the time goes in v3:
time: 508 us; the launch traced here: 504 us
  Pallas kernels  454 us (89%)
  local copies, waits for them, and re-layouts  29.6 us (6%)
  between operations  14.3 us (3%)
  other arithmetic  5.73 us (1%)
    pallas_call x1, Pallas kernels, way_in(): pl.pallas_call(functools.partial(front_kernel, chips), out_shape=(jax.Sha...  135 us
    pallas_call x1, Pallas kernels, way_back(): pl.pallas_call(functools.partial(back_kernel, chips), out_shape=(jax.Shap...  115 us
    pallas_call x1, Pallas kernels, scan_both(): pl.pallas_call(scan_kernel, out_shape=(jax.ShapeDtypeStruct((rows, channe...  75 us
    pallas_call x1, Pallas kernels, weight_grad(): pl.pallas_call(grad_kernel if block == rows else grad_part_kernel, out_sh...  59.7 us
    pallas_call x1, Pallas kernels, weight_grad_two(): pl.pallas_call(grad_two_kernel, out_shape=jax.ShapeDtypeStruct((mods, dee...  34.9 us
    pallas_call x1, Pallas kernels, sum_over_ch(): pl.pallas_call(functools.partial(sum_kernel, n // 2), out_shape=jax.Shape...  14.3 us
    pallas_call x1, Pallas kernels, routed_spread(): pl.pallas_call(functools.partial(spread_kernel, transposed), out_shape=ja...  10.4 us
    pallas_call x1, Pallas kernels, conv_backward(): pl.pallas_call(conv_back_kernel, out_shape=(jax.ShapeDtypeStruct((rows, c...  10.3 us
  transfers between devices with their start and end apart: 4, of which 0 were waited for; matrix products, arithmetic and copies ran while one was open for 5% of the time, Pallas kernels for 63%

profile of v3, /device:TPU:0, one launch (start us, length us, event | category | flops | bytes accessed | tf_op | source)
XLA Modules:
  0.0 504.5 jit_solution(11394919982979029145)
XLA Ops:
  7.2 0.0 all-gather.6.cloned.1.call-start
  7.2 1.3 broadcast_in_dim.21.cb_ref
  8.5 1.3 broadcast_in_dim.19.gain_ref
  9.8 1.2 broadcast_in_dim.20.label_ref
  11.0 134.9 %way_in.1 = (bf16[4096,2048]{1,0:T(8,128)(2,1)}, bf16[512,2048]{1,0:T(8,128)(2,1)}, bf16[512,2048]{1,0:T(8,128)(2,1)}, s32[4,8,8,128]{3,2,1,0:T(8,128)}, bf16[10...) custom-call(bf16[128,2048]{1,0:T(8,128)(2,1)} %input_ref.3, ...), custom_call_target="tpu_custom_call" | custom-call | flops 99999997952 | bytes 100000000 | tf_op jit(solution)/shard_map/way_in/pallas_call | solution.py:754
  145.9 0.0 all-gather.6.cloned.1.call-update
  145.9 0.0 all-gather.4.cloned.1.call-start
  146.0 0.9 slice.27
  146.9 0.0 copy-start.6
  147.0 0.1 copy.29
  147.1 0.7 reshape_reshape.3.label_row_ref
  147.7 1.0 reshape.63.label_ref
  148.7 0.0 copy-done.12
  148.7 0.6 broadcast_in_dim.22.skip_ref
  149.3 75.0 %scan_both.1 = (bf16[1024,512]{1,0:T(8,128)(2,1)}, bf16[1024,512]{1,0:T(8,128)(2,1)}, f32[1024,512]{1,0:T(8,128)}, f32[160,1024]{1,0:T(8,128)}, f32[3,128,512]{2...) custom-call(f32[1024,512]{1,0:T(8,128)} %get-tuple-element.45.conv_ref, ...), custom_call_target="tpu_custom_call" | custom-call | flops 41943040000 | bytes 10485760 | tf_op jit(solution)/shard_map/scan_both/pallas_call | solution.py:307
  224.4 0.0 all-gather.4.cloned.1.call-update
  224.4 0.2 all-reduce.2.cloned.1.call-start
  224.6 1.1 copy.33.label_ref
  225.7 1.1 copy-done.1
  226.8 14.3 %sum_over_ch.1.dproj_ref = f32[160,1024]{1,0:T(8,128)S(1)} custom-call(f32[160,1024]{1,0:T(8,128)S(1)} %copy-done.1), custom_call_target="tpu_custom_call" | custom-call | tf_op jit(solution)/shard_map/sum_over_ch/pallas_call | solution.py:467
  241.1 0.0 copy-start
  241.1 0.8 copy-done
  241.9 10.3 %conv_backward.1 = (bf16[1024,512]{1,0:T(8,128)(2,1)}, f32[3,160,512]{2,1,0:T(8,128)}, f32[4,512]{1,0:T(4,128)}, f32[1,512]{1,0:T(1,128)}) custom-call(f32[1024,512]{1,0:T(8,128)} %get-tuple-element.45.conv_ref, bf16[1024,512]{1,0:T(8,128)(2,1)} %get-tuple-element.51.inner_ref, f32[1024,512]{1,0:T(8,128)} %get-tuple-element.52.dact_ref, ...), custom_call_target="tpu_custom_call" | custom-call | tf_op jit(solution)/shard_map/conv_backward/pallas_call | solution.py:380
  252.3 0.0 copy-start.4
  252.3 0.0 copy-start.7
  252.3 0.0 copy-start.8
  252.3 0.0 copy-start.10
  252.3 0.0 copy-start.11
  252.4 114.6 %way_back.1 = (bf16[2,4096,512]{2,1,0:T(8,128)(2,1)}, f32[128,2048]{1,0:T(8,128)}, f32[8,256]{1,0:T(8,128)}, bf16[2048,2048]{1,0:T(8,128)(2,1)}) custom-call(bf16[1024,512]{1,0:T(8,128)(2,1)} %get-tuple-element.54.dinner_ref, bf16[1024,512]{1,0:T(8,128)(2,1)} %get-tuple-element.55.dgate_ref, bf16[3,2048,1024]{2,1,0:T(8,128)(2,1)} %w_ref.2, ...), custom_call_target="tpu_custom_call" | custom-call | flops 99999997952 | bytes 100000000 | tf_op jit(solution)/shard_map/way_back/pallas_call | solution.py:965
  367.0 4.9 concatenate.3
  371.9 0.0 all-reduce.2.cloned.1.call-update
  372.0 0.3 reduce-scatter.2.cloned.1.call-start
  372.2 10.4 %routed_spread.1 = bf16[1024,2048]{1,0:T(8,128)(2,1)} custom-call(bf16[1024,512]{1,0:T(8,128)(2,1)} %get-tuple-element.65.x_ref, s32[1024,1]{1,0:T(8,128)} %copy.33.label_ref, bf16[3,512,2048]{2,1,0:T(8,128)(2,1)} %w_ref.3), custom_call_target="tpu_custom_call" | custom-call | flops 6442450944 | bytes 11534336 | tf_op jit(solution)/shard_map/routed_spread/pallas_call | solution.py:108
  382.6 0.0 reduce-scatter.2.cloned.1.call-update
  382.7 0.6 reverse_select_fusion.1
  383.3 2.7 copy.36
  386.0 3.2 reverse_select_fusion
  389.2 1.3 slice.28
  390.4 34.9 %weight_grad_two.1 = f32[3,512,2048]{2,1,0:T(8,128)} custom-call(bf16[4096,512]{1,0:T(8,128)(2,1)} %bitcast.23, bf16[2048,2048]{1,0:T(8,128)(2,1)} %all-gather.6.cloned.1.call-done.half_cot_ref.right_ref, bf16[2048,2048]{1,0:T(8,128)(2,1)} %get-tuple-element.77.other_ref, s32[1,4096]{1,0:T(1,128)} %bitcast.33), custom_call_target="tpu_custom_call" | custom-call | flops 25769803776 | bytes 33554432 | tf_op jit(solution)/shard_map/weight_grad_two/pallas_call | solution.py:1007
  425.4 59.7 %weight_grad.1 = f32[3,2048,1024]{2,1,0:T(8,128)} custom-call(bf16[4096,2048]{1,0:T(8,128)(2,1)} %get-tuple-element.68.left_ref, bf16[2,4096,512]{2,1,0:T(8,128)(2,1)} %get-tuple-element.69.right_ref, s32[1,4096]{1,0:T(1,128)} %bitcast.31), custom_call_target="tpu_custom_call" | custom-call | flops 51539607552 | bytes 50331648 | tf_op jit(solution)/shard_map/weight_grad/pallas_call | solution.py:1051
  485.0 1.4 slice.39
  486.4 1.3 slice.38
  487.8 1.4 slice.41
  489.1 2.1 slice.37
  491.2 2.2 slice.36
  493.4 1.3 fusion
  494.7 2.0 add_convert_fusion
  496.7 1.0 copy.41
  (23 shorter events, 0.1 us)
Async XLA Ops:
  7.2 245.1 %all-gather.6.cloned.1.call-start = ((), (), s32[]{:S(2)}) async-start(), calls=%async_computation.4 | async-start | bytes 10485760 | tf_op jit(solution)/shard_map/all_gather | solution.py:1147
  11.0 137.7 %copy-start.12 = (bf16[512]{0:T(512)(128)(2,1)S(1)}, bf16[512]{0:T(512)(128)(2,1)}, u32[]{:S(2)}) copy-start(bf16[512]{0:T(512)(128)(2,1)} %param.22) | copy-start | bytes 3076
  145.9 237.4 %all-gather.4.cloned.1.call-start = ((), (), s32[]{:S(2)}) async-start(), calls=%async_computation.3 | async-start | bytes 5242880 | tf_op jit(solution)/shard_map/all_gather | solution.py:1201
  146.9 235.8 %copy-start.6 = (s32[4,8,1,128]{3,2,1,0:T(1,128)}, s32[4,8,1,128]{3,2,1,0:T(1,128)S(1)}, u32[]{:S(2)}) copy-start(s32[4,8,1,128]{3,2,1,0:T(1,128)S(1)} %slice.27) | copy-start | bytes 49156
  224.4 260.7 %all-reduce.2.cloned.1.call-start = ((), (), s32[]{:S(2)}) async-start(), calls=%async_computation.2 | async-start | bytes 3670016 | tf_op jit(solution)/shard_map/psum | solution.py:1224
  225.7 1.1 copy-start.1
  241.1 0.8 copy-start
  252.3 114.7 %copy-start.3 = (f32[3,160,512]{2,1,0:T(8,128)S(1)}, f32[3,160,512]{2,1,0:T(8,128)}, u32[]{:S(2)}) copy-start(f32[3,160,512]{2,1,0:T(8,128)} %get-tuple-element.70) | copy-start | bytes 2949124
  252.3 114.7 %copy-start.4 = (f32[3,128,512]{2,1,0:T(8,128)S(1)}, f32[3,128,512]{2,1,0:T(8,128)}, u32[]{:S(2)}) copy-start(f32[3,128,512]{2,1,0:T(8,128)} %get-tuple-element.71) | copy-start | bytes 2359300
  252.3 114.7 %copy-start.7 = (f32[16,512]{1,0:T(8,128)S(1)}, f32[16,512]{1,0:T(8,128)}, u32[]{:S(2)}) copy-start(f32[16,512]{1,0:T(8,128)} %get-tuple-element.75) | copy-start | bytes 98308
  252.3 114.7 %copy-start.8 = (f32[3,512]{1,0:T(4,128)S(1)}, f32[3,512]{1,0:T(4,128)}, u32[]{:S(2)}) copy-start(f32[3,512]{1,0:T(4,128)} %get-tuple-element.72) | copy-start | bytes 18436
  252.3 114.7 %copy-start.9 = (f32[4,512]{1,0:T(4,128)S(1)}, f32[4,512]{1,0:T(4,128)}, u32[]{:S(2)}) copy-start(f32[4,512]{1,0:T(4,128)} %get-tuple-element.73) | copy-start | bytes 24580
  252.3 114.7 %copy-start.10 = (f32[1,512]{1,0:T(1,128)S(1)}, f32[1,512]{1,0:T(1,128)}, u32[]{:S(2)}) copy-start(f32[1,512]{1,0:T(1,128)} %get-tuple-element.76) | copy-start | bytes 6148
  252.3 114.7 %copy-start.11 = (f32[1,512]{1,0:T(1,128)S(1)}, f32[1,512]{1,0:T(1,128)}, u32[]{:S(2)}) copy-start(f32[1,512]{1,0:T(1,128)} %get-tuple-element.74) | copy-start | bytes 6148
  372.0 122.8 %reduce-scatter.2.cloned.1.call-start = ((), (), s32[]{:S(2)}) async-start(), calls=%async_computation.1 | async-start | bytes 4718592 | tf_op jit(solution)/shard_map/reduce_scatter | solution.py:1205
  425.4 69.4 %copy-start.5 = (bf16[128,2048]{1,0:T(8,128)(2,1)S(1)}, bf16[128,2048]{1,0:T(8,128)(2,1)}, u32[]{:S(2)}) copy-start(bf16[128,2048]{1,0:T(8,128)(2,1)} %input_ref.3) | copy-start | bytes 1572868
  485.0 11.7 %copy-start.2 = (f32[128,2048]{1,0:T(8,128)S(1)}, f32[128,2048]{1,0:T(8,128)}, u32[]{:S(2)}) copy-start(f32[128,2048]{1,0:T(8,128)} %get-tuple-element.93) | copy-start | bytes 3145732
Sparse Core Ops, SparseCore 0:
  146.1 86.5 all-gather.5
  235.1 74.3 all-gather.3
  372.1 64.4 all-reduce.1
  438.8 49.9 reduce-scatter.1

commit v4 on v3

--- a/solution.py
+++ b/solution.py
@@ -45,7 +45,7 @@
 
 
 def sigmoid(x):
-    return 1.0 / (1.0 + jnp.exp(-x))
+    return 0.5 * jnp.tanh(0.5 * x) + 0.5
 
 
 def select_kernel(transposed, x_ref, label_ref, w_ref, out_ref):
@@ -169,39 +169,41 @@
 
 
 def scan_kernel(
-    conv_ref, proj_ref, gate_ref, grad_ref, label_ref, label_row_ref, dtw_ref, dtb_ref, alog_ref, skip_ref,
+    conv_ref, proj_ref, gate_ref, grad_ref, label_ref, dtw_ref, dtb_ref, alog_ref, skip_ref,
     gated_ref, dgate_ref, dact_ref, dproj_ref, ddtw_ref, ddtb_ref, dalog_ref, dskip_ref,
-    hist, mix, prod, rate, drate, act, step, slope, dout, scanned, ddrive, dstep, dlow,
+    hist, mix, prod, rate, act, step, slope, dout, scanned, dstep, dlow, low_turned, low_rank, label,
 ):
     rows, width = conv_ref.shape
     length = rows // GROUP
     states = alog_ref.shape[0]
     mods, low_width = dtw_ref.shape[0], dtw_ref.shape[1]
     tile = pl.program_id(0)
-    label = label_ref[...]
+    ddrive = scanned
 
     @pl.when(tile == 0)
     def _():
         prod[...] = jnp.zeros_like(prod)
         dlow[...] = jnp.zeros_like(dlow)
-        high, low = halves(proj_ref[pl.ds(low_width, 2 * states), :])
-        row = lax.broadcasted_iota(jnp.int32, (2 * states, width), 0)
-        for s in range(2 * states):
-            spread = (row == s).astype(BF16)
-            mix[s] = dot_at(high, spread) + dot_at(low, spread)
-
-    low_high, low_low = halves(proj_ref[pl.ds(0, low_width), :])
-    parts = [
-        dot_at(low_high, dtw_ref[m]) + dot_at(low_low, dtw_ref[m]) + dtb_ref[pl.ds(m, 1), :].astype(F32) for m in range(mods)
-    ]
-    speed = pick(parts, label)
+        label[...] = jnp.broadcast_to(label_ref[...], (rows, width))
+        low_rank[...] = proj_ref[pl.ds(0, low_width), :].astype(BF16)
+        low_turned[...] = proj_ref[pl.ds(0, low_width), :].T.astype(BF16)
+        turned = proj_ref[pl.ds(low_width, 2 * states), :].T.astype(BF16)
+        row = lax.broadcasted_iota(jnp.int32, (2 * states, 2 * width), 0)
+        column = lax.broadcasted_iota(jnp.int32, (2 * states, 2 * width), 1)
+        for s in range(0, 2 * states, 2):
+            spread = dot(turned, (row == s + (column >= width).astype(jnp.int32)).astype(BF16))
+            mix[s] = spread[:, :width]
+            mix[s + 1] = spread[:, width:]
+
+    kind = label[...]
+    parts = [dot(low_turned[...], dtw_ref[m]) + dtb_ref[pl.ds(m, 1), :].astype(F32) for m in range(mods)]
+    speed = pick(parts, kind)
     step[...] = jnp.maximum(speed, 0.0) + jnp.log1p(jnp.exp(-jnp.abs(speed)))
     slope[...] = sigmoid(speed)
     conv = conv_ref[...]
     act[...] = conv * sigmoid(conv)
     for s in range(states):
         rate[s] = jnp.broadcast_to(-LOG2E * jnp.exp(alog_ref[pl.ds(s, 1), :].astype(F32)), (GROUP, width))
-        drate[s] = jnp.zeros((GROUP, width), F32)
         hist[0, s] = jnp.zeros((GROUP, width), F32)
 
     def forward(t, state):
@@ -220,7 +222,7 @@
         return tuple(new)
 
     zero = jnp.zeros((GROUP, width), F32)
-    lax.fori_loop(0, length, forward, (zero,) * states)
+    lax.fori_loop(0, length, forward, (zero,) * states, unroll=8)
 
     gate = by_time(gate_ref[...])
     grad = by_time(grad_ref[...])
@@ -242,7 +244,7 @@
         drive = now * act[at, :]
         out = dout[at, :]
         dd, ds = None, None
-        new = []
+        new, drates = [], []
         for s in range(states):
             decay = jnp.exp2(now * rate[s])
             dstate = carry[s] + mix[states + s, at, :] * out
@@ -255,25 +257,24 @@
             change = passed * hist[t, s]
             term = change * rate[s]
             ds = term if ds is None else ds + term
-            drate[s] += change * now
+            drates.append(carry[states + s] + change * now)
         ddrive[at, :] = dd
         dstep[at, :] = ds
-        return tuple(new)
-
-    lax.fori_loop(0, length, backward, (zero,) * states)
+        return tuple(new + drates)
+
+    final = lax.fori_loop(0, length, backward, (zero,) * (2 * states), unroll=4)
 
     for s in range(states):
-        dalog_ref[pl.ds(s, 1), :] = LN2 * jnp.sum(drate[s] * rate[s], axis=0, keepdims=True)
+        dalog_ref[pl.ds(s, 1), :] = LN2 * jnp.sum(final[states + s] * rate[s], axis=0, keepdims=True)
     dact_ref[...] = ddrive[...] * step[...] + skip * dout[...]
     dspeed = (dstep[...] * LN2 + ddrive[...] * act[...]) * slope[...]
-    high, low = halves(dspeed)
-    parts = [dot_bt(dtw_ref[m], high) + dot_bt(dtw_ref[m], low) for m in range(mods)]
-    dlow[...] += pick(parts, label_row_ref[...])
+    rounded = dspeed.astype(BF16)
+    of_rank = kind if width == low_width else label_ref[...]
+    dlow[...] += pick([dot_bt(rounded, dtw_ref[m]) for m in range(mods)], of_rank)
     for m in range(mods):
-        own = label == m
+        own = kind == m
         masked = jnp.where(own, dspeed, 0.0)
-        high, low = halves(masked)
-        ddtw_ref[m] = dot(low_high, high) + dot(low_high, low) + dot(low_low, high)
+        ddtw_ref[m] = dot(low_rank[...], masked.astype(BF16))
         ddtb_ref[pl.ds(m, 1), :] = jnp.sum(masked, axis=0, keepdims=True)
 
     @pl.when(tile == pl.num_programs(0) - 1)
@@ -281,14 +282,12 @@
         column = lax.broadcasted_iota(jnp.int32, (width, 2 * states), 1)
         sums = jnp.zeros((rows, 2 * states), F32)
         for s in range(2 * states):
-            gather = (column == s).astype(BF16)
-            high, low = halves(prod[s])
-            sums = sums + (dot(high, gather) + dot(low, gather))
-        dproj_ref[pl.ds(0, low_width), :] = dlow[...]
+            sums = sums + dot(prod[s].astype(BF16), (column == s).astype(BF16))
+        dproj_ref[pl.ds(0, low_width), :] = dlow[...].T
         dproj_ref[pl.ds(low_width, 2 * states), :] = sums.T
 
 
-def scan_both(conv, proj, gate, grad, label, label_row, dtw, dtb, alog, skip):
+def scan_both(conv, proj, gate, grad, label, dtw, dtb, alog, skip):
     rows, channels = conv.shape
     width = min(128, channels)
     length = rows // GROUP
@@ -318,7 +317,7 @@
         ),
         grid=(channels // width,),
         in_specs=[
-            cut(rows), whole((wide, rows)), cut(rows), cut(rows), whole((rows, 1)), whole((1, rows)),
+            cut(rows), whole((wide, rows)), cut(rows), cut(rows), whole((rows, 1)),
             cut(mods, low_width), cut(mods), cut(states), cut(1),
         ],
         out_specs=(
@@ -329,14 +328,16 @@
             pltpu.VMEM((2 * states, rows, width), F32),
             pltpu.VMEM((2 * states, rows, width), F32),
             pltpu.VMEM((states,) + plane, F32),
-            pltpu.VMEM((states,) + plane, F32),
-            flat, flat, flat, flat, flat, flat, flat,
-            pltpu.VMEM((low_width, rows), F32),
+            flat, flat, flat, flat, flat, flat,
+            pltpu.VMEM((rows, low_width), F32),
+            pltpu.VMEM((rows, low_width), BF16),
+            pltpu.VMEM((low_width, rows), BF16),
+            pltpu.VMEM((rows, width), jnp.int32),
         ],
         compiler_params=params(),
         cost_estimate=pl.CostEstimate(flops=5000 * rows * channels * states, bytes_accessed=20 * rows * channels, transcendentals=0),
         name="scan_both",
-    )(conv, proj, gate, grad, label, label_row, dtw, dtb, alog, skip[None, :])
+    )(conv, proj, gate, grad, label, dtw, dtb, alog, skip[None, :])
 
 
 def conv_back_kernel(
@@ -351,13 +352,12 @@
     soft = sigmoid(conv)
     act = conv * soft
     dproj = dproj_ref[...]
-    high, low = halves(dproj)
-    parts = [dot_at(high, xw_ref[m]) + dot_at(low, xw_ref[m]) for m in range(xw_ref.shape[0])]
+    turned = dproj.T.astype(BF16)
+    parts = [dot(turned, xw_ref[m]) for m in range(xw_ref.shape[0])]
     dact = dact_ref[...] + pick(parts, label)
-    act_high, act_low = halves(act)
+    rounded = act.astype(BF16)
     for m in range(xw_ref.shape[0]):
-        high, low = halves(jnp.where(label_row == m, dproj, 0.0))
-        dxw_ref[m] = dot(high, act_high) + dot(low, act_high) + dot(high, act_low)
+        dxw_ref[m] = dot(jnp.where(label_row == m, dproj, 0.0).astype(BF16), rounded)
     dconv = dact * (soft + act * (1.0 - soft))
     dcb_ref[...] = jnp.sum(dconv, axis=0, keepdims=True)
     pad_ref[pl.ds(0, rows), :] = dconv
@@ -394,7 +394,10 @@
 MESH = pl.DeviceIdType.MESH
 
 
-def sum_body(chips, x_ref, out_ref, near, mine, far, total, every, other, near_sems, far_sems, back_sems, other_sems):
+def sum_body(
+    chips, x_ref, out_ref, near, mine, far, total, every, other, near_sems, far_sems, back_sems, other_sems,
+    work=lambda i: None,
+):
     wide, rows = x_ref.shape
     half, part = rows // 2, rows // 2 // chips
     tok, ch = lax.axis_index("tok"), lax.axis_index("ch")
@@ -413,12 +416,15 @@
         return pl.ds(pl.multiple_of(index * size, size), size)
 
     copy = send(x_ref.at[:, columns(1 - core, half)], near, near_sems, partner)
+    work(0)
     copy.wait()
     mine[...] = (x_ref[:, columns(core, half)] + near[...]).astype(BF16)
     copies = [
         send(mine.at[:, columns(chip ^ d, part)], far.at[d - 1], far_sems.at[d - 1], chips_away[d - 1])
         for d in range(1, chips)
     ]
+    work(1)
+    work(2)
     value = mine[:, columns(chip, part)].astype(F32)
     for d, copy in enumerate(copies):
         copy.wait()
@@ -427,6 +433,7 @@
     copies = [send(total, every.at[d - 1], back_sems.at[d - 1], chips_away[d - 1]) for d in range(1, chips)]
     copies += [send(total, other.at[0], other_sems.at[0], partner)]
     out_ref[:, columns(core * chips + chip, part)] = total[...].astype(F32)
+    work(3)
     for d in range(1, chips):
         copies[d - 1].wait()
         copies += [send(every.at[d - 1], other.at[d], other_sems.at[d], partner)]
@@ -434,15 +441,6 @@
     for d in range(chips):
         copies[chips - 1 + d].wait()
         out_ref[:, columns((1 - core) * chips + (chip ^ d), part)] = other[d].astype(F32)
-
-
-def sum_kernel(chips, *refs):
-    tok, ch = lax.axis_index("tok"), lax.axis_index("ch")
-    barrier = pltpu.get_barrier_semaphore()
-    for device in [(tok, ch ^ 1)] + [(tok, ch ^ (2 * d)) for d in range(1, chips)]:
-        pl.semaphore_signal(barrier, inc=1, device_id=device, device_id_type=MESH)
-    pl.semaphore_wait(barrier, chips)
-    sum_body(chips, *refs)
 
 
 def sum_scratch(wide, rows, chips):
@@ -462,26 +460,103 @@
     ]
 
 
-def sum_over_ch(x, n, collective_id):
-    wide, rows = x.shape
+def middle_kernel(
+    chips, dproj_part_ref, gated_ref, label_seq_ref, ow_ref, conv_ref, inner_ref, dact_ref, label_ref, label_row_ref, cw_ref, xw_ref,
+    branch_ref, every_gated_ref, dinner_ref, dxw_ref, dcw_ref, dcb_ref,
+    weights, dproj, pad, w_sem, own_sem, tok_send, tok_recv, *sum_refs,
+):
+    group = gated_ref.shape[0]
+    deep = ow_ref.shape[2]
+    tok, ch = lax.axis_index("tok"), lax.axis_index("ch")
+    fetch = pltpu.make_async_copy(ow_ref, weights, w_sem)
+    fetch.start()
+
+    def rows_of(index):
+        return pl.ds(pl.multiple_of(index * group, group), group)
+
+    own = pltpu.make_async_copy(gated_ref, every_gated_ref.at[rows_of(tok)], own_sem)
+    own.start()
+    barrier = pltpu.get_barrier_semaphore()
+    peers = [(tok, ch ^ 1)] + [(tok, ch ^ (2 * d)) for d in range(1, chips)] + [(tok ^ g, ch) for g in (1, 2)]
+    for device in peers:
+        pl.semaphore_signal(barrier, inc=1, device_id=device, device_id_type=MESH)
+    pl.semaphore_wait(barrier, len(peers))
+    copies = [
+        pltpu.make_async_remote_copy(
+            src_ref=gated_ref,
+            dst_ref=every_gated_ref.at[rows_of(tok)],
+            send_sem=tok_send.at[side],
+            recv_sem=tok_recv.at[side],
+            device_id=(tok ^ (1 + side), ch),
+            device_id_type=MESH,
+        )
+        for side in range(2)
+    ]
+    for copy in copies:
+        copy.start()
+    wide = deep // 4
+
+    def work(i):
+        if i == 0:
+            fetch.wait()
+        x, label = gated_ref[...], label_seq_ref[...]
+        total = None
+        for m in range(ow_ref.shape[0]):
+            part = dot(jnp.where(label == m, x, jnp.zeros_like(x)), weights[m, :, pl.ds(i * wide, wide)])
+            total = part if total is None else total + part
+        branch_ref[:, pl.ds(i * wide, wide)] = total.astype(BF16)
+
+    sum_body(chips, dproj_part_ref, dproj, *sum_refs, work=work)
+    conv_back_kernel(
+        conv_ref, inner_ref, dact_ref, dproj, label_ref, label_row_ref, cw_ref, xw_ref,
+        dinner_ref, dxw_ref, dcw_ref, dcb_ref, pad,
+    )
+    for side in range(2):
+        whole = every_gated_ref.at[rows_of(tok ^ (1 + side))]
+        pltpu.make_async_copy(whole, whole, tok_recv.at[side]).wait()
+        copies[side].wait_send()
+    own.wait()
+
+
+def middle(dproj_part, gated, label_seq, ow, conv, inner, dact, label, label_row, cw, xw, n, collective_id):
+    group, channels = conv.shape
+    mods, wide = xw.shape[0], xw.shape[1]
+    taps, deep = cw.shape[0], ow.shape[2]
+    dma = pltpu.SemaphoreType.DMA
+    vmem = pl.BlockSpec(memory_space=pltpu.VMEM)
+    any_space = pl.BlockSpec(memory_space=pl.ANY)
     return pl.pallas_call(
-        functools.partial(sum_kernel, n // 2),
-        out_shape=jax.ShapeDtypeStruct((wide, rows), F32),
-        in_specs=[pl.BlockSpec(memory_space=pltpu.VMEM)],
-        out_specs=pl.BlockSpec(memory_space=pltpu.VMEM),
-        scratch_shapes=sum_scratch(wide, rows, n // 2),
-        compiler_params=pltpu.CompilerParams(collective_id=collective_id, has_side_effects=True, vmem_limit_bytes=16 << 20),
-        name="sum_over_ch",
-    )(x)
+        functools.partial(middle_kernel, n // 2),
+        out_shape=(
+            jax.ShapeDtypeStruct((group, deep), BF16),
+            jax.ShapeDtypeStruct((4 * group, channels), BF16),
+            jax.ShapeDtypeStruct((group, channels), BF16),
+            jax.ShapeDtypeStruct((mods, wide, channels), F32),
+            jax.ShapeDtypeStruct((taps, channels), F32),
+            jax.ShapeDtypeStruct((1, channels), F32),
+        ),
+        in_specs=[vmem, vmem, vmem, any_space] + [vmem] * 7,
+        out_specs=(vmem, any_space, vmem, vmem, vmem, vmem),
+        scratch_shapes=[
+            pltpu.VMEM(ow.shape, BF16),
+            pltpu.VMEM((wide, group), F32),
+            pltpu.VMEM((group + (taps - 1) * GROUP, channels), F32),
+            dma, dma, dma((2,)), dma((2,)),
+        ] + sum_scratch(wide, group, n // 2),
+        compiler_params=params(collective_id=collective_id, has_side_effects=True),
+        cost_estimate=pl.CostEstimate(flops=2 * 10**10, bytes_accessed=10**7, transcendentals=0),
+        name="middle",
+    )(dproj_part, gated, label_seq, ow, conv, inner, dact, label, label_row, cw, xw)
 
 
 def front_kernel(
     chips, input_ref, gain_ref, cot_ref, label_ref, iw_ref, ow_ref, cw_ref, cb_ref, xw_ref,
-    scaled_ref, core_cot_ref, near_cot_ref, labels_ref, gate_ref, gated_grad_ref, conv_ref, inner_out_ref, proj_ref,
+    scaled_ref, core_cot_ref, near_cot_ref, pair_cot_ref, labels_ref, gate_ref, gated_grad_ref, conv_ref, inner_out_ref, proj_ref,
     own_rows, in_w, out_w, chunk_rows, staged, xz, proj_part, pad,
     in_sem, out_sem, load_sem, own_sem,
     line_send, line_recv, near_send, near_recv, tok_send, tok_recv, diag_send, diag_recv,
-    xz_send, xz_recv, lab_send, lab_recv, lab_tok_send, lab_tok_recv, *sum_refs,
+    xz_send, xz_recv, lab_send, lab_recv, lab_tok_send, lab_tok_recv,
+    keep_sem, pair_send, pair_recv, pair_diag_send, pair_diag_recv, *sum_refs,
 ):
     n = 2 * chips
     length, deep = input_ref.shape
@@ -571,9 +646,27 @@
             for side in range(2):
                 tok_copy(o, side).start()
 
+    base = chip - chip % 2
+
+    def pair_copy(i, side):
+        src, dst = from_line(1, base + i), pair_cot_ref.at[tok, i]
+        return remote(src, dst, pair_send.at[side, i], pair_recv.at[side, i], (tok ^ (1 + side), ch))
+
+    def pair_diag(i, side):
+        ref = pair_cot_ref.at[tok ^ (1 + side), i, pl.ds(side * (length // 2), length // 2)]
+        return remote(ref, ref, pair_diag_send.at[side, i], pair_diag_recv.at[side, i], (tok ^ (2 - side), ch))
+
+    def pair_pass(i):
+        for side in range(2):
+            arrive(pair_cot_ref.at[tok ^ (1 + side), i], pair_recv.at[side, i])
+            pair_diag(i, side).start()
+
     def accept(x, o):
         arrive(from_line(x, o), line_recv.at[x, o])
         launch(x, o)
+        if x == 1:
+            for side in range(2):
+                pl.when(o // 2 == chip // 2)(pair_copy(o % 2, side).start)
 
     def pass_on(o):
         for side in range(2):
@@ -639,6 +732,13 @@
         parts = [dot_bt(x, out_w[m]) for m in range(mods)]
         gated_grad_ref[pl.ds(pl.multiple_of(o * chunk, chunk), chunk), :] = pick(parts, label).astype(BF16)
 
+        @pl.when(o // 2 == chip // 2)
+        def _():
+            mine = chunk_rows.at[pl.ds(pl.multiple_of(core * length, length), length)]
+            copy = pltpu.make_async_copy(mine, pair_cot_ref.at[tok, o % 2], keep_sem)
+            copy.start()
+            copy.wait()
+
     def both_sides(i, fn):
         for o in (chip - i, chip + i):
             pl.when((o >= 0) & (o < chips))(functools.partial(fn, o))
@@ -669,6 +769,8 @@
     lax.fori_loop(1, chips, step, 0)
     own[1].wait()
     launch(1, chip)
+    for side in range(2):
+        pair_copy(chip % 2, side).start()
     label_tok = [
         remote(labels_ref.at[tok], labels_ref.at[tok], lab_tok_send.at[g - 1], lab_tok_recv.at[g - 1], (tok ^ g, ch))
         for g in range(1, 4)
@@ -686,6 +788,7 @@
 
     lax.fori_loop(1, chips - 1, step_back, 0)
     every_distance(pass_last)
+    pair_pass(chip % 2)
 
     for o in range(chips):
         for a in range(2):
@@ -714,6 +817,7 @@
     proj_part[...] = total
 
     both_sides(chips - 1, functools.partial(accept, 1))
+    pair_pass(1 - chip % 2)
     sum_body(chips, proj_part, proj_ref, *sum_refs)
     both_sides(chips - 1, project_back)
 
@@ -731,6 +835,12 @@
         return carry
 
     lax.fori_loop(0, chips, finish, 0)
+    for i in range(2):
+        for side in range(2):
+            pair_copy(i, side).wait_send()
+            pair_diag(i, side).wait_send()
+            part = pair_cot_ref.at[tok ^ 3, i, pl.ds(side * (length // 2), length // 2)]
+            arrive(part, pair_diag_recv.at[side, i])
     for o in range(chips):
         for h in range(2):
             target, copy, _ = xz_copies(o, h)
@@ -757,6 +867,7 @@
             jax.ShapeDtypeStruct((4 * group, deep), BF16),
             jax.ShapeDtypeStruct((chips * length, deep), BF16),
             jax.ShapeDtypeStruct((chips * length, deep), BF16),
+            jax.ShapeDtypeStruct((4, 2, length, deep), BF16),
             jax.ShapeDtypeStruct((4, n, 8, length), jnp.int32),
             jax.ShapeDtypeStruct((group, width), BF16),
             jax.ShapeDtypeStruct((group, width), BF16),
@@ -765,7 +876,7 @@
             jax.ShapeDtypeStruct((wide, group), F32),
         ),
         in_specs=[vmem, vmem, any_space, vmem, any_space, any_space, vmem, vmem, vmem],
-        out_specs=(any_space, any_space, any_space, vmem, vmem, vmem, vmem, vmem, vmem),
+        out_specs=(any_space, any_space, any_space, any_space, vmem, vmem, vmem, vmem, vmem, vmem),
         scratch_shapes=[
             pltpu.VMEM((length, deep), BF16),
             pltpu.VMEM(in_weight.shape, BF16),
@@ -779,6 +890,7 @@
             dma((2, 2, chips)), dma((2, chips)), dma((2, 4, chips)), dma((2, 4, chips)),
             dma((2, chips)), dma((2, chips)), dma((2, chips)), dma((2, chips)),
             dma((chips, 2)), dma((2, chips)), dma((n - 1,)), dma((n - 1,)), dma((3,)), dma((3,)),
+            dma, dma((2, 2)), dma((2, 2)), dma((2, 2)), dma((2, 2)),
         ] + sum_scratch(wide, group, chips),
         compiler_params=params(collective_id=collective_id, has_side_effects=True),
         cost_estimate=pl.CostEstimate(flops=10**11, bytes_accessed=10**8, transcendentals=0),
@@ -789,11 +901,23 @@
     )
 
 
+def small_places(values):
+    start, places = 0, []
+    for value in values:
+        for m in range(value.shape[0]) if len(value.shape) == 3 else [None]:
+            places.append((start, (value, m)))
+            start += -(-value.shape[-2] // 8) * 8
+    return places
+
+
 def back_kernel(
-    chips, dinner_ref, dgate_ref, w_ref, label_ref, input_ref, cot_ref, gain_ref, half_cot_ref,
-    xall_ref, row_grad_ref, gain_sum_ref, near_cot_ref,
-    weights, sends, near_part, chip_sums, arrived, mine, gain_send, gain_arrived, gain_mine, gain_others,
-    w_sem, to_col, from_own, to_tok, from_tok, to_diag, from_diag, to_near, from_near, to_row, from_row, to_gain, from_gain, to_gain_tok, from_gain_tok, cot_sems,
+    chips, dinner_ref, dgate_ref, w_ref, label_ref, input_ref, cot_ref, gain_ref, pair_cot_ref, rest_cot_ref, scaled_ref, label_row_ref, every_gated_ref,
+    dxw_ref, ddtw_ref, ddtb_ref, dcw_ref, dcb_ref, dalog_ref, dskip_ref,
+    xall_ref, row_grad_ref, gain_sum_ref, near_pair_ref, near_rest_ref, grad_part_ref, small_ref, diag_gated_ref,
+    weights, sends, near_part, chip_sums, arrived, mine, gain_send, gain_arrived, gain_mine, gain_others, left, made,
+    packed, rounded, small_in, small_all,
+    w_sem, to_col, from_own, to_tok, from_tok, to_diag, from_diag, to_near, from_near, to_row, from_row, to_gain, from_gain, to_gain_tok, from_gain_tok, cot_sems, left_sems, made_sems, to_small, from_small, to_all, from_all,
+    to_gated_diag, from_gated_diag,
 ):
     n = 2 * chips
     group, width = dinner_ref.shape
@@ -807,6 +931,52 @@
     fetch = pltpu.make_async_copy(w_ref, weights, w_sem)
     fetch.start()
 
+    first = tok - tok % 2
+    tile_rows = left.shape[3]
+    tiles = deep // tile_rows
+
+    def left_copies(i):
+        at = pl.ds(pl.multiple_of(i * tile_rows, tile_rows), tile_rows)
+        return [
+            pltpu.make_async_copy(
+                scaled_ref.at[pl.ds(pl.multiple_of((first + g) * group, group), group), at],
+                left.at[lax.rem(i, 2), g],
+                left_sems.at[lax.rem(i, 2), g],
+            )
+            for g in range(2)
+        ]
+
+    def made_copy(i):
+        at = pl.ds(pl.multiple_of(i * tile_rows, tile_rows), tile_rows)
+        return pltpu.make_async_copy(made.at[lax.rem(i, 2)], grad_part_ref.at[:, at], made_sems.at[lax.rem(i, 2)])
+
+    def grad_tile(i, carry):
+        for copy in left_copies(i):
+            copy.wait()
+        pl.when(i >= 2)(made_copy(i - 2).wait)
+        slot = lax.rem(i, 2)
+        lanes = [pl.ds(pl.multiple_of((first + g) * group, group), group) for g in range(2)]
+        turned = [left[slot, g].T for g in range(2)]
+        for m in range(mods):
+            masked = [
+                jnp.where(label_row_ref[:, lanes[g]] == m, turned[g], jnp.zeros_like(turned[g])) for g in range(2)
+            ]
+            for h in range(2):
+                total = dot(masked[0], xall_ref[h, lanes[0], :]) + dot(masked[1], xall_ref[h, lanes[1], :])
+                made[slot, m, :, pl.ds(h * width, width)] = total
+        made_copy(i).start()
+
+        @pl.when(i + 2 < tiles)
+        def _():
+            for copy in left_copies(i + 2):
+                copy.start()
+
+        return carry
+
+    for i in range(2):
+        for copy in left_copies(i):
+            copy.start()
+
     barrier = pltpu.get_barrier_semaphore()
     peers = [(tok, ch ^ e) for e in range(1, n)] + [(tok ^ g, ch) for g in range(1, 4)]
     for device in peers:
@@ -824,7 +994,10 @@
     def all_rows(group_index, chunk_index):
         return pl.ds(pl.multiple_of(group_index * group + chunk_index * chunk, chunk), chunk)
 
-    cot_near = remote(half_cot_ref, near_cot_ref, cot_sems.at[0], cot_sems.at[1], (tok, ch ^ 1))
+    cot_copies = [
+        remote(src, dst, cot_sems.at[i, 0], cot_sems.at[i, 1], (tok, ch ^ 1))
+        for i, (src, dst) in enumerate(((pair_cot_ref, near_pair_ref), (rest_cot_ref, near_rest_ref)))
+    ]
 
     order = [2, 3, 1, 0]
     owners = [ch // 2, chips + ch // 2]
@@ -844,8 +1017,25 @@
 
     give(order[0])
     give(order[1])
+    half = group // 2
+    gated_copies = []
+    for side, (source, target) in enumerate(((beside, below), (below, beside))):
+        src = every_gated_ref.at[rows_of(2 * source + side, half)]
+        dst = diag_gated_ref.at[pl.ds(side * half, half)]
+        copy = remote(src, dst, to_gated_diag.at[side], from_gated_diag.at[side], (target, ch))
+        copy.start()
+        gated_copies.append(copy)
+    quarter = rounded.shape[0] // 4
+    packed[...] = jnp.zeros_like(packed)
+    for start, (ref, m) in small_places(
+        (dxw_ref, ddtw_ref, ddtb_ref, dcw_ref, dcb_ref, dalog_ref, dskip_ref)
+    ):
+        value = ref[...] if m is None else ref[m]
+        packed[pl.ds(start, value.shape[0]), :] = value
+    rounded[...] = packed[...].astype(BF16)
     fetch.wait()
-    cot_near.start()
+    for copy in cot_copies:
+        copy.start()
     tok_copies, row_copies, diag_copies, near_copies = [], [], [], []
 
     def pass_on(j):
@@ -903,12 +1093,37 @@
         )
         copy.start()
         near_copies.append(copy)
-        if at >= 1:
-            pass_on(order[at - 1])
-            both_cores(order[at - 1])
-    pass_on(order[-1])
-    both_cores(order[-1])
-
+    for j in order:
+        both_cores(j)
+    for j in order:
+        pass_on(j)
+    small_copies = [
+        remote(
+            rounded.at[rows_of(tok ^ g, quarter)],
+            small_in.at[g - 1],
+            to_small.at[g - 1],
+            from_small.at[g - 1],
+            (tok ^ g, ch),
+        )
+        for g in range(1, 4)
+    ]
+    for copy in small_copies:
+        copy.start()
+
+    lax.fori_loop(0, tiles - 4, grad_tile, 0)
+    value = packed[rows_of(tok, quarter), :]
+    for copy in small_copies:
+        copy.wait()
+    for g in range(3):
+        value = value + small_in[g].astype(F32)
+    small_all[tok] = value.astype(BF16)
+    small_copies = [
+        remote(small_all.at[tok], small_all.at[tok], to_all.at[g - 1], from_all.at[g - 1], (tok ^ g, ch))
+        for g in range(1, 4)
+    ]
+    for copy in small_copies:
+        copy.start()
+    lax.fori_loop(tiles - 4, tiles - 2, grad_tile, 0)
     total = mine[...]
     for e in range(chips - 1):
         pltpu.make_async_copy(arrived.at[e], arrived.at[e], from_row.at[e]).wait()
@@ -929,6 +1144,7 @@
         copy = remote(gain_send.at[ch ^ e], gain_arrived.at[e - 1], to_gain.at[e - 1], from_gain.at[e - 1], (tok, ch ^ e))
         copy.start()
         gain_copies.append(copy)
+    grad_tile(tiles - 2, 0)
     value = gain_send[ch]
     for e in range(1, n):
         gain_copies[e - 1].wait()
@@ -939,6 +1155,7 @@
         copy = remote(gain_mine, gain_others.at[g - 1], to_gain_tok.at[g - 1], from_gain_tok.at[g - 1], (tok ^ g, ch))
         copy.start()
         gain_copies.append(copy)
+    grad_tile(tiles - 1, 0)
     for copy in gain_copies:
         copy.wait()
     even, odd = gain_mine[...] + gain_others[0], gain_others[1] + gain_others[2]
@@ -952,15 +1169,30 @@
         pl.when(owner != ch)(copy.wait_send)
     for copy in tok_copies + diag_copies + row_copies + near_copies:
         copy.wait_send()
-    cot_near.wait()
-
-
-def way_back(dinner, dgate, w, label, block_input, cotangent, gain, half_cot, n, collective_id):
+    for copy in cot_copies:
+        copy.wait()
+    for copy in gated_copies:
+        copy.wait()
+    for g in range(1, 4):
+        pltpu.make_async_copy(small_all.at[tok ^ g], small_all.at[tok ^ g], from_all.at[g - 1]).wait()
+        small_copies[g - 1].wait_send()
+    for g in range(4):
+        small_ref[pl.ds(g * quarter, quarter), :] = small_all[g].astype(F32)
+    for i in (tiles - 2, tiles - 1):
+        made_copy(i).wait()
+
+
+def way_back(
+    dinner, dgate, w, label, block_input, cotangent, gain, pair_cot, rest_cot, every_scaled, every_label, every_gated, small, n, collective_id
+):
     group, width = dinner.shape
     mods, deep, _ = w.shape
     chips, length = n // 2, group // n
     dma = pltpu.SemaphoreType.DMA
     vmem = pl.BlockSpec(memory_space=pltpu.VMEM)
+    tile = min(256, deep)
+    last, (value, _) = small_places(small)[-1]
+    quarter = -(-(last + value.shape[-2]) // 64) * 16
     any_space = pl.BlockSpec(memory_space=pl.ANY)
     return pl.pallas_call(
         functools.partial(back_kernel, chips),
@@ -968,10 +1200,15 @@
             jax.ShapeDtypeStruct((2, 4 * group, width), BF16),
             jax.ShapeDtypeStruct((length, deep), F32),
             jax.ShapeDtypeStruct((8, deep // n), F32),
-            jax.ShapeDtypeStruct(half_cot.shape, BF16),
+            jax.ShapeDtypeStruct(pair_cot.shape, BF16),
+            jax.ShapeDtypeStruct(rest_cot.shape, BF16),
+            jax.ShapeDtypeStruct(w.shape, F32),
+            jax.ShapeDtypeStruct((4 * quarter, width), F32),
+            jax.ShapeDtypeStruct((group, width), BF16),
         ),
-        in_specs=[vmem, vmem, any_space, vmem, vmem, vmem, vmem, any_space],
-        out_specs=(vmem, vmem, vmem, any_space),
+        in_specs=[vmem, vmem, any_space, vmem, vmem, vmem, vmem, any_space, any_space, any_space, vmem, any_space]
+        + [vmem] * len(small),
+        out_specs=(vmem, vmem, vmem, any_space, any_space, any_space, vmem, any_space),
         scratch_shapes=[
             pltpu.VMEM(w.shape, BF16),
             pltpu.VMEM((chips, 2 * length, deep), BF16),
@@ -983,32 +1220,46 @@
             pltpu.VMEM((n - 1, 8, deep // n), F32),
             pltpu.VMEM((8, deep // n), F32),
             pltpu.VMEM((3, 8, deep // n), F32),
+            pltpu.VMEM((2, 2, group, tile), BF16),
+            pltpu.VMEM((2, mods, tile, 2 * width), F32),
+            pltpu.VMEM((4 * quarter, width), F32),
+            pltpu.VMEM((4 * quarter, width), BF16),
+            pltpu.VMEM((3, quarter, width), BF16),
+            pltpu.VMEM((4, quarter, width), BF16),
             dma, dma((chips, 2)), dma((chips, 2)), dma((2, chips)), dma((2, chips)), dma((2, chips)), dma((2, chips)),
-            dma((chips,)), dma((chips,)), dma((chips - 1,)), dma((chips - 1,)), dma((n - 1,)), dma((n - 1,)), dma((3,)), dma((3,)), dma((2,)),
+            dma((chips,)), dma((chips,)), dma((chips - 1,)), dma((chips - 1,)), dma((n - 1,)), dma((n - 1,)), dma((3,)), dma((3,)), dma((2, 2)), dma((2, 2)), dma((2,)),
+            dma((3,)), dma((3,)), dma((3,)), dma((3,)),
+            dma((2,)), dma((2,)),
         ],
         compiler_params=params(collective_id=collective_id, has_side_effects=True),
         cost_estimate=pl.CostEstimate(flops=10**11, bytes_accessed=10**8, transcendentals=0),
         name="way_back",
-    )(dinner, dgate, w, label, block_input, cotangent, gain[None, :], half_cot)
-
-
-def grad_two_kernel(left_ref, right_ref, other_ref, label_ref, out_ref):
-    half = right_ref.shape[0]
+    )(dinner, dgate, w, label, block_input, cotangent, gain[None, :], pair_cot, rest_cot, every_scaled, every_label, every_gated, *small)
+
+
+def grad_parts_kernel(left_ref, label_ref, *refs):
+    right_refs, out_ref = refs[:-1], refs[-1]
+    size = right_refs[0].shape[0]
     turned, label = left_ref[...].T, label_ref[...]
     for m in range(out_ref.shape[0]):
         masked = jnp.where(label == m, turned, jnp.zeros_like(turned))
-        out_ref[m] = dot(masked[:, :half], right_ref[...]) + dot(masked[:, half:], other_ref[...])
-
-
-def weight_grad_two(left, right, other, label, mods, tile):
+        total = None
+        for i, right_ref in enumerate(right_refs):
+            part = dot(masked[:, i * size : (i + 1) * size], right_ref[...])
+            total = part if total is None else total + part
+        out_ref[m] = total
+
+
+def weight_grad_parts(left, rights, label, mods, tile):
     rows, deep = left.shape
-    half, wide = right.shape
-    whole = pl.BlockSpec((half, wide), lambda i: (0, 0), pipeline_mode=pl.Buffered(1))
+    size, wide = rights[0].shape
+    whole = pl.BlockSpec((size, wide), lambda i: (0, 0), pipeline_mode=pl.Buffered(1))
     return pl.pallas_call(
-        grad_two_kernel,
+        grad_parts_kernel,
         out_shape=jax.ShapeDtypeStruct((mods, deep, wide), F32),
         grid=(deep // tile,),
-        in_specs=[pl.BlockSpec((rows, tile), lambda i: (0, i)), whole, whole, pl.BlockSpec((1, rows), lambda i: (0, 0))],
+        in_specs=[pl.BlockSpec((rows, tile), lambda i: (0, i)), pl.BlockSpec((1, rows), lambda i: (0, 0))]
+        + [whole] * len(rights),
         out_specs=pl.BlockSpec((mods, tile, wide), lambda i: (0, i, 0)),
         compiler_params=params(),
         cost_estimate=pl.CostEstimate(
@@ -1016,8 +1267,53 @@
             bytes_accessed=2 * rows * (deep + wide) + 4 * mods * deep * wide,
             transcendentals=0,
         ),
-        name="weight_grad_two",
-    )(left, right, other, label)
+        name="weight_grad_parts",
+    )(left, label, *rights)
+
+
+def grad_last_kernel(which_ref, left_ref, right_ref, label_ref, left2_ref, right2_ref, label2_ref, part_ref, out_ref, made):
+    del which_ref
+    turned = [left_ref[...].T, left2_ref[...].T]
+    labels = [label_ref[...], label2_ref[...]]
+    wide = right_ref.shape[2]
+    for m in range(out_ref.shape[0]):
+        masked = [jnp.where(label == m, x, jnp.zeros_like(x)) for label, x in zip(labels, turned, strict=True)]
+        for h in range(right_ref.shape[0]):
+            at = pl.ds(h * wide, wide)
+            made[...] = dot(masked[0], right_ref[h]) + dot(masked[1], right2_ref[h])
+            out_ref[m, :, at] = part_ref[m, :, at] + made[...]
+
+
+def weight_grad_last(left, right, label, part, which, tile):
+    mods, deep, wide = part.shape
+    group = left.shape[0] // 4
+    of_group = [
+        spec
+        for g in range(2)
+        for spec in (
+            pl.BlockSpec((group, tile), lambda i, which, g=g: (which[g], i)),
+            pl.BlockSpec((right.shape[0], group, right.shape[2]), lambda i, which, g=g: (0, which[g], 0)),
+            pl.BlockSpec((1, group), lambda i, which, g=g: (0, which[g])),
+        )
+    ]
+    return pl.pallas_call(
+        grad_last_kernel,
+        out_shape=jax.ShapeDtypeStruct(part.shape, F32),
+        grid_spec=pltpu.PrefetchScalarGridSpec(
+            num_scalar_prefetch=1,
+            grid=(deep // tile,),
+            in_specs=of_group + [pl.BlockSpec((mods, tile, wide), lambda i, which: (0, i, 0))],
+            out_specs=pl.BlockSpec((mods, tile, wide), lambda i, which: (0, i, 0)),
+            scratch_shapes=[pltpu.VMEM((tile, right.shape[2]), F32)],
+        ),
+        compiler_params=params(),
+        cost_estimate=pl.CostEstimate(
+            flops=4 * mods * group * deep * wide,
+            bytes_accessed=8 * mods * deep * wide,
+            transcendentals=0,
+        ),
+        name="weight_grad_last",
+    )(which, left, right, label, left, right, label, part)
 
 
 def grad_kernel(left_ref, right_ref, label_ref, out_ref):
@@ -1140,11 +1436,12 @@
 
     token_group = n * length
     if fast:
-        every_scaled, core_cot, _, labels, gate, gated_grad, conv, inner_by_time, proj = way_in(
+        every_scaled, core_cot, _, pair_cot, labels, gate, gated_grad, conv, inner_by_time, proj = way_in(
             block_input, norm_gain, cotangent, modality, in_weight, out_weight, conv_weight, conv_bias, x_weight, n, 0
         )
         every_label = labels[:, :, 0, :].reshape(4 * token_group)
-        half_cot = lax.all_gather(core_cot, "tok", axis=0, tiled=False)
+        rest = (1 - lax.axis_index("ch") // 4) * 2 * length
+        rest_cot = lax.all_gather(lax.dynamic_slice_in_dim(core_cot, rest, 2 * length, 0), "tok", axis=0, tiled=True)
     else:
         every_label = lax.all_gather(modality, ("tok", "ch"), axis=0, tiled=True)
     group_label = lax.dynamic_slice_in_dim(every_label, lax.axis_index("tok") * token_group, token_group, 0)
@@ -1166,27 +1463,37 @@
         proj = lax.psum(proj_part, "ch")
 
     gated, dgate, dact, dproj_part, ddtw, ddtb, dalog, dskip = by_groups(
-        lambda a, b, c, d, e, f: scan_both(a, b, c, d, e, f, dt_weight, dt_bias, a_log, skip_gain),
+        lambda a, b, c, d, e: scan_both(a, b, c, d, e, dt_weight, dt_bias, a_log, skip_gain),
         count,
-        (conv, proj, gate, gated_grad, label_by_time, label_row),
-        (0, 1, 0, 0, 0, 1),
+        (conv, proj, gate, gated_grad, label_by_time),
+        (0, 1, 0, 0, 0),
         (0, 0, 0, 1),
     )
-    dproj = sum_over_ch(dproj_part, n, 1) if fast else lax.psum(dproj_part, "ch")
-
-    dinner, dxw, dcw, dcb = by_groups(
-        lambda a, b, c, d, e, f: conv_backward(a, b, c, d, e, f, conv_weight, x_weight),
-        count,
-        (conv, inner_by_time, dact, dproj, label_by_time, label_row),
-        (0, 0, 0, 1, 0, 1),
-        (0,),
-    )
+    if fast:
+        branch_part, every_gated, dinner, dxw, dcw, dcb = middle(
+            dproj_part, gated, label, out_weight, conv, inner_by_time, dact, label_by_time, label_row, conv_weight, x_weight, n, 1
+        )
+    else:
+        dproj = lax.psum(dproj_part, "ch")
+        dinner, dxw, dcw, dcb = by_groups(
+            lambda a, b, c, d, e, f: conv_backward(a, b, c, d, e, f, conv_weight, x_weight),
+            count,
+            (conv, inner_by_time, dact, dproj, label_by_time, label_row),
+            (0, 0, 0, 1, 0, 1),
+            (0,),
+        )
+        branch_part = routed_spread(gated, label, out_weight, 512, False, BF16)
+        every_gated = lax.all_gather(gated, "tok", axis=0, tiled=True)
     every_label = every_label[None, :]
+    small = (dxw, ddtw, ddtb, dcw, dcb, dalog, dskip)
     if fast:
-        half_cot = half_cot.reshape(2 * token_group, half_cot.shape[-1])
-        every_grad, row_grad, gain_grad, near_cot = way_back(
-            dinner, dgate, in_weight, label, block_input, cotangent, norm_gain, half_cot, n, 2
+        pair_cot = pair_cot.reshape(rest_cot.shape)
+        every_grad, row_grad, gain_grad, near_pair, near_rest, grad_part, total, diag_gated = way_back(
+            dinner, dgate, in_weight, label, block_input, cotangent, norm_gain, pair_cot, rest_cot, every_scaled, every_label,
+            every_gated, small, n, 2,
         )
+        fourth = (lax.axis_index("tok") ^ 3) * token_group
+        every_gated = lax.dynamic_update_slice_in_dim(every_gated, diag_gated, fourth, 0)
         gain_grad = gain_grad[0]
     else:
         xz_grad = to_columns(dinner, dgate, n)
@@ -1197,35 +1504,49 @@
         row_grad = cotangent.astype(F32) + inverse * (ng - normed * jnp.mean(ng * normed, axis=-1, keepdims=True))
         every_grad = lax.all_gather(xz_grad, "tok", axis=0, tiled=True)[None]
 
-    small = (dxw, ddtw, ddtb, dcw, dcb, dalog, dskip)
-    every_gated = lax.all_gather(gated, "tok", axis=0, tiled=True)
     if fast:
-        gated, row_grad, small = lax.optimization_barrier((gated, row_grad, small))
-    branch_part = routed_spread(gated, label, out_weight, 512, False, BF16)
+        branch_part, row_grad = lax.optimization_barrier((branch_part, row_grad))
     branch = lax.psum_scatter(branch_part, "ch", scatter_dimension=0, tiled=True).astype(F32)
     block_out = (rows_float + branch).astype(BF16)
     if fast:
-        core = lax.axis_index("ch") % 2
+        ch = lax.axis_index("ch")
 
         def own_first(value):
-            halved = value.reshape((-1, 2, length) + value.shape[1:])
-            swapped = jnp.where(core == 0, halved, halved[:, ::-1])
-            return jnp.moveaxis(swapped, 1, 0).reshape(value.shape)
-
-        out_weight_grad = weight_grad_two(
-            own_first(every_gated), half_cot, near_cot, own_first(every_label[0])[None, :], mods, 128
+            split = value.reshape((4, 2, 2, 2, length) + value.shape[1:])
+            split = jnp.where(ch // 4 == 0, split, split[:, ::-1])
+            split = jnp.where(ch % 2 == 0, split, split[:, :, :, ::-1])
+            return jnp.moveaxis(split, (1, 3), (0, 1)).reshape(value.shape)
+
+        out_weight_grad = weight_grad_parts(
+            own_first(every_gated),
+            (pair_cot, near_pair, rest_cot, near_rest),
+            own_first(every_label[0])[None, :],
+            mods,
+            128,
         )
     else:
         out_weight_grad = weight_grad(every_gated, every_cot[None], every_label, mods, 128)
-    in_weight_grad = weight_grad(every_scaled, every_grad, every_label, mods, 256)
-    if not fast:
+    if fast:
+        others = (2 - lax.axis_index("tok") // 2 * 2 + jnp.arange(2)).astype(jnp.int32)
+        in_weight_grad = weight_grad_last(every_scaled, every_grad, every_label, grad_part, others, 256)
+    else:
+        in_weight_grad = weight_grad(every_scaled, every_grad, every_label, mods, 256)
+    sums = []
+    if fast:
+        for start, (value, m) in small_places(small):
+            rows = lax.slice_in_dim(total, start, start + value.shape[-2], axis=0)
+            if not m:
+                sums.append([])
+            sums[-1].append(rows)
+        sums = [rows[0] if len(value.shape) == 2 else jnp.stack(rows) for rows, value in zip(sums, small, strict=True)]
+    else:
         gain_grad = lax.psum(gain_grad, "tok")
-    flat = [value.reshape(-1, value.shape[-1]) for value in small]
-    total = lax.psum(jnp.concatenate(flat, axis=0), "tok")
-    start, sums = 0, []
-    for value, rows in zip(small, flat, strict=True):
-        sums.append(lax.slice_in_dim(total, start, start + rows.shape[0], axis=0).reshape(value.shape))
-        start += rows.shape[0]
+        flat = [value.reshape(-1, value.shape[-1]) for value in small]
+        total = lax.psum(jnp.concatenate(flat, axis=0), "tok")
+        start = 0
+        for value, rows in zip(small, flat, strict=True):
+            sums.append(lax.slice_in_dim(total, start, start + rows.shape[0], axis=0).reshape(value.shape))
+            start += rows.shape[0]
     dxw, ddtw, ddtb, dcw, dcb, dalog, dskip = sums
     return (
         block_out,

time: 508 us -> 468 us (0.921)
  Pallas kernels: 454 us -> 421 us
  local copies, waits for them, and re-layouts: 29.6 us -> 19.7 us
    pallas_call x5 -> x3, Pallas kernels: 130 us -> 102 us  [the longest x1 34.9 us: weight_grad_parts(): pl.pallas_call(grad_parts_kernel, out_shape=jax.ShapeDtypeStruct((mods, d...]
    pallas_call x1, Pallas kernels: 75 us -> 56.4 us  [scan_both(): pl.pallas_call(scan_kernel, out_shape=(jax.ShapeDtypeStruct((rows, channe...]
    pallas_call x1, Pallas kernels: 115 us -> 127 us  [way_back(): pl.pallas_call(functools.partial(back_kernel, chips), out_shape=(jax.Shap...]
    slice x6 -> x4, local copies, waits for them, and re-layouts: 9.68 us -> 2.4 us  [on_device(): rows = lax.slice_in_dim(total, start, start + value.shape[-2], axis=0)]
  transfers between devices with their start and end apart: 4 -> 2, of which waited for: 0 -> 0; matrix products, arithmetic and copies ran while one was open for 5% -> 4% of each run, Pallas kernels for 63% -> 34%
where the time goes in v4:
time: 468 us; the launch traced here: 465 us
  Pallas kernels  421 us (90%)
  local copies, waits for them, and re-layouts  19.7 us (4%)
  between operations  14.4 us (3%)
  other arithmetic  9.18 us (2%)
    pallas_call x1, Pallas kernels, way_in(): pl.pallas_call(functools.partial(front_kernel, chips), out_shape=(jax.Sha...  136 us
    pallas_call x1, Pallas kernels, way_back(): pl.pallas_call(functools.partial(back_kernel, chips), out_shape=(jax.Shap...  127 us
    pallas_call x1, Pallas kernels, scan_both(): pl.pallas_call(scan_kernel, out_shape=(jax.ShapeDtypeStruct((rows, channe...  56.4 us
    pallas_call x1, Pallas kernels, weight_grad_parts(): pl.pallas_call(grad_parts_kernel, out_shape=jax.ShapeDtypeStruct((mods, d...  34.9 us
    pallas_call x1, Pallas kernels, weight_grad_last(): pl.pallas_call(grad_last_kernel, out_shape=jax.ShapeDtypeStruct(part.shap...  34.3 us
    pallas_call x1, Pallas kernels, middle(): pl.pallas_call(functools.partial(middle_kernel, n // 2), out_shape=(jax.S...  33 us
  transfers between devices with their start and end apart: 2, of which 0 were waited for; matrix products, arithmetic and copies ran while one was open for 4% of the time, Pallas kernels for 34%

profile of v4, /device:TPU:0, one launch (start us, length us, event | category | flops | bytes accessed | tf_op | source)
XLA Modules:
  0.0 464.6 jit_solution(12788155552846179010)
XLA Ops:
  7.2 0.0 all-gather.2.cloned.1.call-start
  7.2 1.3 broadcast_in_dim.21.cb_ref
  8.5 1.3 broadcast_in_dim.19.gain_ref
  9.8 1.2 broadcast_in_dim.20.label_ref
  11.0 135.7 %way_in.1 = (bf16[4096,2048]{1,0:T(8,128)(2,1)}, bf16[512,2048]{1,0:T(8,128)(2,1)}, bf16[512,2048]{1,0:T(8,128)(2,1)}, bf16[4,2,128,2048]{3,2,1,0:T(8,128)(2,1)}...) custom-call(bf16[128,2048]{1,0:T(8,128)(2,1)} %input_ref.3, ...), custom_call_target="tpu_custom_call" | custom-call | flops 99999997952 | bytes 100000000 | tf_op jit(solution)/shard_map/way_in/pallas_call | solution.py:864
  146.8 2.3 constant_dynamic-slice_fusion
  149.1 0.0 all-gather.2.cloned.1.call-update
  149.1 0.0 reduce-scatter.2.cloned.1.call-start
  149.2 0.9 slice.39
  150.1 0.0 copy-start.4
  150.1 0.1 copy.29
  150.2 0.7 reshape_reshape.3.label_row_ref
  150.9 1.0 reshape.45.label_ref
  151.9 0.0 copy-done.6
  151.9 0.6 broadcast_in_dim.22.skip_ref
  152.5 1.0 copy.32.label_seq_ref.label_ref
  153.5 56.4 %scan_both.1 = (bf16[1024,512]{1,0:T(8,128)(2,1)}, bf16[1024,512]{1,0:T(8,128)(2,1)}, f32[1024,512]{1,0:T(8,128)}, f32[160,1024]{1,0:T(8,128)}, f32[3,128,512]{2...) custom-call(f32[1024,512]{1,0:T(8,128)} %get-tuple-element.45.conv_ref, ...), custom_call_target="tpu_custom_call" | custom-call | flops 41943040000 | bytes 10485760 | tf_op jit(solution)/shard_map/scan_both/pallas_call | solution.py:306
  210.0 0.0 copy-done.4
  210.0 33.0 %middle.1 = (bf16[1024,2048]{1,0:T(8,128)(2,1)}, bf16[4096,512]{1,0:T(8,128)(2,1)}, bf16[1024,512]{1,0:T(8,128)(2,1)}, f32[3,160,512]{2,1,0:T(8,128)}, f32[4,512]{1,0:T(4,128)}, /*index=5*/f32[1,512]{1,0:T(1,128)}) custom-call(f32[160,1024]{1,0:T(8,128)} %get-tuple-element.50.dproj_part_ref, bf16[1024,512]{1,0:T(8,128)(2,1)} %get-tuple-element.51.gated_ref, ...), custom_call_target="tpu_custom_call" | custom-call | flops 20000000000 | bytes 10000000 | tf_op jit(solution)/shard_map/middle/pallas_call | solution.py:528
  243.0 0.0 all-gather.2.cloned.1.call-done.rest_cot_ref.refs_2_
  243.0 126.8 %way_back.1 = (bf16[2,4096,512]{2,1,0:T(8,128)(2,1)}, f32[128,2048]{1,0:T(8,128)}, f32[8,256]{1,0:T(8,128)}, bf16[1024,2048]{1,0:T(8,128)(2,1)}, bf16[1024,2048]...) custom-call(bf16[1024,512]{1,0:T(8,128)(2,1)} %get-tuple-element.55.dinner_ref, ...), custom_call_target="tpu_custom_call" | custom-call | flops 99999997952 | bytes 100000000 | tf_op jit(solution)/shard_map/way_back/pallas_call | solution.py:1197
  369.9 0.0 copy-start.5
  369.9 0.0 copy-start
  369.9 0.0 copy-start.1
  369.9 0.0 reduce-scatter.2.cloned.1.call-update
  370.0 0.6 copy-done.5
  370.6 0.5 iota_add_fusion.which_ref
  371.1 0.6 reverse_select_fusion.2
  371.7 0.0 copy-done
  371.7 0.6 slice.47
  372.4 0.6 slice.48
  372.9 0.6 slice.50
  373.6 0.0 copy-done.1
  373.6 1.0 constant_dynamic-update-slice_fusion
  374.6 2.7 copy.36
  377.3 1.3 slice.40
  378.6 0.1 slice_bitcast_fusion.5
  378.7 0.9 pad_maximum_fusion.1
  379.6 0.1 slice_bitcast_fusion.2
  379.7 1.0 pad_maximum_fusion
  380.7 0.6 fusion
  381.3 1.1 reverse_select_fusion.1
  382.3 3.1 reverse_select_fusion
  385.4 34.3 %weight_grad_last.1 = f32[3,2048,1024]{2,1,0:T(8,128)} custom-call(s32[2]{0:T(128)} %iota_add_fusion.which_ref, bf16[4096,2048]{1,0:T(8,128)(2,1)} %get-tuple-element.59.scaled_ref.left_ref.left2_ref, bf16[2,4096,512]{2,1,0:T(8,128)(2,1)} %get-tuple-element.72.right_ref.right2_ref, s32[1,4096]{1,0:T(1,128)} %bitcast.36, ...), custom_call_target="tpu_custom_call" | custom-call | flops 25769803776 | bytes 50331648 | tf_op jit(solution)/shard_map/weight_grad_last/pallas_call | solution.py:1299
  419.7 34.9 %weight_grad_parts.1 = f32[3,512,2048]{2,1,0:T(8,128)} custom-call(bf16[4096,512]{1,0:T(8,128)(2,1)} %bitcast.32, s32[1,4096]{1,0:T(1,128)} %bitcast.40, bf16[1024,2048]{1,0:T(8,128)(2,1)} %bitcast.45, bf16[1024,2048]{1,0:T(8,128)(2,1)} %get-tuple-element.76.refs_1_, bf16[1024,2048]{1,0:T(8,128)(2,1)} %all-gather.2.cloned.1.call-done.rest_cot_ref.refs_2_, ...), custom_call_target="tpu_custom_call" | custom-call | flops 25769803776 | bytes 33554432 | tf_op jit(solution)/shard_map/weight_grad_parts/pallas_call | solution.py:1257
  454.6 0.0 copy-done.3
  454.6 2.0 add_convert_fusion
  456.6 1.0 copy.41
  (9 shorter events, 0.0 us)
Async XLA Ops:
  7.2 235.8 %all-gather.2.cloned.1.call-start = ((), (), s32[]{:S(2)}) async-start(), calls=%async_computation.1 | async-start | bytes 5242880 | tf_op jit(solution)/shard_map/all_gather | solution.py:1444
  11.0 140.9 %copy-start.6 = (bf16[512]{0:T(512)(128)(2,1)S(1)}, bf16[512]{0:T(512)(128)(2,1)}, u32[]{:S(2)}) copy-start(bf16[512]{0:T(512)(128)(2,1)} %param.22) | copy-start | bytes 3076
  149.1 305.5 %reduce-scatter.2.cloned.1.call-start = ((), (), s32[]{:S(2)}) async-start(), calls=%async_computation.2 | async-start | bytes 4718592 | tf_op jit(solution)/shard_map/reduce_scatter | solution.py:1509
  150.1 59.9 %copy-start.4 = (s32[4,8,1,128]{3,2,1,0:T(1,128)}, s32[4,8,1,128]{3,2,1,0:T(1,128)S(1)}, u32[]{:S(2)}) copy-start(s32[4,8,1,128]{3,2,1,0:T(1,128)S(1)} %slice.39) | copy-start | bytes 49156
  369.9 0.7 copy-start.5
  369.9 1.9 copy-start
  369.9 3.7 copy-start.1
  419.7 35.0 %copy-start.3 = (bf16[128,2048]{1,0:T(8,128)(2,1)S(1)}, bf16[128,2048]{1,0:T(8,128)(2,1)}, u32[]{:S(2)}) copy-start(bf16[128,2048]{1,0:T(8,128)(2,1)} %input_ref.3) | copy-start | bytes 1572868
  419.7 36.9 %copy-start.2 = (f32[128,2048]{1,0:T(8,128)S(1)}, f32[128,2048]{1,0:T(8,128)}, u32[]{:S(2)}) copy-start(f32[128,2048]{1,0:T(8,128)} %get-tuple-element.99) | copy-start | bytes 3145732
Sparse Core Ops, SparseCore 0:
  149.2 51.4 all-gather.1
  370.0 48.7 reduce-scatter.1

commit v5 on v4

--- a/solution.py
+++ b/solution.py
@@ -42,6 +42,10 @@
     for index in range(len(parts) - 2, -1, -1):
         total = jnp.where(label == index, parts[index], total)
     return total
+
+
+def by_kind(turned, label, mods):
+    return jnp.concatenate([jnp.where(label == m, turned, jnp.zeros_like(turned)) for m in range(mods)], axis=0)
 
 
 def sigmoid(x):
@@ -551,7 +555,7 @@
 
 def front_kernel(
     chips, input_ref, gain_ref, cot_ref, label_ref, iw_ref, ow_ref, cw_ref, cb_ref, xw_ref,
-    scaled_ref, core_cot_ref, near_cot_ref, pair_cot_ref, labels_ref, gate_ref, gated_grad_ref, conv_ref, inner_out_ref, proj_ref,
+    scaled_ref, core_cot_ref, near_cot_ref, pair_cot_ref, labels_ref, label_ref_seq, label_ref_time, label_ref_row, gate_ref, gated_grad_ref, conv_ref, inner_out_ref, proj_ref,
     own_rows, in_w, out_w, chunk_rows, staged, xz, proj_part, pad,
     in_sem, out_sem, load_sem, own_sem,
     line_send, line_recv, near_send, near_recv, tok_send, tok_recv, diag_send, diag_recv,
@@ -572,8 +576,8 @@
 
     rows = input_ref[...].astype(F32)
     inverse = lax.rsqrt(jnp.mean(rows * rows, axis=-1, keepdims=True) + 1e-05)
-    own_rows[...] = (rows * inverse * gain_ref[...].astype(F32)).astype(BF16)
-    labels_ref[tok, ch] = label_ref[...]
+    own_rows[...] = (rows * inverse * gain_ref[...].astype(F32)[None, :]).astype(BF16)
+    labels_ref[tok, ch] = jnp.broadcast_to(label_ref[...][None, :], (8, length))
 
     def block(g, device):
         return pl.ds(pl.multiple_of(g * group + device * length, length), length)
@@ -800,7 +804,7 @@
     inner_out_ref[...] = inner.astype(BF16)
     pad[pl.ds(0, lead), :] = jnp.zeros((lead, width), F32)
     pad[pl.ds(lead, group), :] = inner
-    conv = jnp.broadcast_to(cb_ref[...].astype(F32), (group, width))
+    conv = jnp.broadcast_to(cb_ref[...].astype(F32)[None, :], (group, width))
     for tap in range(taps):
         conv = conv + cw_ref[pl.ds(tap, 1), :].astype(F32) * pad[pl.ds(tap * GROUP, group), :]
     conv_ref[...] = conv
@@ -808,7 +812,11 @@
     label = jnp.concatenate(
         [jnp.broadcast_to(labels_ref[tok, d].astype(F32).T[:, 0:1], (length, 128)) for d in range(n)], axis=0
     )
-    label = jnp.concatenate([by_time(label)] * (width // 128), axis=1)
+    label_ref_seq[...] = label[:, 0:1].astype(jnp.int32)
+    label = by_time(label)
+    label_ref_time[...] = label[:, 0:1].astype(jnp.int32)
+    label_ref_row[...] = label.T[0:1, :].astype(jnp.int32)
+    label = jnp.concatenate([label] * (width // 128), axis=1)
     total = None
     for m in range(mods):
         high, low = halves(jnp.where(label == m, act, 0.0))
@@ -869,6 +877,9 @@
             jax.ShapeDtypeStruct((chips * length, deep), BF16),
             jax.ShapeDtypeStruct((4, 2, length, deep), BF16),
             jax.ShapeDtypeStruct((4, n, 8, length), jnp.int32),
+            jax.ShapeDtypeStruct((group, 1), jnp.int32),
+            jax.ShapeDtypeStruct((group, 1), jnp.int32),
+            jax.ShapeDtypeStruct((1, group), jnp.int32),
             jax.ShapeDtypeStruct((group, width), BF16),
             jax.ShapeDtypeStruct((group, width), BF16),
             jax.ShapeDtypeStruct((group, width), F32),
@@ -876,7 +887,7 @@
             jax.ShapeDtypeStruct((wide, group), F32),
         ),
         in_specs=[vmem, vmem, any_space, vmem, any_space, any_space, vmem, vmem, vmem],
-        out_specs=(any_space, any_space, any_space, any_space, vmem, vmem, vmem, vmem, vmem, vmem),
+        out_specs=(any_space,) * 4 + (vmem,) * 9,
         scratch_shapes=[
             pltpu.VMEM((length, deep), BF16),
             pltpu.VMEM(in_weight.shape, BF16),
@@ -896,8 +907,7 @@
         cost_estimate=pl.CostEstimate(flops=10**11, bytes_accessed=10**8, transcendentals=0),
         name="way_in",
     )(
-        block_input, gain[None, :], cotangent, jnp.broadcast_to(modality[None, :], (8, length)),
-        in_weight, out_weight, conv_weight, conv_bias[None, :], x_weight,
+        block_input, gain, cotangent, modality, in_weight, out_weight, conv_weight, conv_bias, x_weight,
     )
 
 
@@ -956,14 +966,11 @@
         pl.when(i >= 2)(made_copy(i - 2).wait)
         slot = lax.rem(i, 2)
         lanes = [pl.ds(pl.multiple_of((first + g) * group, group), group) for g in range(2)]
-        turned = [left[slot, g].T for g in range(2)]
-        for m in range(mods):
-            masked = [
-                jnp.where(label_row_ref[:, lanes[g]] == m, turned[g], jnp.zeros_like(turned[g])) for g in range(2)
-            ]
-            for h in range(2):
-                total = dot(masked[0], xall_ref[h, lanes[0], :]) + dot(masked[1], xall_ref[h, lanes[1], :])
-                made[slot, m, :, pl.ds(h * width, width)] = total
+        stacked = [by_kind(left[slot, g].T, label_row_ref[:, lanes[g]], mods) for g in range(2)]
+        for h in range(2):
+            total = dot(stacked[0], xall_ref[h, lanes[0], :]) + dot(stacked[1], xall_ref[h, lanes[1], :])
+            for m in range(mods):
+                made[slot, m, :, pl.ds(h * width, width)] = total[m * tile_rows : (m + 1) * tile_rows]
         made_copy(i).start()
 
         @pl.when(i + 2 < tiles)
@@ -1033,6 +1040,19 @@
         value = ref[...] if m is None else ref[m]
         packed[pl.ds(start, value.shape[0]), :] = value
     rounded[...] = packed[...].astype(BF16)
+    small_copies = [
+        remote(
+            rounded.at[rows_of(tok ^ g, quarter)],
+            small_in.at[g - 1],
+            to_small.at[g - 1],
+            from_small.at[g - 1],
+            (tok ^ g, ch),
+        )
+        for g in range(1, 4)
+    ]
+    for copy in small_copies:
+        copy.start()
+
     fetch.wait()
     for copy in cot_copies:
         copy.start()
@@ -1095,22 +1115,6 @@
         near_copies.append(copy)
     for j in order:
         both_cores(j)
-    for j in order:
-        pass_on(j)
-    small_copies = [
-        remote(
-            rounded.at[rows_of(tok ^ g, quarter)],
-            small_in.at[g - 1],
-            to_small.at[g - 1],
-            from_small.at[g - 1],
-            (tok ^ g, ch),
-        )
-        for g in range(1, 4)
-    ]
-    for copy in small_copies:
-        copy.start()
-
-    lax.fori_loop(0, tiles - 4, grad_tile, 0)
     value = packed[rows_of(tok, quarter), :]
     for copy in small_copies:
         copy.wait()
@@ -1123,7 +1127,9 @@
     ]
     for copy in small_copies:
         copy.start()
-    lax.fori_loop(tiles - 4, tiles - 2, grad_tile, 0)
+    for j in order:
+        pass_on(j)
+    lax.fori_loop(0, tiles - 2, grad_tile, 0)
     total = mine[...]
     for e in range(chips - 1):
         pltpu.make_async_copy(arrived.at[e], arrived.at[e], from_row.at[e]).wait()
@@ -1237,30 +1243,56 @@
     )(dinner, dgate, w, label, block_input, cotangent, gain[None, :], pair_cot, rest_cot, every_scaled, every_label, every_gated, *small)
 
 
-def grad_parts_kernel(left_ref, label_ref, *refs):
-    right_refs, out_ref = refs[:-1], refs[-1]
-    size = right_refs[0].shape[0]
-    turned, label = left_ref[...].T, label_ref[...]
-    for m in range(out_ref.shape[0]):
-        masked = jnp.where(label == m, turned, jnp.zeros_like(turned))
+def grad_parts_kernel(which_ref, *refs):
+    del which_ref
+    count = (len(refs) - 1) // 3
+    out_ref = refs[-1]
+    mods, tile, wide = out_ref.shape
+    stacked = []
+    for left_ref, label_ref in zip(refs[:count], refs[count : 2 * count], strict=True):
+        groups, _, chips, _, length, _ = left_ref.shape
+        turned = left_ref[...].reshape(groups * chips * length, tile).T
+        blocks = [
+            by_kind(turned[:, (g * chips + o) * length : (g * chips + o + 1) * length], label_ref[g, 0, o, 0], mods)
+            for g in range(groups)
+            for o in range(chips)
+        ]
+        stacked.append(jnp.concatenate(blocks, axis=1))
+    step = min(512, wide)
+    for start in range(0, wide, step):
+        at = pl.ds(start, step)
         total = None
-        for i, right_ref in enumerate(right_refs):
-            part = dot(masked[:, i * size : (i + 1) * size], right_ref[...])
+        for rows, right_ref in zip(stacked, refs[2 * count : -1], strict=True):
+            part = dot(rows, right_ref[:, at])
             total = part if total is None else total + part
-        out_ref[m] = total
-
-
-def weight_grad_parts(left, rights, label, mods, tile):
-    rows, deep = left.shape
+        for m in range(mods):
+            out_ref[m, :, at] = total[m * tile : (m + 1) * tile]
+
+
+def weight_grad_parts(left, rights, label, which, mods, tile):
+    groups, pairs, chips, cores, length, deep = left.shape
     size, wide = rights[0].shape
-    whole = pl.BlockSpec((size, wide), lambda i: (0, 0), pipeline_mode=pl.Buffered(1))
+    rows = left.size // deep
+    chosen = [(flip, turn) for flip in range(2) for turn in range(2)]
+
+    def block(last, moves, flip, turn):
+        def index(i, which):
+            return (0, which[0] ^ flip, 0, which[1] ^ turn, 0, i if moves else 0)
+
+        return pl.BlockSpec((groups, 1, chips, 1) + last, index)
+
+    whole = pl.BlockSpec((size, wide), lambda i, which: (0, 0), pipeline_mode=pl.Buffered(1))
     return pl.pallas_call(
         grad_parts_kernel,
         out_shape=jax.ShapeDtypeStruct((mods, deep, wide), F32),
-        grid=(deep // tile,),
-        in_specs=[pl.BlockSpec((rows, tile), lambda i: (0, i)), pl.BlockSpec((1, rows), lambda i: (0, 0))]
-        + [whole] * len(rights),
-        out_specs=pl.BlockSpec((mods, tile, wide), lambda i: (0, i, 0)),
+        grid_spec=pltpu.PrefetchScalarGridSpec(
+            num_scalar_prefetch=1,
+            grid=(deep // tile,),
+            in_specs=[block((length, tile), True, *c) for c in chosen]
+            + [block((1, length), False, *c) for c in chosen]
+            + [whole] * len(rights),
+            out_specs=pl.BlockSpec((mods, tile, wide), lambda i, which: (0, i, 0)),
+        ),
         compiler_params=params(),
         cost_estimate=pl.CostEstimate(
             flops=2 * mods * rows * deep * wide,
@@ -1268,20 +1300,21 @@
             transcendentals=0,
         ),
         name="weight_grad_parts",
-    )(left, label, *rights)
+    )(which, *[left] * 4, *[label] * 4, *rights)
 
 
 def grad_last_kernel(which_ref, left_ref, right_ref, label_ref, left2_ref, right2_ref, label2_ref, part_ref, out_ref, made):
     del which_ref
-    turned = [left_ref[...].T, left2_ref[...].T]
-    labels = [label_ref[...], label2_ref[...]]
+    mods, tile, _ = out_ref.shape
     wide = right_ref.shape[2]
-    for m in range(out_ref.shape[0]):
-        masked = [jnp.where(label == m, x, jnp.zeros_like(x)) for label, x in zip(labels, turned, strict=True)]
-        for h in range(right_ref.shape[0]):
-            at = pl.ds(h * wide, wide)
-            made[...] = dot(masked[0], right_ref[h]) + dot(masked[1], right2_ref[h])
-            out_ref[m, :, at] = part_ref[m, :, at] + made[...]
+    stacked = [
+        by_kind(x[...].T, label[...], mods) for x, label in ((left_ref, label_ref), (left2_ref, label2_ref))
+    ]
+    for h in range(right_ref.shape[0]):
+        at = pl.ds(h * wide, wide)
+        made[...] = dot(stacked[0], right_ref[h]) + dot(stacked[1], right2_ref[h])
+        for m in range(mods):
+            out_ref[m, :, at] = part_ref[m, :, at] + made[pl.ds(m * tile, tile), :]
 
 
 def weight_grad_last(left, right, label, part, which, tile):
@@ -1304,7 +1337,7 @@
             grid=(deep // tile,),
             in_specs=of_group + [pl.BlockSpec((mods, tile, wide), lambda i, which: (0, i, 0))],
             out_specs=pl.BlockSpec((mods, tile, wide), lambda i, which: (0, i, 0)),
-            scratch_shapes=[pltpu.VMEM((tile, right.shape[2]), F32)],
+            scratch_shapes=[pltpu.VMEM((mods * tile, right.shape[2]), F32)],
         ),
         compiler_params=params(),
         cost_estimate=pl.CostEstimate(
@@ -1436,7 +1469,7 @@
 
     token_group = n * length
     if fast:
-        every_scaled, core_cot, _, pair_cot, labels, gate, gated_grad, conv, inner_by_time, proj = way_in(
+        every_scaled, core_cot, _, pair_cot, labels, label, label_by_time, label_row, gate, gated_grad, conv, inner_by_time, proj = way_in(
             block_input, norm_gain, cotangent, modality, in_weight, out_weight, conv_weight, conv_bias, x_weight, n, 0
         )
         every_label = labels[:, :, 0, :].reshape(4 * token_group)
@@ -1444,12 +1477,11 @@
         rest_cot = lax.all_gather(lax.dynamic_slice_in_dim(core_cot, rest, 2 * length, 0), "tok", axis=0, tiled=True)
     else:
         every_label = lax.all_gather(modality, ("tok", "ch"), axis=0, tiled=True)
-    group_label = lax.dynamic_slice_in_dim(every_label, lax.axis_index("tok") * token_group, token_group, 0)
-    label = group_label[:, None]
-    label_by_time = group_label.reshape(count, GROUP, length).transpose(0, 2, 1).reshape(token_group, 1)
-    label_row = label_by_time.reshape(1, token_group)
-
     if not fast:
+        group_label = lax.dynamic_slice_in_dim(every_label, lax.axis_index("tok") * token_group, token_group, 0)
+        label = group_label[:, None]
+        label_by_time = group_label.reshape(count, GROUP, length).transpose(0, 2, 1).reshape(token_group, 1)
+        label_row = label_by_time.reshape(1, token_group)
         group_rows = lax.all_gather(scaled, "ch", axis=0, tiled=True)
         every_scaled = lax.all_gather(scaled, ("tok", "ch"), axis=0, tiled=True)
         every_cot = lax.all_gather(cotangent, ("tok", "ch"), axis=0, tiled=True)
@@ -1510,19 +1542,14 @@
     block_out = (rows_float + branch).astype(BF16)
     if fast:
         ch = lax.axis_index("ch")
-
-        def own_first(value):
-            split = value.reshape((4, 2, 2, 2, length) + value.shape[1:])
-            split = jnp.where(ch // 4 == 0, split, split[:, ::-1])
-            split = jnp.where(ch % 2 == 0, split, split[:, :, :, ::-1])
-            return jnp.moveaxis(split, (1, 3), (0, 1)).reshape(value.shape)
-
+        split = (4, 2, 2, 2)
         out_weight_grad = weight_grad_parts(
-            own_first(every_gated),
+            every_gated.reshape(split + (length, every_gated.shape[1])),
             (pair_cot, near_pair, rest_cot, near_rest),
-            own_first(every_label[0])[None, :],
+            every_label.reshape(split + (1, length)),
+            jnp.stack([ch // 4, ch % 2]).astype(jnp.int32),
             mods,
-            128,
+            256,
         )
     else:
         out_weight_grad = weight_grad(every_gated, every_cot[None], every_label, mods, 128)
@@ -1533,12 +1560,10 @@
         in_weight_grad = weight_grad(every_scaled, every_grad, every_label, mods, 256)
     sums = []
     if fast:
-        for start, (value, m) in small_places(small):
-            rows = lax.slice_in_dim(total, start, start + value.shape[-2], axis=0)
-            if not m:
-                sums.append([])
-            sums[-1].append(rows)
-        sums = [rows[0] if len(value.shape) == 2 else jnp.stack(rows) for rows, value in zip(sums, small, strict=True)]
+        starts = [start for start, (_, m) in small_places(small) if not m]
+        for start, value in zip(starts, small, strict=True):
+            size = math.prod(value.shape[:-1])
+            sums.append(lax.slice_in_dim(total, start, start + size, axis=0).reshape(value.shape))
     else:
         gain_grad = lax.psum(gain_grad, "tok")
         flat = [value.reshape(-1, value.shape[-1]) for value in small]

time: 468 us -> 444 us (0.949)
  Pallas kernels: 421 us -> 409 us
  local copies, waits for them, and re-layouts: 19.7 us -> 13 us
  other arithmetic: 9.18 us -> 3.13 us
    pallas_call x1, Pallas kernels: 127 us -> 112 us  [way_back(): pl.pallas_call(functools.partial(back_kernel, chips), out_shape=(jax.Shap...]
    select_n x4 -> x0, other arithmetic: 4.76 us -> none  [the longest x2 3.68 us: own_first(): split = jnp.where(ch % 2 == 0, split, split[:, :, :, ::-1])]
  transfers between devices with their start and end apart: 2 -> 2, of which waited for: 0 -> 0; matrix products, arithmetic and copies ran while one was open for 4% -> 2% of each run, Pallas kernels for 34% -> 36%
where the time goes in v5:
time: 444 us; the launch traced here: 439 us
  Pallas kernels  409 us (92%)
  between operations  14.5 us (3%)
  local copies, waits for them, and re-layouts  13 us (3%)
    pallas_call x1, Pallas kernels, way_in(): pl.pallas_call(functools.partial(front_kernel, chips), out_shape=(jax.Sha...  136 us
    pallas_call x1, Pallas kernels, way_back(): pl.pallas_call(functools.partial(back_kernel, chips), out_shape=(jax.Shap...  112 us
    pallas_call x1, Pallas kernels, scan_both(): pl.pallas_call(scan_kernel, out_shape=(jax.ShapeDtypeStruct((rows, channe...  55.9 us
    pallas_call x1, Pallas kernels, weight_grad_parts(): pl.pallas_call(grad_parts_kernel, out_shape=jax.ShapeDtypeStruct((mods, d...  36.7 us
    pallas_call x1, Pallas kernels, weight_grad_last(): pl.pallas_call(grad_last_kernel, out_shape=jax.ShapeDtypeStruct(part.shap...  34.4 us
    pallas_call x1, Pallas kernels, middle(): pl.pallas_call(functools.partial(middle_kernel, n // 2), out_shape=(jax.S...  33.3 us
  transfers between devices with their start and end apart: 2, of which 0 were waited for; matrix products, arithmetic and copies ran while one was open for 2% of the time, Pallas kernels for 36%

profile of v5, /device:TPU:0, one launch (start us, length us, event | category | flops | bytes accessed | tf_op | source)
XLA Modules:
  0.0 439.3 jit_solution(18402266781358764547)
XLA Ops:
  7.2 0.0 all-gather.2.cloned.1.call-start
  7.2 0.0 copy-start.4
  7.3 0.0 copy-start.5
  7.3 136.1 %way_in.1 = (bf16[4096,2048]{1,0:T(8,128)(2,1)}, bf16[512,2048]{1,0:T(8,128)(2,1)}, bf16[512,2048]{1,0:T(8,128)(2,1)}, bf16[4,2,128,2048]{3,2,1,0:T(8,128)(2,1)}...) custom-call(bf16[128,2048]{1,0:T(8,128)(2,1)} %input_ref.3, ...), custom_call_target="tpu_custom_call" | custom-call | flops 99999997952 | bytes 100000000 | tf_op jit(solution)/shard_map/way_in/pallas_call | solution.py:872
  143.3 2.3 constant_dynamic-slice_fusion
  145.7 0.0 all-gather.2.cloned.1.call-update
  145.7 0.0 reduce-scatter.2.cloned.1.call-start
  145.7 0.0 copy-done.4
  145.7 0.6 broadcast_in_dim.7.gain_ref
  146.3 0.0 copy-done.5
  146.3 0.6 broadcast_in_dim.6.skip_ref
  146.9 1.5 slice.27
  148.4 55.9 %scan_both.1 = (bf16[1024,512]{1,0:T(8,128)(2,1)}, bf16[1024,512]{1,0:T(8,128)(2,1)}, f32[1024,512]{1,0:T(8,128)}, f32[160,1024]{1,0:T(8,128)}, f32[3,128,512]{2...) custom-call(f32[1024,512]{1,0:T(8,128)} %get-tuple-element.48.conv_ref, ...), custom_call_target="tpu_custom_call" | custom-call | flops 41943040000 | bytes 10485760 | tf_op jit(solution)/shard_map/scan_both/pallas_call | solution.py:310
  204.3 33.3 %middle.1 = (bf16[1024,2048]{1,0:T(8,128)(2,1)}, bf16[4096,512]{1,0:T(8,128)(2,1)}, bf16[1024,512]{1,0:T(8,128)(2,1)}, f32[3,160,512]{2,1,0:T(8,128)}, f32[4,512]{1,0:T(4,128)}, /*index=5*/f32[1,512]{1,0:T(1,128)}) custom-call(f32[160,1024]{1,0:T(8,128)} %get-tuple-element.53.dproj_part_ref, bf16[1024,512]{1,0:T(8,128)(2,1)} %get-tuple-element.54.gated_ref, ...), custom_call_target="tpu_custom_call" | custom-call | flops 20000000000 | bytes 10000000 | tf_op jit(solution)/shard_map/middle/pallas_call | solution.py:532
  237.7 0.0 all-gather.2.cloned.1.call-done.rest_cot_ref.refs_10_
  237.7 112.3 %way_back.1 = (bf16[2,4096,512]{2,1,0:T(8,128)(2,1)}, f32[128,2048]{1,0:T(8,128)}, f32[8,256]{1,0:T(8,128)}, bf16[1024,2048]{1,0:T(8,128)(2,1)}, bf16[1024,2048]...) custom-call(bf16[1024,512]{1,0:T(8,128)(2,1)} %get-tuple-element.60.dinner_ref, ...), custom_call_target="tpu_custom_call" | custom-call | flops 99999997952 | bytes 100000000 | tf_op jit(solution)/shard_map/way_back/pallas_call | solution.py:1203
  350.0 0.0 copy-start
  350.0 0.0 copy-start.1
  350.0 0.0 reduce-scatter.2.cloned.1.call-update
  350.1 0.5 iota_add_fusion.which_ref
  350.6 0.7 pad_add_fusion.which_ref
  351.2 0.3 copy-done
  351.5 0.6 slice.32
  352.1 0.6 slice.31
  352.7 0.6 slice.34
  353.3 0.9 slice.30
  354.3 1.0 slice.29
  355.3 1.3 slice.28
  356.5 0.0 copy-done.1
  356.6 1.0 constant_dynamic-update-slice_fusion
  357.6 0.6 fusion
  358.2 34.4 %weight_grad_last.1 = f32[3,2048,1024]{2,1,0:T(8,128)} custom-call(s32[2]{0:T(128)} %iota_add_fusion.which_ref, bf16[4096,2048]{1,0:T(8,128)(2,1)} %get-tuple-element.64.scaled_ref.left_ref.left2_ref, bf16[2,4096,512]{2,1,0:T(8,128)(2,1)} %get-tuple-element.78.right_ref.right2_ref, s32[1,4096]{1,0:T(1,128)} %bitcast.14, ...), custom_call_target="tpu_custom_call" | custom-call | flops 25769803776 | bytes 50331648 | tf_op jit(solution)/shard_map/weight_grad_last/pallas_call | solution.py:1332
  392.6 0.0 copy-start.3
  392.6 0.0 copy-start.2
  392.6 36.7 %weight_grad_parts.1 = f32[3,512,2048]{2,1,0:T(8,128)} custom-call(s32[2]{0:T(128)} %pad_add_fusion.which_ref, bf16[4,2,2,2,128,512]{5,4,3,2,1,0:T(8,128)(2,1)} %bitcast.23, bf16[4,2,2,2,128,512]{5,4,3,2,1,0:T(8,128)(2,1)} %bitcast.24, bf16[4,2,2,2,128,512]{5,4,3,2,1,0:T(8,128)(2,1)} %bitcast.25, bf16[4,2,2,2,128,512]{5,4,3,2,1,0:T(8,128)(2,1)} %bitcast.26, ...), custom_call_target="tpu_custom_call" | custom-call | flops 25769803776 | bytes 33554432 | tf_op jit(solution)/shard_map/weight_grad_parts/pallas_call | solution.py:1285
  429.2 0.0 reduce-scatter.2.cloned.1.call-done
  429.2 0.0 copy-done.3
  429.3 2.0 add_convert_fusion
  431.2 0.0 copy-done.2
  431.2 1.0 copy.27
Async XLA Ops:
  7.2 230.5 %all-gather.2.cloned.1.call-start = ((), (), s32[]{:S(2)}) async-start(), calls=%async_computation.1 | async-start | bytes 5242880 | tf_op jit(solution)/shard_map/all_gather | solution.py:1477
  7.2 138.5 %copy-start.4 = (bf16[2048]{0:T(1024)(128)(2,1)S(1)}, bf16[2048]{0:T(1024)(128)(2,1)}, u32[]{:S(2)}) copy-start(bf16[2048]{0:T(1024)(128)(2,1)} %gain_ref.1) | copy-start | bytes 12292
  7.3 139.1 %copy-start.5 = (bf16[512]{0:T(512)(128)(2,1)S(1)}, bf16[512]{0:T(512)(128)(2,1)}, u32[]{:S(2)}) copy-start(bf16[512]{0:T(512)(128)(2,1)} %param.22) | copy-start | bytes 3076
  145.7 283.6 %reduce-scatter.2.cloned.1.call-start = ((), (), s32[]{:S(2)}) async-start(), calls=%async_computation.2 | async-start | bytes 4718592 | tf_op jit(solution)/shard_map/reduce_scatter | solution.py:1541
  350.0 1.5 copy-start
  350.0 6.6 %copy-start.1 = (bf16[1024,512]{1,0:T(8,128)(2,1)S(1)}, bf16[1024,512]{1,0:T(8,128)(2,1)}, u32[]{:S(2)}) copy-start(bf16[1024,512]{1,0:T(8,128)(2,1)} %get-tuple-element.81) | copy-start | bytes 3145732
  392.6 36.7 %copy-start.3 = (bf16[128,2048]{1,0:T(8,128)(2,1)S(1)}, bf16[128,2048]{1,0:T(8,128)(2,1)}, u32[]{:S(2)}) copy-start(bf16[128,2048]{1,0:T(8,128)(2,1)} %input_ref.3) | copy-start | bytes 1572868
  392.6 38.7 %copy-start.2 = (f32[128,2048]{1,0:T(8,128)S(1)}, f32[128,2048]{1,0:T(8,128)}, u32[]{:S(2)}) copy-start(f32[128,2048]{1,0:T(8,128)} %get-tuple-element.99) | copy-start | bytes 3145732
Sparse Core Ops, SparseCore 0:
  145.8 51.4 all-gather.1
  350.1 49.0 reduce-scatter.1

commit v6 on v5

--- a/solution.py
+++ b/solution.py
@@ -228,7 +228,7 @@
     zero = jnp.zeros((GROUP, width), F32)
     lax.fori_loop(0, length, forward, (zero,) * states, unroll=8)
 
-    gate = by_time(gate_ref[...])
+    gate = gate_ref[...].astype(F32)
     grad = by_time(grad_ref[...])
     soft = sigmoid(gate)
     opened = gate * soft
@@ -555,7 +555,7 @@
 
 def front_kernel(
     chips, input_ref, gain_ref, cot_ref, label_ref, iw_ref, ow_ref, cw_ref, cb_ref, xw_ref,
-    scaled_ref, core_cot_ref, near_cot_ref, pair_cot_ref, labels_ref, label_ref_seq, label_ref_time, label_ref_row, gate_ref, gated_grad_ref, conv_ref, inner_out_ref, proj_ref,
+    scaled_ref, core_cot_ref, near_cot_ref, pair_cot_ref, rest_cot_ref, labels_ref, label_ref_all, label_ref_seq, label_ref_time, label_ref_row, gate_ref, gated_grad_ref, conv_ref, inner_out_ref, proj_ref,
     own_rows, in_w, out_w, chunk_rows, staged, xz, proj_part, pad,
     in_sem, out_sem, load_sem, own_sem,
     line_send, line_recv, near_send, near_recv, tok_send, tok_recv, diag_send, diag_recv,
@@ -729,6 +729,11 @@
             pl.when(target != ch)(copy.start)
             pl.when(target == ch)(local.start)
 
+    def keep(dst):
+        copy = pltpu.make_async_copy(chunk_rows.at[pl.ds(pl.multiple_of(core * length, length), length)], dst, keep_sem)
+        copy.start()
+        copy.wait()
+
     def project_back(o):
         load(1, o)
         label = label_column(o)
@@ -738,10 +743,11 @@
 
         @pl.when(o // 2 == chip // 2)
         def _():
-            mine = chunk_rows.at[pl.ds(pl.multiple_of(core * length, length), length)]
-            copy = pltpu.make_async_copy(mine, pair_cot_ref.at[tok, o % 2], keep_sem)
-            copy.start()
-            copy.wait()
+            keep(pair_cot_ref.at[tok, o % 2])
+
+        @pl.when(o // 2 != chip // 2)
+        def _():
+            keep(rest_cot_ref.at[pl.ds(pl.multiple_of(o % 2 * length, length), length)])
 
     def both_sides(i, fn):
         for o in (chip - i, chip + i):
@@ -797,7 +803,7 @@
     for o in range(chips):
         for a in range(2):
             arrive(xz.at[a, pl.ds(o * chunk, chunk)], xz_recv.at[a, o])
-    gate_ref[...] = xz[1]
+    gate_ref[...] = by_time(xz[1]).astype(BF16)
     taps = cw_ref.shape[0]
     lead = (taps - 1) * GROUP
     inner = by_time(xz[0])
@@ -826,8 +832,9 @@
 
     both_sides(chips - 1, functools.partial(accept, 1))
     pair_pass(1 - chip % 2)
-    sum_body(chips, proj_part, proj_ref, *sum_refs)
-    both_sides(chips - 1, project_back)
+    sum_body(
+        chips, proj_part, proj_ref, *sum_refs, work=lambda i: both_sides(chips - 1, project_back) if i == 1 else None
+    )
 
     def finish(o, carry):
         for g in range(4):
@@ -858,6 +865,9 @@
     for g in range(1, 4):
         arrive(labels_ref.at[tok ^ g], lab_tok_recv.at[g - 1])
         label_tok[g - 1].wait_send()
+    for g in range(4):
+        for d in range(n):
+            label_ref_all[:, pl.ds((g * n + d) * length, length)] = labels_ref[g, d, 0:1, :]
 
 
 def way_in(block_input, gain, cotangent, modality, in_weight, out_weight, conv_weight, conv_bias, x_weight, n, collective_id):
@@ -876,7 +886,9 @@
             jax.ShapeDtypeStruct((chips * length, deep), BF16),
             jax.ShapeDtypeStruct((chips * length, deep), BF16),
             jax.ShapeDtypeStruct((4, 2, length, deep), BF16),
+            jax.ShapeDtypeStruct((2 * length, deep), BF16),
             jax.ShapeDtypeStruct((4, n, 8, length), jnp.int32),
+            jax.ShapeDtypeStruct((1, 4 * group), jnp.int32),
             jax.ShapeDtypeStruct((group, 1), jnp.int32),
             jax.ShapeDtypeStruct((group, 1), jnp.int32),
             jax.ShapeDtypeStruct((1, group), jnp.int32),
@@ -887,7 +899,7 @@
             jax.ShapeDtypeStruct((wide, group), F32),
         ),
         in_specs=[vmem, vmem, any_space, vmem, any_space, any_space, vmem, vmem, vmem],
-        out_specs=(any_space,) * 4 + (vmem,) * 9,
+        out_specs=(any_space,) * 5 + (vmem,) * 10,
         scratch_shapes=[
             pltpu.VMEM((length, deep), BF16),
             pltpu.VMEM(in_weight.shape, BF16),
@@ -1469,12 +1481,10 @@
 
     token_group = n * length
     if fast:
-        every_scaled, core_cot, _, pair_cot, labels, label, label_by_time, label_row, gate, gated_grad, conv, inner_by_time, proj = way_in(
+        every_scaled, _, _, pair_cot, rest_cot, _, every_label, label, label_by_time, label_row, gate, gated_grad, conv, inner_by_time, proj = way_in(
             block_input, norm_gain, cotangent, modality, in_weight, out_weight, conv_weight, conv_bias, x_weight, n, 0
         )
-        every_label = labels[:, :, 0, :].reshape(4 * token_group)
-        rest = (1 - lax.axis_index("ch") // 4) * 2 * length
-        rest_cot = lax.all_gather(lax.dynamic_slice_in_dim(core_cot, rest, 2 * length, 0), "tok", axis=0, tiled=True)
+        rest_cot = lax.all_gather(rest_cot, "tok", axis=0, tiled=True)
     else:
         every_label = lax.all_gather(modality, ("tok", "ch"), axis=0, tiled=True)
     if not fast:
@@ -1487,6 +1497,7 @@
         every_cot = lax.all_gather(cotangent, ("tok", "ch"), axis=0, tiled=True)
         xz = routed_select(group_rows, label, in_weight, 256, False)
         inner, gate = to_owners(xz, n)
+        gate = gate.reshape(count, GROUP, length, -1).swapaxes(1, 2).reshape(gate.shape)
         group_cot = lax.all_gather(cotangent, "ch", axis=0, tiled=True)
         gated_grad = routed_select(group_cot, label, out_weight, 128, True)
         conv, inner_by_time, proj_part = by_groups(
@@ -1516,7 +1527,8 @@
         )
         branch_part = routed_spread(gated, label, out_weight, 512, False, BF16)
         every_gated = lax.all_gather(gated, "tok", axis=0, tiled=True)
-    every_label = every_label[None, :]
+    if not fast:
+        every_label = every_label[None, :]
     small = (dxw, ddtw, ddtb, dcw, dcb, dalog, dskip)
     if fast:
         pair_cot = pair_cot.reshape(rest_cot.shape)

time: 444 us -> 436 us (0.982)
  transfers between devices with their start and end apart: 2 -> 2, of which waited for: 0 -> 0; matrix products, arithmetic and copies ran while one was open for 2% -> 2% of each run, Pallas kernels for 36% -> 37%
where the time goes in v6:
time: 436 us; the launch traced here: 431 us
  Pallas kernels  405 us (93%)
  between operations  14.5 us (3%)
  local copies, waits for them, and re-layouts  9.19 us (2%)
    pallas_call x1, Pallas kernels, way_in(): pl.pallas_call(functools.partial(front_kernel, chips), out_shape=(jax.Sha...  133 us
    pallas_call x1, Pallas kernels, way_back(): pl.pallas_call(functools.partial(back_kernel, chips), out_shape=(jax.Shap...  112 us
    pallas_call x1, Pallas kernels, scan_both(): pl.pallas_call(scan_kernel, out_shape=(jax.ShapeDtypeStruct((rows, channe...  55.5 us
    pallas_call x1, Pallas kernels, weight_grad_parts(): pl.pallas_call(grad_parts_kernel, out_shape=jax.ShapeDtypeStruct((mods, d...  36.6 us
    pallas_call x1, Pallas kernels, weight_grad_last(): pl.pallas_call(grad_last_kernel, out_shape=jax.ShapeDtypeStruct(part.shap...  34.3 us
    pallas_call x1, Pallas kernels, middle(): pl.pallas_call(functools.partial(middle_kernel, n // 2), out_shape=(jax.S...  33.3 us
  transfers between devices with their start and end apart: 2, of which 0 were waited for; matrix products, arithmetic and copies ran while one was open for 2% of the time, Pallas kernels for 37%

profile of v6, /device:TPU:0, one launch (start us, length us, event | category | flops | bytes accessed | tf_op | source)
XLA Modules:
  0.0 431.5 jit_solution(12202279031176079944)
XLA Ops:
  7.2 0.0 copy-start.4
  7.2 0.0 copy-start.5
  7.2 0.0 all-gather.2.cloned.1.call-start
  7.2 133.0 %way_in.1 = (bf16[4096,2048]{1,0:T(8,128)(2,1)}, bf16[512,2048]{1,0:T(8,128)(2,1)}, bf16[512,2048]{1,0:T(8,128)(2,1)}, bf16[4,2,128,2048]{3,2,1,0:T(8,128)(2,1)}...) custom-call(bf16[128,2048]{1,0:T(8,128)(2,1)} %input_ref.3, ...), custom_call_target="tpu_custom_call" | custom-call | flops 99999997952 | bytes 100000000 | tf_op jit(solution)/shard_map/way_in/pallas_call | solution.py:882
  140.3 0.0 all-gather.2.cloned.1.call-update
  140.3 0.0 reduce-scatter.2.cloned.1.call-start
  140.4 0.0 copy-done.4
  140.4 0.6 broadcast_in_dim.7.gain_ref
  141.0 0.0 copy-done.5
  141.0 0.6 broadcast_in_dim.6.skip_ref
  141.6 55.5 %scan_both.1 = (bf16[1024,512]{1,0:T(8,128)(2,1)}, bf16[1024,512]{1,0:T(8,128)(2,1)}, f32[1024,512]{1,0:T(8,128)}, f32[160,1024]{1,0:T(8,128)}, f32[3,128,512]{2...) custom-call(f32[1024,512]{1,0:T(8,128)} %get-tuple-element.48.conv_ref, ...), custom_call_target="tpu_custom_call" | custom-call | flops 41943040000 | bytes 10485760 | tf_op jit(solution)/shard_map/scan_both/pallas_call | solution.py:310
  197.0 33.3 %middle.1 = (bf16[1024,2048]{1,0:T(8,128)(2,1)}, bf16[4096,512]{1,0:T(8,128)(2,1)}, bf16[1024,512]{1,0:T(8,128)(2,1)}, f32[3,160,512]{2,1,0:T(8,128)}, f32[4,512]{1,0:T(4,128)}, /*index=5*/f32[1,512]{1,0:T(1,128)}) custom-call(f32[160,1024]{1,0:T(8,128)} %get-tuple-element.53.dproj_part_ref, bf16[1024,512]{1,0:T(8,128)(2,1)} %get-tuple-element.54.gated_ref, ...), custom_call_target="tpu_custom_call" | custom-call | flops 20000000000 | bytes 10000000 | tf_op jit(solution)/shard_map/middle/pallas_call | solution.py:532
  230.3 0.0 all-gather.2.cloned.1.call-done.rest_cot_ref.refs_10_
  230.4 111.9 %way_back.1 = (bf16[2,4096,512]{2,1,0:T(8,128)(2,1)}, f32[128,2048]{1,0:T(8,128)}, f32[8,256]{1,0:T(8,128)}, bf16[1024,2048]{1,0:T(8,128)(2,1)}, bf16[1024,2048]...) custom-call(bf16[1024,512]{1,0:T(8,128)(2,1)} %get-tuple-element.60.dinner_ref, ...), custom_call_target="tpu_custom_call" | custom-call | flops 99999997952 | bytes 100000000 | tf_op jit(solution)/shard_map/way_back/pallas_call | solution.py:1215
  342.3 0.0 copy-start
  342.3 0.0 copy-start.1
  342.3 0.0 reduce-scatter.2.cloned.1.call-update
  342.3 0.5 iota_add_fusion.which_ref
  342.8 0.6 pad_add_fusion.which_ref
  343.4 0.4 copy-done
  343.8 0.6 slice.28
  344.4 0.6 slice.27
  345.0 0.6 slice.30
  345.6 0.9 slice.26
  346.5 1.0 slice.25
  347.6 1.3 slice.24
  348.8 0.0 copy-done.1
  348.8 1.0 constant_dynamic-update-slice_fusion
  349.9 0.6 fusion
  350.5 34.3 %weight_grad_last.1 = f32[3,2048,1024]{2,1,0:T(8,128)} custom-call(s32[2]{0:T(128)} %iota_add_fusion.which_ref, bf16[4096,2048]{1,0:T(8,128)(2,1)} %get-tuple-element.64.scaled_ref.left_ref.left2_ref, bf16[2,4096,512]{2,1,0:T(8,128)(2,1)} %get-tuple-element.78.right_ref.right2_ref, s32[1,4096]{1,0:T(1,128)} %get-tuple-element.65.label_row_ref.label_ref.label2_ref, ...), custom_call_target="tpu_custom_call" | custom-call | flops 25769803776 | bytes 50331648 | tf_op jit(solution)/shard_map/weight_grad_last/pallas_call | solution.py:1344
  384.8 0.0 copy-start.3
  384.8 0.0 copy-start.2
  384.8 36.6 %weight_grad_parts.1 = f32[3,512,2048]{2,1,0:T(8,128)} custom-call(s32[2]{0:T(128)} %pad_add_fusion.which_ref, bf16[4,2,2,2,128,512]{5,4,3,2,1,0:T(8,128)(2,1)} %bitcast.19, bf16[4,2,2,2,128,512]{5,4,3,2,1,0:T(8,128)(2,1)} %bitcast.20, bf16[4,2,2,2,128,512]{5,4,3,2,1,0:T(8,128)(2,1)} %bitcast.21, bf16[4,2,2,2,128,512]{5,4,3,2,1,0:T(8,128)(2,1)} %bitcast.22, ...), custom_call_target="tpu_custom_call" | custom-call | flops 25769803776 | bytes 33554432 | tf_op jit(solution)/shard_map/weight_grad_parts/pallas_call | solution.py:1297
  421.4 0.0 reduce-scatter.2.cloned.1.call-done
  421.4 0.0 copy-done.3
  421.4 2.0 add_convert_fusion
  423.4 0.0 copy-done.2
  423.4 1.0 copy.27
Async XLA Ops:
  7.2 133.2 %copy-start.4 = (bf16[2048]{0:T(1024)(128)(2,1)S(1)}, bf16[2048]{0:T(1024)(128)(2,1)}, u32[]{:S(2)}) copy-start(bf16[2048]{0:T(1024)(128)(2,1)} %gain_ref.1) | copy-start | bytes 12292
  7.2 133.8 %copy-start.5 = (bf16[512]{0:T(512)(128)(2,1)S(1)}, bf16[512]{0:T(512)(128)(2,1)}, u32[]{:S(2)}) copy-start(bf16[512]{0:T(512)(128)(2,1)} %param.22) | copy-start | bytes 3076
  7.2 223.2 %all-gather.2.cloned.1.call-start = ((), (), s32[]{:S(2)}) async-start(), calls=%async_computation.1 | async-start | bytes 5242880 | tf_op jit(solution)/shard_map/all_gather | solution.py:1487
  140.3 281.1 %reduce-scatter.2.cloned.1.call-start = ((), (), s32[]{:S(2)}) async-start(), calls=%async_computation.2 | async-start | bytes 4718592 | tf_op jit(solution)/shard_map/reduce_scatter | solution.py:1553
  342.3 1.5 copy-start
  342.3 6.6 %copy-start.1 = (bf16[1024,512]{1,0:T(8,128)(2,1)S(1)}, bf16[1024,512]{1,0:T(8,128)(2,1)}, u32[]{:S(2)}) copy-start(bf16[1024,512]{1,0:T(8,128)(2,1)} %get-tuple-element.81) | copy-start | bytes 3145732
  384.8 36.6 %copy-start.3 = (bf16[128,2048]{1,0:T(8,128)(2,1)S(1)}, bf16[128,2048]{1,0:T(8,128)(2,1)}, u32[]{:S(2)}) copy-start(bf16[128,2048]{1,0:T(8,128)(2,1)} %input_ref.3) | copy-start | bytes 1572868
  384.8 38.6 %copy-start.2 = (f32[128,2048]{1,0:T(8,128)S(1)}, f32[128,2048]{1,0:T(8,128)}, u32[]{:S(2)}) copy-start(f32[128,2048]{1,0:T(8,128)} %get-tuple-element.99) | copy-start | bytes 3145732
Sparse Core Ops, SparseCore 0:
  140.4 51.4 all-gather.1
  342.4 49.4 reduce-scatter.1

commit v7 on v6

--- a/solution.py
+++ b/solution.py
@@ -1257,28 +1257,25 @@
 
 def grad_parts_kernel(which_ref, *refs):
     del which_ref
-    count = (len(refs) - 1) // 3
-    out_ref = refs[-1]
-    mods, tile, wide = out_ref.shape
-    stacked = []
-    for left_ref, label_ref in zip(refs[:count], refs[count : 2 * count], strict=True):
-        groups, _, chips, _, length, _ = left_ref.shape
-        turned = left_ref[...].reshape(groups * chips * length, tile).T
-        blocks = [
-            by_kind(turned[:, (g * chips + o) * length : (g * chips + o + 1) * length], label_ref[g, 0, o, 0], mods)
-            for g in range(groups)
-            for o in range(chips)
-        ]
-        stacked.append(jnp.concatenate(blocks, axis=1))
-    step = min(512, wide)
-    for start in range(0, wide, step):
-        at = pl.ds(start, step)
-        total = None
-        for rows, right_ref in zip(stacked, refs[2 * count : -1], strict=True):
-            part = dot(rows, right_ref[:, at])
-            total = part if total is None else total + part
-        for m in range(mods):
-            out_ref[m, :, at] = total[m * tile : (m + 1) * tile]
+    count = (len(refs) - 2) // 3
+    out_ref, stacked = refs[-2:]
+    mods, deep, _ = out_ref.shape
+
+    @pl.when(pl.program_id(0) == 0)
+    def _():
+        for i, (left_ref, label_ref) in enumerate(zip(refs[:count], refs[count : 2 * count], strict=True)):
+            groups, _, chips, _, length, _ = left_ref.shape
+            for g in range(groups):
+                for o in range(chips):
+                    at = pl.ds((g * chips + o) * length, length)
+                    stacked[i, :, at] = by_kind(left_ref[g, 0, o, 0].T, label_ref[g, 0, o, 0], mods)
+
+    total = None
+    for i, right_ref in enumerate(refs[2 * count : 3 * count]):
+        part = dot(stacked[i], right_ref[...])
+        total = part if total is None else total + part
+    for m in range(mods):
+        out_ref[m] = total[m * deep : (m + 1) * deep]
 
 
 def weight_grad_parts(left, rights, label, which, mods, tile):
@@ -1287,23 +1284,24 @@
     rows = left.size // deep
     chosen = [(flip, turn) for flip in range(2) for turn in range(2)]
 
-    def block(last, moves, flip, turn):
+    def block(last, flip, turn):
         def index(i, which):
-            return (0, which[0] ^ flip, 0, which[1] ^ turn, 0, i if moves else 0)
-
-        return pl.BlockSpec((groups, 1, chips, 1) + last, index)
-
-    whole = pl.BlockSpec((size, wide), lambda i, which: (0, 0), pipeline_mode=pl.Buffered(1))
+            return (0, which[0] ^ flip, 0, which[1] ^ turn, 0, 0)
+
+        return pl.BlockSpec((groups, 1, chips, 1) + last, index, pipeline_mode=pl.Buffered(1))
+
+    cut = pl.BlockSpec((size, tile), lambda i, which: (0, i))
     return pl.pallas_call(
         grad_parts_kernel,
         out_shape=jax.ShapeDtypeStruct((mods, deep, wide), F32),
         grid_spec=pltpu.PrefetchScalarGridSpec(
             num_scalar_prefetch=1,
-            grid=(deep // tile,),
-            in_specs=[block((length, tile), True, *c) for c in chosen]
-            + [block((1, length), False, *c) for c in chosen]
-            + [whole] * len(rights),
-            out_specs=pl.BlockSpec((mods, tile, wide), lambda i, which: (0, i, 0)),
+            grid=(wide // tile,),
+            in_specs=[block((length, deep), *c) for c in chosen]
+            + [block((1, length), *c) for c in chosen]
+            + [cut] * len(rights),
+            out_specs=pl.BlockSpec((mods, deep, tile), lambda i, which: (0, 0, i)),
+            scratch_shapes=[pltpu.VMEM((len(rights), mods * deep, size), BF16)],
         ),
         compiler_params=params(),
         cost_estimate=pl.CostEstimate(

time: 436 us -> 436 us (level)
  no operation moved by 1% of the time
where the time goes in v7:
time: 436 us; the launch traced here: 432 us
  Pallas kernels  405 us (93%)
  between operations  14.5 us (3%)
  local copies, waits for them, and re-layouts  9.19 us (2%)
    pallas_call x1, Pallas kernels, way_in(): pl.pallas_call(functools.partial(front_kernel, chips), out_shape=(jax.Sha...  133 us
    pallas_call x1, Pallas kernels, way_back(): pl.pallas_call(functools.partial(back_kernel, chips), out_shape=(jax.Shap...  112 us
    pallas_call x1, Pallas kernels, scan_both(): pl.pallas_call(scan_kernel, out_shape=(jax.ShapeDtypeStruct((rows, channe...  55.5 us
    pallas_call x1, Pallas kernels, weight_grad_parts(): pl.pallas_call(grad_parts_kernel, out_shape=jax.ShapeDtypeStruct((mods, d...  36.9 us
    pallas_call x1, Pallas kernels, weight_grad_last(): pl.pallas_call(grad_last_kernel, out_shape=jax.ShapeDtypeStruct(part.shap...  34.3 us
    pallas_call x1, Pallas kernels, middle(): pl.pallas_call(functools.partial(middle_kernel, n // 2), out_shape=(jax.S...  33.3 us
  transfers between devices with their start and end apart: 2, of which 0 were waited for; matrix products, arithmetic and copies ran while one was open for 2% of the time, Pallas kernels for 37%

profile of v7, /device:TPU:0, one launch (start us, length us, event | category | flops | bytes accessed | tf_op | source)
XLA Modules:
  0.0 431.7 jit_solution(16516094014641512183)
XLA Ops:
  7.2 0.0 copy-start.4
  7.2 0.0 copy-start.5
  7.2 0.0 all-gather.2.cloned.1.call-start
  7.2 133.0 %way_in.1 = (bf16[4096,2048]{1,0:T(8,128)(2,1)}, bf16[512,2048]{1,0:T(8,128)(2,1)}, bf16[512,2048]{1,0:T(8,128)(2,1)}, bf16[4,2,128,2048]{3,2,1,0:T(8,128)(2,1)}...) custom-call(bf16[128,2048]{1,0:T(8,128)(2,1)} %input_ref.3, ...), custom_call_target="tpu_custom_call" | custom-call | flops 99999997952 | bytes 100000000 | tf_op jit(solution)/shard_map/way_in/pallas_call | solution.py:882
  140.3 0.0 all-gather.2.cloned.1.call-update
  140.3 0.0 reduce-scatter.2.cloned.1.call-start
  140.4 0.0 copy-done.4
  140.4 0.6 broadcast_in_dim.7.gain_ref
  141.0 0.0 copy-done.5
  141.0 0.6 broadcast_in_dim.6.skip_ref
  141.6 55.5 %scan_both.1 = (bf16[1024,512]{1,0:T(8,128)(2,1)}, bf16[1024,512]{1,0:T(8,128)(2,1)}, f32[1024,512]{1,0:T(8,128)}, f32[160,1024]{1,0:T(8,128)}, f32[3,128,512]{2...) custom-call(f32[1024,512]{1,0:T(8,128)} %get-tuple-element.48.conv_ref, ...), custom_call_target="tpu_custom_call" | custom-call | flops 41943040000 | bytes 10485760 | tf_op jit(solution)/shard_map/scan_both/pallas_call | solution.py:310
  197.0 33.3 %middle.1 = (bf16[1024,2048]{1,0:T(8,128)(2,1)}, bf16[4096,512]{1,0:T(8,128)(2,1)}, bf16[1024,512]{1,0:T(8,128)(2,1)}, f32[3,160,512]{2,1,0:T(8,128)}, f32[4,512]{1,0:T(4,128)}, /*index=5*/f32[1,512]{1,0:T(1,128)}) custom-call(f32[160,1024]{1,0:T(8,128)} %get-tuple-element.53.dproj_part_ref, bf16[1024,512]{1,0:T(8,128)(2,1)} %get-tuple-element.54.gated_ref, ...), custom_call_target="tpu_custom_call" | custom-call | flops 20000000000 | bytes 10000000 | tf_op jit(solution)/shard_map/middle/pallas_call | solution.py:532
  230.3 0.0 all-gather.2.cloned.1.call-done.rest_cot_ref.refs_10_
  230.4 111.9 %way_back.1 = (bf16[2,4096,512]{2,1,0:T(8,128)(2,1)}, f32[128,2048]{1,0:T(8,128)}, f32[8,256]{1,0:T(8,128)}, bf16[1024,2048]{1,0:T(8,128)(2,1)}, bf16[1024,2048]...) custom-call(bf16[1024,512]{1,0:T(8,128)(2,1)} %get-tuple-element.60.dinner_ref, ...), custom_call_target="tpu_custom_call" | custom-call | flops 99999997952 | bytes 100000000 | tf_op jit(solution)/shard_map/way_back/pallas_call | solution.py:1215
  342.3 0.0 copy-start
  342.3 0.0 copy-start.1
  342.3 0.0 reduce-scatter.2.cloned.1.call-update
  342.3 0.5 iota_add_fusion.which_ref
  342.8 0.6 pad_add_fusion.which_ref
  343.4 0.4 copy-done
  343.8 0.6 slice.28
  344.4 0.6 slice.27
  345.0 0.6 slice.30
  345.6 0.9 slice.26
  346.5 1.0 slice.25
  347.6 1.3 slice.24
  348.8 0.0 copy-done.1
  348.8 1.0 constant_dynamic-update-slice_fusion
  349.9 0.6 fusion
  350.5 34.3 %weight_grad_last.1 = f32[3,2048,1024]{2,1,0:T(8,128)} custom-call(s32[2]{0:T(128)} %iota_add_fusion.which_ref, bf16[4096,2048]{1,0:T(8,128)(2,1)} %get-tuple-element.64.scaled_ref.left_ref.left2_ref, bf16[2,4096,512]{2,1,0:T(8,128)(2,1)} %get-tuple-element.78.right_ref.right2_ref, s32[1,4096]{1,0:T(1,128)} %get-tuple-element.65.label_row_ref.label_ref.label2_ref, ...), custom_call_target="tpu_custom_call" | custom-call | flops 25769803776 | bytes 50331648 | tf_op jit(solution)/shard_map/weight_grad_last/pallas_call | solution.py:1342
  384.8 0.0 copy-start.3
  384.8 0.0 copy-start.2
  384.8 36.9 %weight_grad_parts.1 = f32[3,512,2048]{2,1,0:T(8,128)} custom-call(s32[2]{0:T(128)} %pad_add_fusion.which_ref, bf16[4,2,2,2,128,512]{5,4,3,2,1,0:T(8,128)(2,1)} %bitcast.19, bf16[4,2,2,2,128,512]{5,4,3,2,1,0:T(8,128)(2,1)} %bitcast.20, bf16[4,2,2,2,128,512]{5,4,3,2,1,0:T(8,128)(2,1)} %bitcast.21, bf16[4,2,2,2,128,512]{5,4,3,2,1,0:T(8,128)(2,1)} %bitcast.22, ...), custom_call_target="tpu_custom_call" | custom-call | flops 25769803776 | bytes 33554432 | tf_op jit(solution)/shard_map/weight_grad_parts/pallas_call | solution.py:1294
  421.7 0.0 reduce-scatter.2.cloned.1.call-done
  421.7 0.0 copy-done.3
  421.7 2.0 add_convert_fusion
  423.6 0.0 copy-done.2
  423.6 1.0 copy.27
Async XLA Ops:
  7.2 133.2 %copy-start.4 = (bf16[2048]{0:T(1024)(128)(2,1)S(1)}, bf16[2048]{0:T(1024)(128)(2,1)}, u32[]{:S(2)}) copy-start(bf16[2048]{0:T(1024)(128)(2,1)} %gain_ref.1) | copy-start | bytes 12292
  7.2 133.8 %copy-start.5 = (bf16[512]{0:T(512)(128)(2,1)S(1)}, bf16[512]{0:T(512)(128)(2,1)}, u32[]{:S(2)}) copy-start(bf16[512]{0:T(512)(128)(2,1)} %param.22) | copy-start | bytes 3076
  7.2 223.2 %all-gather.2.cloned.1.call-start = ((), (), s32[]{:S(2)}) async-start(), calls=%async_computation.1 | async-start | bytes 5242880 | tf_op jit(solution)/shard_map/all_gather | solution.py:1485
  140.3 281.3 %reduce-scatter.2.cloned.1.call-start = ((), (), s32[]{:S(2)}) async-start(), calls=%async_computation.2 | async-start | bytes 4718592 | tf_op jit(solution)/shard_map/reduce_scatter | solution.py:1551
  342.3 1.5 copy-start
  342.3 6.6 %copy-start.1 = (bf16[1024,512]{1,0:T(8,128)(2,1)S(1)}, bf16[1024,512]{1,0:T(8,128)(2,1)}, u32[]{:S(2)}) copy-start(bf16[1024,512]{1,0:T(8,128)(2,1)} %get-tuple-element.81) | copy-start | bytes 3145732
  384.8 36.9 %copy-start.3 = (bf16[128,2048]{1,0:T(8,128)(2,1)S(1)}, bf16[128,2048]{1,0:T(8,128)(2,1)}, u32[]{:S(2)}) copy-start(bf16[128,2048]{1,0:T(8,128)(2,1)} %input_ref.3) | copy-start | bytes 1572868
  384.8 38.9 %copy-start.2 = (f32[128,2048]{1,0:T(8,128)S(1)}, f32[128,2048]{1,0:T(8,128)}, u32[]{:S(2)}) copy-start(f32[128,2048]{1,0:T(8,128)} %get-tuple-element.99) | copy-start | bytes 3145732
Sparse Core Ops, SparseCore 0:
  140.4 51.4 all-gather.1
  342.4 49.4 reduce-scatter.1
